TPU v7x, 32 devices: a whole 2x2x4 slice. The times are simulated.
32 devices in a mesh: req: 4 (over x, core), tok: 8 (over z, y).
Axes of the slice: x: 2, y: 2, z: 4, core: 2. Of those that a mesh axis runs over, the one named last changes fastest.
Arguments:
- hidden: bfloat16 [4, 1024, 2048], P('req', 'tok'), may hold values from -4 to 4
- queries: bfloat16 [4, 1024, 3072], P('req', 'tok'), may hold values from -18 to 18
- fresh_latent: bfloat16 [4, 1024, 576], P('req', 'tok'), may hold values from -8 to 8
- latent_cache: bfloat16 [4, 8, 128, 576], P('req', 'tok'), may hold values from -8 to 8
- page_table: int32 [4, 8], P('req'), may hold values from 0 to 7, each once within a row
- cache_lengths: int32 [4], P('req'), may hold values from 2 to 1024, as said below
- routes: int32 [4, 1024, 6], P('req', 'tok'), may hold values from 0 to 63, all different within a row; in each aligned block of 128 rows (0 to 127, 128 to 255, ..., all dimensions but the last counted through in order) at most 14 rows name the same one
- route_gates: float32 [4, 1024, 6], P('req', 'tok'), may hold values from 0.05 to 0.45
- kv_up: bfloat16 [512, 4096], replicated, may hold values from -0.25 to 0.25
- out_proj: bfloat16 [2048, 2048], replicated, may hold values from -0.125 to 0.125
- latent_gain: float32 [512], replicated, may hold values from 0.1 to 1.9
- norm_gain: float32 [2048], replicated, may hold values from 0.1 to 1.9
- expert_in: bfloat16 [128, 2048, 1408], P(('req', 'tok')), may hold values from -0.125 to 0.125
- expert_out: bfloat16 [128, 704, 2048], P(('req', 'tok')), may hold values from -0.15625 to 0.15625
Outputs:
- layer_out: bfloat16 [4, 1024, 2048], P('req', 'tok')
- new_latent: bfloat16 [4, 1024, 576], P('req', 'tok')
Inputs may be any that keep to these rules, and one draw needn't show every extreme that they name: `page_table`: each request's row names every pool page once. `cache_lengths`: some request has exactly 1024 cached tokens. `routes`: the 6 experts of a token differ; among the rows of one device no expert is named more than 14 times, and that bound is reached.
All inputs are finite; a program needn't handle non-finite values.
Results may differ from a plain program's by a relative error of at most 0.013.
Values may be sent and summed in bfloat16 or wider, within the bound.
No kernel may reach another device: no remote copies, remote signals or barrier semaphores. Data moves between devices by JAX's collectives and lax.ppermute only.
A program may use at most 192 MiB of HBM per device.

v0:
```python
import math

import jax
import jax.numpy as jnp
from jax import lax
from jax.sharding import PartitionSpec as P

H = 16
NOPE = 128
VD = 128
EXPERTS = 64
CAP = 14


epsilon = 1e-06
theta_base = 10000.0
floor_score = -1e30


def rotary(values, angles):
    half_width = values.shape[-1] // 2
    front_part = values[..., :half_width]
    back_part = values[..., half_width:]
    cosine = jnp.cos(angles)
    sine_part = jnp.sin(angles)
    return jnp.concatenate(
        [front_part * cosine - back_part * sine_part, back_part * cosine + front_part * sine_part],
        axis=-1,
    )


def rms_scale(values, gain):
    return values * lax.rsqrt(jnp.mean(values * values, axis=-1, keepdims=True) + epsilon) * gain


def local(
    hidden,
    queries,
    fresh_latent,
    latent_cache,
    page_table,
    cache_lengths,
    routes,
    route_gates,
    kv_up,
    out_proj,
    latent_gain,
    norm_gain,
    expert_in,
    expert_out,
):
    row_count = hidden.shape[1]
    model_width = hidden.shape[2]
    latent_width = latent_gain.shape[0]
    entry_width = fresh_latent.shape[2]
    rotary_width = entry_width - latent_width
    score_scale = 1.0 / math.sqrt(NOPE + rotary_width)
    length = cache_lengths[0]
    first_row = lax.axis_index("tok") * row_count
    positions = length + first_row + jnp.arange(row_count, dtype=jnp.int32)
    frequency = theta_base ** (
        -jnp.arange(rotary_width // 2, dtype=jnp.float32) * 2.0 / rotary_width
    )
    angles = positions.astype(jnp.float32)[:, None] * frequency[None, :]
    raw_latent = fresh_latent[0].astype(jnp.float32)
    latent = rms_scale(raw_latent[:, :latent_width], latent_gain).astype(jnp.bfloat16)
    key_rotated = rotary(raw_latent[:, latent_width:], angles).astype(jnp.bfloat16)
    query_rows = queries[0].reshape(row_count, H, NOPE + rotary_width)
    query_rotated = rotary(query_rows[:, :, NOPE:].astype(jnp.float32), angles[:, None, :]).astype(
        jnp.bfloat16
    )
    weights = kv_up.reshape(latent_width, H, NOPE + VD)
    query_latent = jnp.einsum(
        "thn,lhn->thl",
        query_rows[:, :, :NOPE],
        weights[:, :, :NOPE],
        preferred_element_type=jnp.float32,
    ).astype(jnp.bfloat16)

    def attend(carry, keys_latent, keys_rotated, key_positions, key_valid):
        highest, totals, accumulated = carry
        scores = jnp.einsum(
            "thl,kl->htk", query_latent, keys_latent, preferred_element_type=jnp.float32
        )
        scores = (
            scores
            + jnp.einsum(
                "thr,kr->htk", query_rotated, keys_rotated, preferred_element_type=jnp.float32
            )
        ) * score_scale
        allowed = key_valid[None, None, :] & (
            key_positions[None, None, :] <= positions[None, :, None]
        )
        scores = jnp.where(allowed, scores, -jnp.inf)
        new_highest = jnp.maximum(highest, jnp.max(scores, axis=2))
        fading = jnp.exp(highest - new_highest)
        soft_weights = jnp.exp(scores - new_highest[:, :, None])
        totals = totals * fading + jnp.sum(soft_weights, axis=2)
        accumulated = accumulated * fading[:, :, None] + jnp.einsum(
            "htk,kl->htl",
            soft_weights.astype(jnp.bfloat16),
            keys_latent,
            preferred_element_type=jnp.float32,
        )
        return (new_highest, totals, accumulated)

    pool_size = page_table.shape[1]
    pool_index = jnp.arange(pool_size, dtype=jnp.int32)
    inverse = jnp.sum(
        jnp.where(page_table[0][None, :] == pool_index[:, None], pool_index[None, :], 0), axis=1
    )
    starting = (
        jnp.full((H, row_count), floor_score, dtype=jnp.float32),
        jnp.zeros((H, row_count), dtype=jnp.float32),
        jnp.zeros((H, row_count, latent_width), dtype=jnp.float32),
    )
    piece_latent = lax.all_gather(latent, "tok", axis=0, tiled=True)
    piece_rotated = lax.all_gather(key_rotated, "tok", axis=0, tiled=True)
    key_count = piece_latent.shape[0]
    key_positions = length + jnp.arange(key_count, dtype=jnp.int32)
    key_valid = jnp.ones((key_count,), dtype=bool)
    carried = lax.cond(
        jnp.int32(0) < first_row + row_count,
        lambda current: attend(current, piece_latent, piece_rotated, key_positions, key_valid),
        lambda current: current,
        starting,
    )
    piece = lax.all_gather(latent_cache, "tok", axis=1, tiled=True)
    page_count = piece.shape[1]
    page_size = piece.shape[2]
    flat_pages = piece[0].reshape(page_count * page_size, entry_width)
    page_key_positions = (
        inverse[:, None] * page_size + jnp.arange(page_size, dtype=jnp.int32)[None, :]
    ).reshape(-1)
    page_key_valid = page_key_positions < length
    highest, totals, accumulated = lax.cond(
        jnp.any(page_key_valid),
        lambda current: attend(
            current,
            flat_pages[:, :latent_width],
            flat_pages[:, latent_width:],
            page_key_positions,
            page_key_valid,
        ),
        lambda current: current,
        carried,
    )
    mixed = (accumulated / totals[:, :, None]).astype(jnp.bfloat16)
    head_out = jnp.einsum(
        "htl,lhv->thv", mixed, weights[:, :, NOPE:], preferred_element_type=jnp.float32
    ).astype(jnp.bfloat16)
    attended = jnp.dot(
        head_out.reshape(row_count, H * VD), out_proj, preferred_element_type=jnp.float32
    )
    residual = hidden[0].astype(jnp.float32) + attended
    normed = rms_scale(residual, norm_gain).astype(jnp.bfloat16)
    top_count = routes.shape[2]
    capacity = CAP
    expert_count = EXPERTS
    flat_routes = routes[0].reshape(-1)
    onehot = (flat_routes[:, None] == jnp.arange(expert_count, dtype=jnp.int32)[None, :]).astype(
        jnp.int32
    )
    slot_index = jnp.sum((jnp.cumsum(onehot, axis=0) - 1) * onehot, axis=1)
    target = flat_routes * capacity + slot_index
    placing = (
        target[:, None] == jnp.arange(expert_count * capacity, dtype=jnp.int32)[None, :]
    ).astype(jnp.bfloat16)
    placing = jnp.sum(placing.reshape(row_count, top_count, expert_count * capacity), axis=1)
    outgoing = lax.dot_general(
        placing, normed, (((0,), (0,)), ((), ())), preferred_element_type=jnp.float32
    ).astype(jnp.bfloat16)
    slabs_here = expert_in.shape[0]
    req_count = lax.axis_size("req")
    tok_count = lax.axis_size("tok")
    device_count = req_count * tok_count
    outgoing = jnp.repeat(
        outgoing.reshape(expert_count, 1, capacity, model_width), 2, axis=1
    ).reshape(device_count, slabs_here, capacity, model_width)
    hidden_half = expert_out.shape[1]
    arrived = lax.all_to_all(outgoing, ("req", "tok"), split_axis=0, concat_axis=0, tiled=True)
    results = []
    for slab_index in range(slabs_here):
        slab_rows = arrived[:, slab_index].reshape(-1, model_width)
        projected = jnp.dot(slab_rows, expert_in[slab_index], preferred_element_type=jnp.float32)
        active = (jax.nn.silu(projected[:, :hidden_half]) * projected[:, hidden_half:]).astype(
            jnp.bfloat16
        )
        slab_result = jnp.dot(
            active, expert_out[slab_index], preferred_element_type=jnp.float32
        ).astype(jnp.bfloat16)
        results.append(slab_result.reshape(device_count, -1, model_width))
    returned = lax.all_to_all(
        jnp.stack(results, axis=1), ("req", "tok"), split_axis=0, concat_axis=0, tiled=True
    )
    returned = returned.reshape(expert_count, 2, capacity, model_width).astype(jnp.float32)
    combined = (returned[:, 0] + returned[:, 1]).reshape(expert_count * capacity, model_width)
    picked = jnp.take(combined, target, axis=0).reshape(row_count, top_count, model_width)
    gate_values = route_gates[0]
    routed = jnp.zeros_like(residual)
    for route_index in range(top_count):
        routed = routed + gate_values[:, route_index, None] * picked[:, route_index]
    layer_out = (residual + routed).astype(jnp.bfloat16)
    return (layer_out[None], jnp.concatenate([latent, key_rotated], axis=1)[None])


def solution(mesh):
    placed = (
        P("req", "tok", None),
        P("req", "tok", None),
        P("req", "tok", None),
        P("req", "tok", None, None),
        P("req", None),
        P("req"),
        P("req", "tok", None),
        P("req", "tok", None),
        P(),
        P(),
        P(),
        P(),
        P(("req", "tok"), None, None),
        P(("req", "tok"), None, None),
    )
    return jax.shard_map(
        local,
        mesh=mesh,
        in_specs=placed,
        out_specs=(P("req", "tok", None), P("req", "tok", None)),
        check_vma=False,
    )
```

profile of v0, /device:TPU:0, one launch (start us, length us, event | category | flops | bytes accessed | tf_op | source)
XLA Modules:
  0.0 749.5 jit_solution(10634913644736623500)
XLA Ops:
  17.5 6.5 copy.122
  25.0 28.1 %all_gather.10 = bf16[1024,64]{0,1:T(8,128)(2,1)S(1)} all-gather(bf16[128,64]{0,1:T(8,128)(2,1)S(1)} %pad_maximum_fusion.2), channel_id=1, replica_groups=mesh['req'=4,'tok'=8] {'tok'}, dimensions={0}, use_global_device_ids=true | all-gather | bytes 147456 | tf_op jit(solution)/shard_map/all_gather | solution.py:118
  58.1 15.8 %conditional.2 = (f32[16,128]{1,0:T(8,128)}, f32[16,128]{1,0:T(8,128)S(1)}, f32[16,128,512]{2,1,0:T(8,128)}) conditional(s32[]{:T(128)} %convert_element_type.107, () %tuple.23, (s32[]{:T(128)}, s32[1024]{0:T(1024)S(1)}, s32[128]{0:T(128)S(1)}, bf16[1024,512]{0,1:T(8,128)(2,1)}, bf16[128,16,512]{0,2,1:T(8,128)(2,1)}, ...), branch_computations={%region_3.4_spmd, %region_4.7_spmd} | conditional | flops 4581368832 | bytes 55284280 | solution.py:122
  68.2 5.7 broadcast_add_fusion
  73.9 22.4 %all-gather.5.cloned.1.call-done = bf16[1,8,128,576]{2,3,0,1:T(8,128)(2,1)} async-done(((bf16[1,1,128,576]{2,3,0,1:T(8,128)(2,1)}), bf16[1,8,128,576]{2,3,0,1:T(8,128)(2,1)}) %all-gather.5.cloned.1.call-update) | async-done | bytes 1179664 | tf_op jit(solution)/shard_map/all_gather | solution.py:128
  96.3 16.8 %conditional.3 = ((f32[16,128]{1,0:T(8,128)S(1)}, f32[16,128,512]{2,1,0:T(8,128)})) conditional(s32[]{:T(128)} %convert_element_type.106, (f32[16,128]{1,0:T(8,128)S(1)}, f32[16,128,512]{2,1,0:T(8,128)}) %tuple.25, (s32[8,128]{1,0:T(8,128)S(1)}, s32[8,128]{1,0:T(8,128)S(1)}, s32[]{:T(128)}, s32[8,128]{1,0:T(8,128)S(1)}, s32[128]{0:T(128)S(1)}, ...), branch_computations={%region_7.8_spmd, %region_8.11_spmd} | conditional | flops 4582545408 | bytes 57801244 | solution.py:136
  107.6 5.6 multiply_add_fusion
  116.9 4.8 multiply_reduce_fusion
  124.7 6.0 reshape.294
  134.9 5.5 broadcast_in_dim.93
  140.4 17.0 %reshape_reshape.3 = bf16[32,4,14,2048]{3,1,0,2:T(4,128)(2,1)} reshape(bf16[64,1,2,14,2048]{4,2,0,3,1:T(2,128)(2,1)} %broadcast_in_dim.93) | data formatting | bytes 14680064 | tf_op jit(solution)/shard_map/reshape;reshape | solution.py:179
  157.4 11.5 %copy.137 = bf16[32,4,14,2048]{3,1,2,0:T(4,128)(2,1)} copy(bf16[32,4,14,2048]{3,1,0,2:T(4,128)(2,1)} %reshape_reshape.3) | data formatting | bytes 14680064 | tf_op jit(solution)/shard_map/reshape;reshape | solution.py:179
  168.9 166.0 %all_to_all.10 = bf16[32,4,14,2048]{3,1,2,0:T(4,128)(2,1)S(1)} all-to-all(bf16[32,4,14,2048]{3,1,2,0:T(4,128)(2,1)} %copy.137), channel_id=1, replica_groups=mesh['req'=4,'tok'=8] {'req','tok'}, dimensions={0} | all-to-all | bytes 14680064 | tf_op jit(solution)/shard_map/all_to_all | solution.py:181
  334.9 33.9 %slice_reduce_fusion.3 = (bf16[32,14,2048]{2,1,0:T(8,128)(2,1)}, bf16[32,14,2048]{2,1,0:T(8,128)(2,1)}, bf16[32,14,2048]{2,1,0:T(8,128)(2,1)}, bf16[32,14,2048]{2,1,0:T(8,128)(2,1)}) fusion(bf16[32,4,14,2048]{3,1,2,0:T(4,128)(2,1)S(1)} %all_to_all.10), kind=kLoop, calls=%fused_computation.52 | loop fusion | bytes 14680064 | tf_op jit(solution)/shard_map/slice | solution.py:184
  372.5 5.8 fusion.27
  390.4 6.1 fusion.25
  396.4 4.7 convolution_convert_fusion.3
  408.5 5.8 fusion.23
  426.4 5.8 fusion.21
  432.2 4.7 convolution_convert_fusion.1
  440.6 7.7 %pad_maximum_fusion = bf16[32,4,14,2048]{3,2,0,1:T(8,128)(2,1)} fusion(bf16[32,1,14,2048]{3,2,0,1:T(8,128)(2,1)} %stack_reshape.15, bf16[32,1,14,2048]{3,2,0,1:T(8,128)(2,1)} %stack_reshape.14, bf16[32,1,14,2048]{3,2,0,1:T(8,128)(2,1)} %stack_reshape.13, bf16[32,1,14,2048]{3,2,0,1:T(8,128)(2,1)} %stack_reshape.12), kind=kLoop, calls=%fused_computation.32 | loop fusion | flops 11010048 | bytes 14680064 | tf_op jit(solution)/shard_map/stack | solution.py:194
  448.3 13.3 %copy.138 = bf16[32,4,14,2048]{3,1,2,0:T(4,128)(2,1)} copy(bf16[32,4,14,2048]{3,2,0,1:T(8,128)(2,1)} %pad_maximum_fusion) | data formatting | bytes 14680064 | tf_op jit(solution)/shard_map/stack | solution.py:194
  466.6 165.1 %all-to-all-done.1 = bf16[32,4,14,2048]{3,1,2,0:T(4,128)(2,1)} async-done(((bf16[32,4,14,2048]{3,1,2,0:T(4,128)(2,1)}), bf16[32,4,14,2048]{3,1,2,0:T(4,128)(2,1)}, u32[]{:S(2)}, u32[]{:S(2)}) %all-to-all-start.1) | async-done | bytes 7340064 | tf_op jit(solution)/shard_map/all_to_all | solution.py:193
  631.7 12.5 %copy_convert_fusion = f32[32,4,14,2048]{3,0,2,1:T(8,128)} fusion(bf16[32,4,14,2048]{3,1,2,0:T(4,128)(2,1)} %all-to-all-done.1), kind=kLoop, calls=%fused_computation.34 | loop fusion | flops 3670016 | bytes 22020096 | tf_op jit(solution)/shard_map/convert_element_type | solution.py:196
  644.2 18.6 %copy.140 = f32[32,4,14,2048]{3,1,0,2:T(4,128)} copy(f32[32,4,14,2048]{3,0,2,1:T(8,128)} %copy_convert_fusion) | data formatting | bytes 29360128 | tf_op jit(solution)/shard_map/convert_element_type | solution.py:196
  662.9 19.2 %reshape.297 = f32[64,2,14,2048]{3,1,0,2:T(2,128)} reshape(f32[32,4,14,2048]{3,1,0,2:T(4,128)} %copy.140) | data formatting | bytes 29360128 | tf_op jit(solution)/shard_map/convert_element_type | solution.py:196
  682.0 17.2 %slice_add_fusion = f32[64,1,14,2048]{3,1,0,2:T(1,128)S(1)} fusion(f32[64,2,14,2048]{3,1,0,2:T(2,128)} %reshape.297), kind=kLoop, calls=%fused_computation.33 | loop fusion | flops 1835008 | bytes 22020096 | tf_op jit(solution)/shard_map/add | solution.py:197
  699.2 7.5 %copy.141 = f32[64,1,14,2048]{3,2,0,1:T(8,128)} copy(f32[64,1,14,2048]{3,1,0,2:T(1,128)S(1)} %slice_add_fusion) | data formatting | bytes 14680064 | tf_op jit(solution)/shard_map/add | solution.py:197
  706.8 8.1 %add.189 = f32[896,2048]{1,0:T(8,128)} reshape(f32[64,1,14,2048]{3,2,0,1:T(8,128)} %copy.141) | data formatting | bytes 14680064 | tf_op jit(solution)/shard_map/add | solution.py:197
  714.9 10.3 %gather_fusion = f32[768,2048]{1,0:T(8,128)} fusion(f32[896,2048]{1,0:T(8,128)} %add.189, s32[1024]{0:T(1024)S(1)} %pad_clamp_fusion), kind=kCustom, calls=%fused_computation | custom fusion | bytes 12585984 | tf_op jit(solution)/shard_map/jit(_take)/gather | solution.py:198
  725.2 8.1 %gather.7 = f32[128,6,2048]{2,1,0:T(8,128)} reshape(f32[768,2048]{1,0:T(8,128)} %gather_fusion) | data formatting | bytes 12582912 | tf_op jit(solution)/shard_map/jit(_take)/gather | solution.py:198
  733.3 7.7 %copy_select_fusion = f32[128,6,2048]{2,0,1:T(8,128)S(1)} fusion(f32[128,6,2048]{2,1,0:T(8,128)} %gather.7, pred[128,6]{0,1:T(8,128)(4,1)S(1)} %copy-done.4), kind=kLoop, calls=%fused_computation.35 | loop fusion | flops 1572864 | bytes 12583680 | tf_op jit(solution)/shard_map/jit(_take)/select_n | solution.py:198
  (91 shorter events, 91.7 us)
Async XLA Ops:
  7.2 50.9 %all-gather.3.cloned.1.call-start = ((), (), s32[]{:S(2)}) async-start(), calls=%async_computation.2 | async-start | bytes 1179648 | tf_op jit(solution)/shard_map/all_gather | solution.py:117
  9.7 86.5 %all-gather.5.cloned.1.call-start = ((), (), s32[]{:S(2)}) async-start(), calls=%async_computation.3 | async-start | bytes 1327104 | tf_op jit(solution)/shard_map/all_gather | solution.py:128
  17.5 35.7 %copy-start.2 = (s32[1,128,6]{1,0,2:T(1,128)S(1)}, s32[1,128,6]{1,0,2:T(1,128)}, u32[]{:S(2)}) copy-start(s32[1,128,6]{1,0,2:T(1,128)} %param.24) | copy-start | bytes 9220
  65.5 2.6 copy-start.6
  113.1 3.7 copy-start.1
  116.9 4.8 copy-start.3
  461.6 4.2 copy-start.5
  461.6 4.3 copy-start
  461.6 170.1 %all-to-all-start.1 = ((bf16[32,4,14,2048]{3,1,2,0:T(4,128)(2,1)}), bf16[32,4,14,2048]{3,1,2,0:T(4,128)(2,1)}, u32[]{:S(2)}, u32[]{:S(2)}) async-start(bf16[32,4,14,2048]{3,1,2,0:T(4,128)(2,1)} %copy.138), calls=%async_computation.1 | async-start | bytes 14680064 | tf_op jit(solution)/shard_map/all_to_all | solution.py:193
  725.2 8.1 %copy-start.4 = (pred[128,6]{0,1:T(8,128)(4,1)S(1)}, pred[128,6]{0,1:T(8,128)(4,1)}, u32[]{:S(2)}) copy-start(pred[128,6]{0,1:T(8,128)(4,1)} %get-tuple-element.194) | copy-start | bytes 2308
Sparse Core Ops, SparseCore 0:
  10.6 42.6 all-gather.2
  55.5 40.7 all-gather.4
where the time goes:
time: 761 us; the launch traced here: 749 us
  local copies, waits for them, and re-layouts  204 us (27%)
  blocking collectives  194 us (25%)
  waiting for transfers between devices  188 us (25%)
  matrix products  80.5 us (11%)
  other arithmetic  62.3 us (8%)
  between operations  15.9 us (2%)
    all_to_all x1, blocking collectives, local(): lax.all_to_all(outgoing, ('req', 'tok'), split_axis=0, concat_axis=0, til...  166 us
    all_to_all x1, waiting for transfers between devices, local(): lax.all_to_all(jnp.stack(results, axis=1), ('req', 'tok'), split_axis=0,...  165 us
    convert_element_type x2, local copies, waits for them, and re-layouts, local(): returned.reshape(expert_count, 2, capacity, model_width).astype(jnp.float32)  37.8 us
    slice x1, local copies, waits for them, and re-layouts, local(): slab_rows = arrived[:, slab_index].reshape(-1, model_width)  33.9 us
    another operation x2, local copies, waits for them, and re-layouts, local(): outgoing = jnp.repeat(outgoing.reshape(expert_count, 1, capacity, model_w...  28.5 us
    all_gather x1, blocking collectives, local(): piece_rotated = lax.all_gather(key_rotated, 'tok', axis=0, tiled=True)  28.1 us
    another operation x5, local copies, waits for them, and re-layouts, local(): jnp.stack(results, axis=1)  27.7 us
    dot_general x4, matrix products, local(): jnp.dot(slab_rows, expert_in[slab_index], preferred_element_type=jnp.floa...  23.6 us
  transfers between devices with their start and end apart: 3, of which 2 were waited for; matrix products, arithmetic and copies ran while one was open for 5% of the time, Pallas kernels for 0%

commit v1 on v0

v1 whole, which is shorter than its diff:
```python
import functools
import math

import jax
import jax.numpy as jnp
from jax import lax
from jax.experimental import pallas as pl
from jax.experimental.pallas import tpu as pltpu
from jax.sharding import Mesh
from jax.sharding import PartitionSpec as P

H = 16
NOPE = 128
VD = 128
CAP = 14
PLANES = 4
PAIR = 2
GROUPS = 2
PARTS = 2

epsilon = 1e-06
theta_base = 10000.0
hidden_score = -1e30
PLANE_AXES = ("x", "core", "y")
MIB = 1 << 20
FACT_ROWS = 16
NEAR = [(0, 1), (1, 0), (2, 3), (3, 2)]
MIDDLE = [(1, 2), (2, 1)]
OUTWARD = [(1, 0), (2, 3)]
INWARD = [(0, 1), (3, 2)]


def shifted(values, axis, step):
    count = lax.axis_size(axis)
    return lax.ppermute(values, axis, [(i, (i + step) % count) for i in range(count)])


def entries_kernel(fresh_ref, page_ref, facts_ref, cos_ref, sin_ref, gain_ref, block_ref, new_ref):
    latent_width = gain_ref.shape[0] * gain_ref.shape[1]
    entry_width = fresh_ref.shape[0]
    half = cos_ref.shape[0]
    rows = fresh_ref.shape[1]
    raw = fresh_ref[:latent_width, :].astype(jnp.float32)
    mean = jnp.mean(raw * raw, axis=0, keepdims=True)
    gain = jnp.concatenate(
        [
            jnp.broadcast_to(gain_ref[i : i + 1, :], (rows, gain_ref.shape[1])).T
            for i in range(gain_ref.shape[0])
        ],
        axis=0,
    )
    latent = (raw * lax.rsqrt(mean + epsilon) * gain).astype(jnp.bfloat16)
    front = fresh_ref[latent_width : latent_width + half, :].astype(jnp.float32)
    back = fresh_ref[latent_width + half :, :].astype(jnp.float32)
    cosine = cos_ref[...]
    sine = sin_ref[...]
    turned_front = (front * cosine - back * sine).astype(jnp.bfloat16)
    turned_back = (back * cosine + front * sine).astype(jnp.bfloat16)
    new_ref[:latent_width, :] = latent
    new_ref[latent_width : latent_width + half, :] = turned_front
    new_ref[latent_width + half :, :] = turned_back
    block_ref[:entry_width, :rows] = page_ref[...]
    block_ref[:latent_width, rows:] = latent
    block_ref[latent_width : latent_width + half, rows:] = turned_front
    block_ref[latent_width + half : entry_width, rows:] = turned_back
    block_ref[entry_width:, rows:] = facts_ref[...]
    block_ref[entry_width:, :rows] = facts_ref[...]


def attend(nope_ref, rotated_ref, up_ref, facts_ref, marks_ref, keys_ref, score_scale):
    latent_width = up_ref.shape[0]
    head_width = NOPE + VD
    keys_latent = keys_ref[:latent_width, :]
    keys_rotated = keys_ref[latent_width:, :]
    rows = nope_ref.shape[0]
    first_row = (facts_ref[1] * facts_ref[3] + facts_ref[2]) * rows
    query_rows = lax.broadcasted_iota(jnp.int32, (PAIR * rows, 1), 0)
    allowed = marks_ref[...] <= lax.rem(query_rows, rows) + first_row
    scores = []
    for group in range(GROUPS):
        heads = range(group * PAIR, (group + 1) * PAIR)
        query_latent = jnp.concatenate(
            [
                lax.dot_general(
                    nope_ref[:, i * NOPE : (i + 1) * NOPE],
                    up_ref[:, i * head_width : i * head_width + NOPE],
                    (((1,), (1,)), ((), ())),
                    preferred_element_type=jnp.float32,
                ).astype(jnp.bfloat16)
                for i in heads
            ],
            axis=0,
        )
        query_rotated = jnp.concatenate([rotated_ref[i] for i in heads], axis=0)
        value = jnp.dot(query_latent, keys_latent, preferred_element_type=jnp.float32)
        value = value + jnp.dot(query_rotated, keys_rotated, preferred_element_type=jnp.float32)
        scores.append(jnp.where(allowed, value, hidden_score))
    results = []
    for group in range(GROUPS):
        highest = jnp.max(scores[group], axis=1, keepdims=True)
        soft = jnp.exp((scores[group] - highest) * score_scale)
        totals = jnp.sum(soft, axis=1, keepdims=True)
        mixed = lax.dot_general(
            soft.astype(jnp.bfloat16),
            keys_latent,
            (((1,), (1,)), ((), ())),
            preferred_element_type=jnp.float32,
        )
        results.append((highest, totals, mixed))
    return results


def fill_keys(facts_ref, block_refs, keys_ref, marks_ref, first_slot, y_count, rows):
    width = block_refs[0].shape[1]
    length, z_index, y_index = facts_ref[0], facts_ref[1], facts_ref[2]
    low = z_index < 2
    pool = facts_ref.shape[0] - 4
    page_size = width - rows
    for index, block_ref in enumerate(block_refs):
        keys_ref[:, index * width : (index + 1) * width] = block_ref[: keys_ref.shape[0], :]
        slot = first_slot + index // y_count
        z_source = (
            z_index,
            z_index + 1 - 2 * lax.rem(z_index, 2),
            jnp.where(low, 2, 1),
            jnp.where(low, 3, 0),
        )[slot]
        y_source = lax.rem(y_index + y_count - index % y_count, y_count)
        source = z_source * y_count + y_source
        logical = jnp.int32(0)
        for place in range(pool):
            logical = logical + jnp.where(facts_ref[4 + place] == source, place, 0)
        cached = lax.broadcasted_iota(jnp.int32, (1, page_size), 1) + logical * page_size
        marks_ref[:, index * width : index * width + page_size] = jnp.where(
            cached < length, -1, 1 << 30
        )
        marks_ref[:, index * width + page_size : (index + 1) * width] = (
            lax.broadcasted_iota(jnp.int32, (1, rows), 1) + source * rows
        )


def merged(result, group, old_refs, score_scale):
    highest, totals, mixed = result
    old_highest, old_totals, old_mixed = [ref[group] for ref in old_refs]
    top = jnp.maximum(highest, old_highest)
    fresh = jnp.exp((highest - top) * score_scale)
    fading = jnp.exp((old_highest - top) * score_scale)
    return top, totals * fresh + old_totals * fading, mixed * fresh + old_mixed * fading


def first_attention_kernel(score_scale, first_slot, y_count, block_count, *refs):
    facts_ref, nope_ref, rotated_ref, up_ref = refs[:4]
    block_refs = refs[4 : 4 + block_count]
    *old_refs, highest_ref, totals_ref, mixed_ref, keys_ref, marks_ref = refs[4 + block_count :]

    @pl.when(pl.program_id(0) == 0)
    def _():
        fill_keys(
            facts_ref, block_refs, keys_ref, marks_ref, first_slot, y_count, nope_ref.shape[0]
        )

    results = attend(nope_ref, rotated_ref, up_ref, facts_ref, marks_ref, keys_ref, score_scale)
    for group, result in enumerate(results):
        if old_refs:
            result = merged(result, group, old_refs, score_scale)
        highest, totals, mixed = result
        highest_ref[group] = highest
        totals_ref[group] = totals
        mixed_ref[group] = mixed


def last_attention_kernel(score_scale, first_slot, y_count, block_count, *refs):
    facts_ref, nope_ref, rotated_ref, up_ref = refs[:4]
    block_refs = refs[4 : 4 + block_count]
    old_refs = refs[4 + block_count : 7 + block_count]
    proj_ref, hidden_ref, gain_ref = refs[7 + block_count : 10 + block_count]
    residual_ref, left_ref, right_ref, keys_ref, marks_ref, total_ref = refs[10 + block_count :]
    step = pl.program_id(0)
    rows = hidden_ref.shape[0]
    head_width = NOPE + VD

    @pl.when(step == 0)
    def _():
        fill_keys(facts_ref, block_refs, keys_ref, marks_ref, first_slot, y_count, rows)

    results = attend(nope_ref, rotated_ref, up_ref, facts_ref, marks_ref, keys_ref, score_scale)
    outs = []
    for group, result in enumerate(results):
        _, totals, mixed = merged(result, group, old_refs, score_scale)
        mixed = (mixed / totals).astype(jnp.bfloat16)
        for i in range(PAIR):
            head = group * PAIR + i
            outs.append(
                jnp.dot(
                    mixed[i * rows : (i + 1) * rows],
                    up_ref[:, head * head_width + NOPE : (head + 1) * head_width],
                    preferred_element_type=jnp.float32,
                ).astype(jnp.bfloat16)
            )
    head_out = jnp.concatenate(outs, axis=1)
    part = jnp.dot(head_out, proj_ref[...], preferred_element_type=jnp.float32)

    @pl.when(step == 0)
    def _():
        total_ref[...] = part

    @pl.when(step > 0)
    def _():
        total_ref[...] += part

    @pl.when(step == pl.num_programs(0) - 1)
    def _():
        residual = hidden_ref[...].astype(jnp.float32) + total_ref[...]
        residual_ref[...] = residual
        mean = jnp.mean(residual * residual, axis=1, keepdims=True)
        normed = (residual * lax.rsqrt(mean + epsilon) * gain_ref[...]).astype(jnp.bfloat16)
        left_ref[...] = normed[:, : left_ref.shape[1]]
        right_ref[...] = normed[:, left_ref.shape[1] :]


def attention_call(score_scale, first_slot, y_count, queries, blocks, old, tail):
    facts, nope, rotated, up = queries
    rows = nope.shape[0]
    latent_width = up.shape[0]
    block_height, width = blocks[0].shape
    keys = width * len(blocks)
    rotary_width = rotated.shape[2]
    heads = PAIR * GROUPS
    whole = lambda *shape: pl.BlockSpec(shape, lambda s: (0,) * len(shape))
    state_specs = [
        pl.BlockSpec((GROUPS, PAIR * rows, size), lambda s: (s, 0, 0))
        for size in (1, 1, latent_width)
    ]
    in_specs = [
        pl.BlockSpec(memory_space=pltpu.SMEM),
        pl.BlockSpec((rows, heads * NOPE), lambda s: (0, s)),
        pl.BlockSpec((heads, rows, rotary_width), lambda s: (s, 0, 0)),
        pl.BlockSpec((latent_width, heads * (NOPE + VD)), lambda s: (0, s)),
    ] + [whole(block_height, width)] * len(blocks)
    scratch = [
        pltpu.VMEM((latent_width + rotary_width, keys), jnp.bfloat16),
        pltpu.VMEM((1, keys), jnp.int32),
    ]
    if old:
        in_specs += state_specs
    if tail:
        proj, hidden, gain = tail
        model_width = hidden.shape[1]
        kernel = last_attention_kernel
        in_specs += [
            pl.BlockSpec((heads * VD, model_width), lambda s: (s, 0)),
            whole(rows, model_width),
            whole(1, model_width),
        ]
        out_specs = [whole(rows, model_width)] + [whole(rows, model_width // 2)] * 2
        out_shape = [
            jax.ShapeDtypeStruct((rows, model_width), jnp.float32),
            jax.ShapeDtypeStruct((rows, model_width // 2), jnp.bfloat16),
            jax.ShapeDtypeStruct((rows, model_width // 2), jnp.bfloat16),
        ]
        scratch.append(pltpu.VMEM((rows, model_width), jnp.float32))
    else:
        kernel = first_attention_kernel
        out_specs = state_specs
        out_shape = [
            jax.ShapeDtypeStruct((H // PAIR, PAIR * rows, size), jnp.float32)
            for size in (1, 1, latent_width)
        ]
    return pl.pallas_call(
        functools.partial(kernel, score_scale, first_slot, y_count, len(blocks)),
        grid=(H // heads,),
        in_specs=in_specs,
        out_specs=out_specs,
        out_shape=out_shape,
        scratch_shapes=scratch,
        compiler_params=pltpu.CompilerParams(vmem_limit_bytes=56 * MIB),
        cost_estimate=pl.CostEstimate(
            flops=2 * H * rows * keys * (2 * latent_width + rotary_width),
            bytes_accessed=16 * MIB,
            transcendentals=H * rows * keys,
        ),
    )(facts, nope, rotated, up, *blocks, *old, *tail)


def experts_kernel(slabs_each, sorting, x_ref, *refs):
    if sorting:
        take_ref, put_ref = refs[:2]
        refs = refs[2:]
    in_refs = refs[:PARTS]
    out_weight_refs = refs[PARTS : 2 * PARTS]
    result_ref = refs[2 * PARTS]
    rows_ref, total_ref = refs[2 * PARTS + 1 :]
    expert = pl.program_id(0)
    slab = pl.program_id(1)

    @pl.when(slab == 0)
    def _():
        if sorting:
            rows_ref[...] = jnp.dot(
                take_ref[0], x_ref[...], preferred_element_type=jnp.float32
            ).astype(jnp.bfloat16)
        else:
            rows_ref[...] = x_ref[...]

    depth = in_refs[0].shape[1]
    projected = None
    for index, in_ref in enumerate(in_refs):
        piece = jnp.dot(
            rows_ref[:, index * depth : (index + 1) * depth],
            in_ref[0],
            preferred_element_type=jnp.float32,
        )
        projected = piece if projected is None else projected + piece
    piece_half = out_weight_refs[0].shape[1]
    half = piece_half * PARTS
    active = (jax.nn.silu(projected[:, :half]) * projected[:, half:]).astype(jnp.bfloat16)
    part = None
    for index, out_weight_ref in enumerate(out_weight_refs):
        piece = jnp.dot(
            active[:, index * piece_half : (index + 1) * piece_half],
            out_weight_ref[0],
            preferred_element_type=jnp.float32,
        )
        part = piece if part is None else part + piece

    if slabs_each > 1:

        @pl.when(slab == 0)
        def _():
            total_ref[...] = part

    @pl.when(slab == slabs_each - 1)
    def _():
        value = part
        if slabs_each > 1:
            value = value + total_ref[...]
        value = value.astype(jnp.bfloat16)
        if sorting:
            value = jnp.dot(put_ref[0], value, preferred_element_type=jnp.float32).astype(
                jnp.bfloat16
            )

            @pl.when(expert == 0)
            def _():
                result_ref[...] = value

            @pl.when(expert > 0)
            def _():
                result_ref[...] += value
        else:
            result_ref[...] = value


def experts(x, expert_in, expert_out, experts_here, group):
    rows, width = x.shape
    slabs_each = expert_in.shape[0] // experts_here
    half = expert_out.shape[1]
    each = rows // experts_here
    sorting = experts_here > 1
    operands = [x]
    in_specs = [pl.BlockSpec((rows, width), lambda e, s: (0, 0))]
    if sorting:
        place = jnp.arange(each, dtype=jnp.int32)
        target = (
            (place // group * experts_here)[None, :]
            + jnp.arange(experts_here, dtype=jnp.int32)[:, None]
        ) * group + (place % group)[None, :]
        column = jnp.arange(rows, dtype=jnp.int32)
        take = (target[:, :, None] == column[None, None, :]).astype(jnp.bfloat16)
        put = (target[:, None, :] == column[None, :, None]).astype(jnp.bfloat16)
        operands += [take, put]
        in_specs += [
            pl.BlockSpec((1, each, rows), lambda e, s: (e, 0, 0)),
            pl.BlockSpec((1, rows, each), lambda e, s: (e, 0, 0)),
        ]

    def piece(height, columns, index):
        return pl.BlockSpec((1, height, columns), lambda e, s: (e * slabs_each + s, index, 0))

    operands += [expert_in] * PARTS + [expert_out] * PARTS
    in_specs += [piece(width // PARTS, 2 * half, i) for i in range(PARTS)]
    in_specs += [piece(half // PARTS, width, i) for i in range(PARTS)]
    return pl.pallas_call(
        functools.partial(experts_kernel, slabs_each, sorting),
        grid=(experts_here, slabs_each),
        in_specs=in_specs,
        out_specs=pl.BlockSpec((rows, width), lambda e, s: (0, 0)),
        out_shape=jax.ShapeDtypeStruct((rows, width), jnp.bfloat16),
        scratch_shapes=[
            pltpu.VMEM((each, width), jnp.bfloat16),
            pltpu.VMEM((each, width), jnp.float32),
        ],
        compiler_params=pltpu.CompilerParams(vmem_limit_bytes=58 * MIB),
        cost_estimate=pl.CostEstimate(
            flops=6 * rows * width * half * slabs_each,
            bytes_accessed=2 * 3 * width * half * experts_here * slabs_each,
            transcendentals=rows * half,
        ),
    )(*operands)


def pack_kernel(layers, place_ref, *refs):
    *token_refs, result_ref = refs
    sides = len(token_refs) // (2 * layers)
    width = token_refs[0].shape[1]
    for side in range(sides):
        blocks = []
        for block in range(2):
            value = None
            for layer in range(layers):
                piece = token_refs[(block * layers + layer) * sides + side][...]
                value = piece if value is None else value + piece
            blocks.append(value)
        tokens = jnp.concatenate(blocks, axis=0)
        result_ref[:, side * width : (side + 1) * width] = jnp.dot(
            place_ref[...], tokens, preferred_element_type=jnp.float32
        ).astype(jnp.bfloat16)


def pack(placing, blocks):
    layers = len(blocks[0])
    operands = [half for block in blocks for layer in block for half in layer]
    rows, tokens = placing.shape
    width = sum(half.shape[1] for half in blocks[0][0])
    return pl.pallas_call(
        functools.partial(pack_kernel, layers),
        out_shape=jax.ShapeDtypeStruct((rows, width), jnp.bfloat16),
        compiler_params=pltpu.CompilerParams(vmem_limit_bytes=40 * MIB),
        cost_estimate=pl.CostEstimate(
            flops=2 * rows * tokens * width, bytes_accessed=6 * rows * width, transcendentals=0
        ),
    )(placing, *operands)


def combine_kernel(weights_ref, rows_ref, *out_refs):
    value = jnp.dot(weights_ref[...], rows_ref[...], preferred_element_type=jnp.float32)
    row = 0
    column = 0
    for out_ref in out_refs:
        height, width = out_ref.shape
        out_ref[...] = value[row : row + height, column : column + width].astype(out_ref.dtype)
        column += width
        if column == value.shape[1]:
            row, column = row + height, 0


def combine(weights, rows, out_shape):
    return pl.pallas_call(
        combine_kernel,
        out_shape=out_shape,
        compiler_params=pltpu.CompilerParams(vmem_limit_bytes=40 * MIB),
        cost_estimate=pl.CostEstimate(
            flops=2 * weights.shape[0] * rows.size,
            bytes_accessed=4 * rows.size,
            transcendentals=0,
        ),
    )(weights, rows)


def finish_kernel(residual_ref, own_ref, *refs):
    *part_refs, out_ref = refs
    width = part_refs[0].shape[1]
    for side in range(2):
        columns = slice(side * width, (side + 1) * width)
        value = residual_ref[:, columns] + own_ref[:, columns]
        for part_ref in part_refs[side::2]:
            value = value + part_ref[...].astype(jnp.float32)
        out_ref[:, columns] = value.astype(out_ref.dtype)


def local(
    hidden,
    queries,
    fresh_latent,
    latent_cache,
    page_table,
    cache_lengths,
    routes,
    route_gates,
    kv_up,
    out_proj,
    latent_gain,
    norm_gain,
    expert_in,
    expert_out,
):
    row_count = hidden.shape[1]
    model_width = hidden.shape[2]
    latent_width = latent_gain.shape[0]
    entry_width = fresh_latent.shape[2]
    rotary_width = entry_width - latent_width
    half_rotary = rotary_width // 2
    score_scale = 1.0 / math.sqrt(NOPE + rotary_width)
    length = cache_lengths[0]
    y_count = lax.axis_size("y")
    z_index = lax.axis_index("z")
    y_index = lax.axis_index("y")
    tok_index = z_index * y_count + y_index
    tok_count = PLANES * y_count

    first_row = tok_index * row_count
    offsets = jnp.arange(row_count, dtype=jnp.int32)
    positions = (length + first_row + offsets).astype(jnp.float32)
    frequency = theta_base ** (-jnp.arange(half_rotary, dtype=jnp.float32) * 2.0 / rotary_width)
    angles = frequency[:, None] * positions[None, :]
    cosine = jnp.cos(angles)
    sine = jnp.sin(angles)
    page_size = latent_cache.shape[2]
    top_count = routes.shape[2]
    own_facts = jnp.concatenate([routes[0].astype(jnp.bfloat16), route_gates[0].astype(jnp.bfloat16)], axis=1).T
    own_facts = jnp.pad(own_facts, ((0, FACT_ROWS - 2 * top_count), (0, 0)))
    own_block, new_entries = pl.pallas_call(
        entries_kernel,
        out_shape=[
            jax.ShapeDtypeStruct((entry_width + FACT_ROWS, page_size + row_count), jnp.bfloat16),
            jax.ShapeDtypeStruct((entry_width, row_count), jnp.bfloat16),
        ],
    )(
        fresh_latent[0].T,
        latent_cache[0, 0].T,
        own_facts,
        cosine,
        sine,
        latent_gain.reshape(latent_width // row_count, row_count),
    )

    inner = jnp.logical_or(z_index == 1, z_index == 2)

    def along_z(values):
        near = lax.ppermute(values, "z", NEAR)
        middle = lax.ppermute(values, "z", MIDDLE)
        middle_far = lax.ppermute(near, "z", MIDDLE)
        outward = lax.ppermute(middle, "z", OUTWARD)
        outward_far = lax.ppermute(middle_far, "z", OUTWARD)
        return near, (middle, outward), (middle_far, outward_far)

    near_block, *far_blocks = along_z(own_block)
    z_blocks = [own_block, near_block] + [jnp.where(inner, *pair) for pair in far_blocks]
    blocks = [
        z_block if j == 0 else shifted(z_block, "y", j)
        for z_block in z_blocks
        for j in range(y_count)
    ]

    query_rows = queries[0].reshape(row_count, H, NOPE + rotary_width)
    nope = query_rows[:, :, :NOPE].reshape(row_count, H * NOPE)
    turning = query_rows[:, :, NOPE:].astype(jnp.float32).transpose(1, 0, 2)
    front, back = turning[:, :, :half_rotary], turning[:, :, half_rotary:]
    token_cosine, token_sine = cosine.T[None], sine.T[None]
    rotated = jnp.concatenate(
        [front * token_cosine - back * token_sine, back * token_cosine + front * token_sine],
        axis=2,
    ).astype(jnp.bfloat16)

    places = jnp.stack(
        [length, z_index.astype(jnp.int32), y_index.astype(jnp.int32), jnp.int32(y_count)]
    )
    prepared = (jnp.concatenate([places, page_table[0]]), nope, rotated, kv_up)
    own_blocks, middle_blocks, last_blocks = (
        blocks[: 2 * y_count],
        blocks[2 * y_count : 3 * y_count],
        blocks[3 * y_count :],
    )
    state = attention_call(score_scale, 0, y_count, prepared, own_blocks, (), ())
    middle_blocks, last_blocks[0] = lax.optimization_barrier((middle_blocks, last_blocks[0]))
    state = attention_call(score_scale, 2, y_count, prepared, middle_blocks, state, ())
    column_facts = [block[entry_width:, page_size:] for block in z_blocks]
    column_facts, state = lax.optimization_barrier((column_facts, state))
    residual, *normed = attention_call(
        score_scale,
        3,
        y_count,
        prepared,
        last_blocks,
        state,
        (out_proj, hidden[0], norm_gain[None, :]),
    )

    slabs_here = expert_in.shape[0]
    experts_here = max(1, slabs_here // 2)
    x_count = lax.axis_size("x")
    plane_devices = x_count * 2 * y_count
    place = jnp.arange(plane_devices, dtype=jnp.int32)
    device_index = (place // y_count) * tok_count + z_index * y_count + place % y_count
    expert_ids = (
        (device_index * slabs_here)[:, None] // 2 + jnp.arange(experts_here, dtype=jnp.int32)
    ).reshape(-1)
    expert_ids = expert_ids.astype(jnp.float32)
    earlier = (offsets[:, None] < offsets[None, :]).astype(jnp.bfloat16)
    group = 2 * CAP
    expert_places = plane_devices * experts_here
    row_ids = jnp.arange(expert_places * group, dtype=jnp.int32)
    spread = (
        row_ids[:, None] // group == jnp.arange(expert_places, dtype=jnp.int32)[None, :]
    ).astype(jnp.bfloat16)
    wanted = (row_ids % group).astype(jnp.float32)[:, None]

    def pair_matrices(first, second):
        codes = []
        weights = []
        for index, fact in enumerate((first, second)):
            match = fact[None, :top_count, :].astype(jnp.float32) == expert_ids[:, None, None]
            named = jnp.any(match, axis=1)
            gates = fact[None, top_count : 2 * top_count, :].astype(jnp.float32)
            weights.append(jnp.sum(jnp.where(match, gates, 0.0), axis=1))
            rank = jnp.dot(
                named.astype(jnp.bfloat16), earlier, preferred_element_type=jnp.float32
            )
            codes.append(jnp.where(named, rank + index * CAP, -1.0))
        code = jnp.concatenate(codes, axis=1).astype(jnp.bfloat16)
        weight = jnp.concatenate(weights, axis=1).astype(jnp.bfloat16)
        chosen = jnp.dot(spread, code, preferred_element_type=jnp.float32) == wanted
        gate_rows = jnp.dot(spread, weight, preferred_element_type=jnp.float32)
        gate_rows = jnp.where(chosen, gate_rows, 0.0).astype(jnp.bfloat16)
        return chosen.astype(jnp.bfloat16), gate_rows.T

    near_matrices = pair_matrices(column_facts[0], column_facts[1])
    far_matrices = pair_matrices(column_facts[2], column_facts[3])

    def exchanged(values):
        return lax.all_to_all(values, PLANE_AXES, split_axis=0, concat_axis=0, tiled=True)

    def all_exchanged(rows):
        rows = rows.reshape(plane_devices, experts_here * group, model_width)
        return exchanged(rows).reshape(expert_places * group, model_width)

    near, *far = zip(*[along_z(half) for half in normed])
    near, middle = lax.optimization_barrier((near, [layers[0] for layers in far[0]]))
    far[0] = [(value, layers[1]) for value, layers in zip(middle, far[0])]
    near_rows = all_exchanged(pack(near_matrices[0], [[normed], [near]]))
    far = [list(zip(*block)) for block in far]
    near_rows, far = lax.optimization_barrier((near_rows, far))
    far_rows = all_exchanged(pack(far_matrices[0], far))
    near_rows = experts(near_rows, expert_in, expert_out, experts_here, group)
    far_rows = experts(far_rows, expert_in, expert_out, experts_here, group)

    def added(first, second):
        value = first.astype(jnp.float32) + second.astype(jnp.float32)
        return value.astype(jnp.bfloat16)

    def moved(value, pairs):
        return lax.ppermute(value, "z", pairs)

    half_shape = jax.ShapeDtypeStruct((row_count, model_width // 2), jnp.bfloat16)
    whole_shape = jax.ShapeDtypeStruct((row_count, model_width), jnp.float32)
    returned = combine(far_matrices[1], all_exchanged(far_rows), [half_shape] * 4)
    returned, near_rows = lax.optimization_barrier((returned, near_rows))
    middle_parts, far_parts = returned[:2], returned[2:]
    far_arrived = [moved(part, INWARD) for part in far_parts]
    middle_parts, far_arrived[1] = lax.optimization_barrier((middle_parts, far_arrived[1]))
    far_parts = [moved(added(*pair), MIDDLE) for pair in zip(far_parts, far_arrived)]
    middle_arrived = [moved(part, INWARD) for part in middle_parts]
    own_part, *near_parts = combine(
        near_matrices[1], all_exchanged(near_rows), [whole_shape] + [half_shape] * 2
    )
    own_part, middle_parts, middle_arrived = lax.optimization_barrier(
        (own_part, middle_parts, middle_arrived)
    )
    middle_arrived = [moved(added(*pair), MIDDLE) for pair in zip(middle_parts, middle_arrived)]
    near_arrived = [moved(added(*pair), NEAR) for pair in zip(near_parts, far_parts)]
    layer_out = pl.pallas_call(
        finish_kernel,
        out_shape=jax.ShapeDtypeStruct((row_count, model_width), jnp.bfloat16),
        compiler_params=pltpu.CompilerParams(vmem_limit_bytes=40 * MIB),
    )(residual, own_part, *near_arrived, *middle_arrived)
    return (layer_out[None], new_entries.T[None])


def solution(mesh):
    req_count, tok_count = mesh.devices.shape
    devices = mesh.devices.reshape(req_count // 2, 2, PLANES, tok_count // PLANES)
    fine = Mesh(devices, ("x", "core", "z", "y"))
    req = ("x", "core")
    tok = ("z", "y")
    placed = (
        P(req, tok, None),
        P(req, tok, None),
        P(req, tok, None),
        P(req, tok, None, None),
        P(req, None),
        P(req),
        P(req, tok, None),
        P(req, tok, None),
        P(),
        P(),
        P(),
        P(),
        P(("x", "core", "z", "y"), None, None),
        P(("x", "core", "z", "y"), None, None),
    )
    return jax.shard_map(
        local,
        mesh=fine,
        in_specs=placed,
        out_specs=(P(req, tok, None), P(req, tok, None)),
        check_vma=False,
    )
```

time: 761 us -> 254 us (0.33)
  the two profiles are of different devices: /device:TPU:0 before, /device:TPU:8 now
where the time goes in v1:
time: 254 us; the launch traced here: 252 us
  Pallas kernels  86.2 us (34%)
  waiting for transfers between devices  78.6 us (31%)
  starting transfers between devices  64.8 us (26%)
  other arithmetic  10.3 us (4%)
  local copies, waits for them, and re-layouts  8.59 us (3%)
    pallas_call x2, Pallas kernels, experts(): pl.pallas_call(functools.partial(experts_kernel, slabs_each, sorting), gr...  42.1 us
    pallas_call x3, Pallas kernels, attention_call(): pl.pallas_call(functools.partial(kernel, score_scale, first_slot, y_count...  36.1 us
    ppermute x10, waiting for transfers between devices, moved(): return lax.ppermute(value, 'z', pairs)  26.3 us
    all_to_all x4, waiting for transfers between devices, exchanged(): lax.all_to_all(values, PLANE_AXES, split_axis=0, concat_axis=0, tiled=True)  22.5 us
    ppermute x10, starting transfers between devices, moved(): return lax.ppermute(value, 'z', pairs)  17 us
    all_to_all x4, starting transfers between devices, exchanged(): lax.all_to_all(values, PLANE_AXES, split_axis=0, concat_axis=0, tiled=True)  15.4 us
    ppermute x3, waiting for transfers between devices, along_z(): outward_far = lax.ppermute(middle_far, 'z', OUTWARD)  10.4 us
    ppermute x3, starting transfers between devices, along_z(): middle = lax.ppermute(values, 'z', MIDDLE)  9.28 us
  transfers between devices with their start and end apart: 33, of which 21 were waited for; matrix products, arithmetic and copies ran while one was open for 6% of the time, Pallas kernels for 17%

profile of v1, /device:TPU:8, one launch (start us, length us, event | category | flops | bytes accessed | tf_op | source)
XLA Modules:
  0.0 252.4 jit_solution(882676360551713679)
XLA Ops:
  6.0 3.5 %collective-permute-start = (bf16[592,256]{1,0:T(8,128)(2,1)}, bf16[592,256]{1,0:T(8,128)(2,1)S(1)}, u32[]{:S(2)}, u32[]{:S(2)}) collective-permute-start(bf16[592,256]{1,0:T(8,128)(2,1)} %get-tuple-element.56.refs_4_), channel_id=1, source_target_pairs={{2,4},{4,2},{3,5},{5,3},{10,12},{12,10},{11,13},{13,11},{18,20},{2... | collective-permute-start | bytes 909320 | tf_op jit(solution)/shard_map/ppermute | solution.py:531
  18.9 2.9 %collective-permute-start.4 = (bf16[592,256]{1,0:T(8,128)(2,1)S(1)}, bf16[592,256]{1,0:T(8,128)(2,1)S(1)}, u32[]{:S(2)}, u32[]{:S(2)}) collective-permute-start(bf16[592,256]{1,0:T(8,128)(2,1)S(1)} %collective-permute-done.3.refs_6_), channel_id=1, source_target_pairs={{2,4},{4,2},{3,5},{5,3},{10,12},{12,10},{11,13},{13,11},{18,20},{2... | collective-permute-start | bytes 909320 | tf_op jit(solution)/shard_map/ppermute | solution.py:532
  26.6 2.0 collective-permute-done.4
  32.2 11.0 %shard_map.150 = (f32[8,256,1]{2,1,0:T(8,128)}, f32[8,256,1]{2,1,0:T(8,128)}, f32[8,256,512]{2,1,0:T(8,128)}) custom-call(s32[12]{0:T(128)} %concatenate.26.refs_0_, bf16[128,2048]{1,0:T(8,128)(2,1)} %copy.56.refs_1_, bf16[16,128,64]{2,1,0:T(8,128)(2,1)} %pad_maximum_fusion.refs_2_, bf16[512,4096]{1,0:T(8,128)(2,1)} %refs_3_.7, ...), custom_call_target="tpu_custom_call" | custom-call | flops 4563402752 | bytes 16777216 | tf_op jit(solution)/shard_map/pallas_call | solution.py:269
  45.6 10.9 %shard_map.151 = (f32[8,256,1]{2,1,0:T(8,128)}, f32[8,256,1]{2,1,0:T(8,128)}, f32[8,256,512]{2,1,0:T(8,128)}) custom-call(s32[12]{0:T(128)} %concatenate.26.refs_0_, bf16[128,2048]{1,0:T(8,128)(2,1)} %copy.56.refs_1_, bf16[16,128,64]{2,1,0:T(8,128)(2,1)} %pad_maximum_fusion.refs_2_, bf16[512,4096]{1,0:T(8,128)(2,1)} %refs_3_.7, bf16[592,256]{1,0:T(8,128)(2,1)} %copy-done.4, ...), custom_call_target="tpu_custom_call" | custom-call | flops 2281701376 | bytes 16777216 | tf_op jit(solution)/shard_map/pallas_call | solution.py:269
  57.5 14.2 %shard_map.152 = (f32[128,2048]{1,0:T(8,128)}, bf16[128,1024]{1,0:T(8,128)(2,1)}, bf16[128,1024]{1,0:T(8,128)(2,1)}) custom-call(s32[12]{0:T(128)} %concatenate.26.refs_0_, bf16[128,2048]{1,0:T(8,128)(2,1)} %copy.56.refs_1_, bf16[16,128,64]{2,1,0:T(8,128)(2,1)} %pad_maximum_fusion.refs_2_, bf16[512,4096]{1,0:T(8,128)(2,1)} %refs_3_.7, ...), custom_call_target="tpu_custom_call" | custom-call | flops 2281701376 | bytes 16777216 | tf_op jit(solution)/shard_map/pallas_call | solution.py:269
  71.7 2.5 collective-permute-start.11
  74.5 3.3 %collective-permute-start.12 = (bf16[128,1024]{1,0:T(8,128)(2,1)}, bf16[128,1024]{1,0:T(8,128)(2,1)S(1)}, u32[]{:S(2)}, u32[]{:S(2)}) collective-permute-start(bf16[128,1024]{1,0:T(8,128)(2,1)} %get-tuple-element.75.refs_1_), channel_id=1, source_target_pairs={{2,4},{4,2},{3,5},{5,3},{10,12},{12,10},{11,13},{13,11},{18,20},{2... | collective-permute-start | bytes 786440 | tf_op jit(solution)/shard_map/ppermute | solution.py:531
  79.6 2.8 %collective-permute-done.10.refs_3_ = bf16[128,1024]{1,0:T(8,128)(2,1)S(1)} collective-permute-done((bf16[128,1024]{1,0:T(8,128)(2,1)}, bf16[128,1024]{1,0:T(8,128)(2,1)S(1)}, u32[]{:S(2)}, u32[]{:S(2)}) %collective-permute-start.10) | collective-permute-done | bytes 262176 | tf_op jit(solution)/shard_map/ppermute | solution.py:530
  86.2 4.3 %all-to-all-start = ((bf16[8,56,2048]{2,1,0:T(8,128)(2,1)}), bf16[8,56,2048]{2,1,0:T(8,128)(2,1)}, u32[]{:S(2)}, u32[]{:S(2)}) async-start(bf16[8,56,2048]{2,1,0:T(8,128)(2,1)} %bitcast.19), calls=%async_computation | async-start | bytes 3670016 | tf_op jit(solution)/shard_map/all_to_all | solution.py:621
  90.5 3.0 %collective-permute-start.15 = (bf16[128,1024]{1,0:T(8,128)(2,1)S(1)}, bf16[128,1024]{1,0:T(8,128)(2,1)S(1)}, u32[]{:S(2)}, u32[]{:S(2)}) collective-permute-start(bf16[128,1024]{1,0:T(8,128)(2,1)S(1)} %collective-permute-done.9.refs_2_), channel_id=1, source_target_pairs={{2,4},{4,2},{3,5},{5,3},{10,12},{12,10},{11,13},{13,11},{18,20},{2... | collective-permute-start | bytes 786440 | tf_op jit(solution)/shard_map/ppermute | solution.py:532
  93.6 2.8 %collective-permute-start.16 = (bf16[128,1024]{1,0:T(8,128)(2,1)S(1)}, bf16[128,1024]{1,0:T(8,128)(2,1)S(1)}, u32[]{:S(2)}, u32[]{:S(2)}) collective-permute-start(bf16[128,1024]{1,0:T(8,128)(2,1)S(1)} %collective-permute-done.10.refs_3_), channel_id=1, source_target_pairs={{2,4},{4,2},{3,5},{5,3},{10,12},{12,10},{11,13},{13,11},{18,20},{2... | collective-permute-start | bytes 786440 | tf_op jit(solution)/shard_map/ppermute | solution.py:532
  99.2 2.4 collective-permute-done.15.refs_4_
  102.9 3.8 %collective-permute-done.16.refs_5_ = bf16[128,1024]{1,0:T(8,128)(2,1)S(1)} collective-permute-done((bf16[128,1024]{1,0:T(8,128)(2,1)S(1)}, bf16[128,1024]{1,0:T(8,128)(2,1)S(1)}, u32[]{:S(2)}, u32[]{:S(2)}) %collective-permute-start.16) | collective-permute-done | bytes 262176 | tf_op jit(solution)/shard_map/ppermute | solution.py:532
  110.1 5.6 %collective-permute-done.17.refs_6_ = bf16[128,1024]{1,0:T(8,128)(2,1)S(1)} collective-permute-done((bf16[128,1024]{1,0:T(8,128)(2,1)S(1)}, bf16[128,1024]{1,0:T(8,128)(2,1)S(1)}, u32[]{:S(2)}, u32[]{:S(2)}) %collective-permute-start.17) | collective-permute-done | bytes 262176 | tf_op jit(solution)/shard_map/ppermute | solution.py:534
  115.7 4.7 %collective-permute-done.18.refs_7_ = bf16[128,1024]{1,0:T(8,128)(2,1)S(1)} collective-permute-done((bf16[128,1024]{1,0:T(8,128)(2,1)S(1)}, bf16[128,1024]{1,0:T(8,128)(2,1)S(1)}, u32[]{:S(2)}, u32[]{:S(2)}) %collective-permute-start.18) | collective-permute-done | bytes 262176 | tf_op jit(solution)/shard_map/ppermute | solution.py:534
  122.4 3.9 %all-to-all-start.1 = ((bf16[8,56,2048]{2,1,0:T(8,128)(2,1)}), bf16[8,56,2048]{2,1,0:T(8,128)(2,1)S(1)}, u32[]{:S(2)}, u32[]{:S(2)}) async-start(bf16[8,56,2048]{2,1,0:T(8,128)(2,1)} %bitcast.21), calls=%async_computation.1 | async-start | bytes 3670016 | tf_op jit(solution)/shard_map/all_to_all | solution.py:621
  128.1 21.1 %all-to-all-done.1 = bf16[8,56,2048]{2,1,0:T(8,128)(2,1)S(1)} async-done(((bf16[8,56,2048]{2,1,0:T(8,128)(2,1)}), bf16[8,56,2048]{2,1,0:T(8,128)(2,1)S(1)}, u32[]{:S(2)}, u32[]{:S(2)}) %all-to-all-start.1) | async-done | bytes 1835040 | tf_op jit(solution)/shard_map/all_to_all | solution.py:621
  150.4 21.0 %shard_map.155 = bf16[448,2048]{1,0:T(8,128)(2,1)} custom-call(bf16[448,2048]{1,0:T(8,128)(2,1)} %bitcast.49, bf16[2,224,448]{2,1,0:T(8,128)(2,1)} %fusion.8.refs_0_, bf16[2,448,224]{2,1,0:T(8,128)(2,1)} %fusion.9.refs_1_, bf16[4,2048,1408]{2,1,0:T(8,128)(2,1)} %refs_3_.9, bf16[4,2048,1408]{2,1,0:T(8,128)(2,1)} %refs_3_.9, bf16[4,704,2048]{2,1,0:T(8,128)(2,1)} %refs_5_.3, ...), custom_call_target="tpu_custom_call" | custom-call | flops 7751073792 | bytes 34603008 | tf_op jit(solution)/shard_map/pallas_call | solution.py:383
  171.5 3.6 %all-to-all-start.2 = ((bf16[8,56,2048]{2,1,0:T(8,128)(2,1)}), bf16[8,56,2048]{2,1,0:T(8,128)(2,1)S(1)}, u32[]{:S(2)}, u32[]{:S(2)}) async-start(bf16[8,56,2048]{2,1,0:T(8,128)(2,1)} %bitcast.48), calls=%async_computation.2 | async-start | bytes 3670016 | tf_op jit(solution)/shard_map/all_to_all | solution.py:621
  175.5 21.1 %shard_map.157 = bf16[448,2048]{1,0:T(8,128)(2,1)} custom-call(bf16[448,2048]{1,0:T(8,128)(2,1)} %bitcast.20.x_ref, bf16[2,224,448]{2,1,0:T(8,128)(2,1)} %fusion.8.refs_0_, bf16[2,448,224]{2,1,0:T(8,128)(2,1)} %fusion.9.refs_1_, bf16[4,2048,1408]{2,1,0:T(8,128)(2,1)} %refs_3_.9, bf16[4,2048,1408]{2,1,0:T(8,128)(2,1)} %refs_3_.9, ...), custom_call_target="tpu_custom_call" | custom-call | flops 7751073792 | bytes 34603008 | tf_op jit(solution)/shard_map/pallas_call | solution.py:383
  198.7 3.6 %all-to-all-start.3 = ((bf16[8,56,2048]{2,1,0:T(8,128)(2,1)}), bf16[8,56,2048]{2,1,0:T(8,128)(2,1)S(1)}, u32[]{:S(2)}, u32[]{:S(2)}) async-start(bf16[8,56,2048]{2,1,0:T(8,128)(2,1)} %bitcast.47), calls=%async_computation.3 | async-start | bytes 3670016 | tf_op jit(solution)/shard_map/all_to_all | solution.py:621
  205.2 8.1 %collective-permute-done.19 = bf16[128,1024]{1,0:T(8,128)(2,1)S(1)} collective-permute-done((bf16[128,1024]{1,0:T(8,128)(2,1)S(1)}, bf16[128,1024]{1,0:T(8,128)(2,1)S(1)}, u32[]{:S(2)}, u32[]{:S(2)}) %collective-permute-start.19) | collective-permute-done | bytes 262176 | tf_op jit(solution)/shard_map/ppermute | solution.py:642
  215.9 3.0 %collective-permute-done.22 = bf16[128,1024]{1,0:T(8,128)(2,1)S(1)} collective-permute-done((bf16[128,1024]{1,0:T(8,128)(2,1)S(1)}, bf16[128,1024]{1,0:T(8,128)(2,1)S(1)}, u32[]{:S(2)}, u32[]{:S(2)}) %collective-permute-start.22) | collective-permute-done | bytes 262176 | tf_op jit(solution)/shard_map/ppermute | solution.py:642
  219.7 3.0 %collective-permute-start.23 = (bf16[128,1024]{1,0:T(8,128)(2,1)}, bf16[128,1024]{1,0:T(8,128)(2,1)}, u32[]{:S(2)}, u32[]{:S(2)}) collective-permute-start(bf16[128,1024]{1,0:T(8,128)(2,1)} %add_convert_fusion.6), channel_id=1, source_target_pairs={{2,4},{4,2},{3,5},{5,3},{10,12},{12,10},{11,13},{13,11},{18,20},{2... | collective-permute-start | bytes 786440 | tf_op jit(solution)/shard_map/ppermute | solution.py:642
  223.5 2.8 %collective-permute-start.25 = (bf16[128,1024]{1,0:T(8,128)(2,1)}, bf16[128,1024]{1,0:T(8,128)(2,1)}, u32[]{:S(2)}, u32[]{:S(2)}) collective-permute-start(bf16[128,1024]{1,0:T(8,128)(2,1)} %add_convert_fusion.4), channel_id=1, source_target_pairs={{2,4},{4,2},{3,5},{5,3},{10,12},{12,10},{11,13},{13,11},{18,20},{2... | collective-permute-start | bytes 786440 | tf_op jit(solution)/shard_map/ppermute | solution.py:642
  227.1 2.8 %collective-permute-done.21 = bf16[128,1024]{1,0:T(8,128)(2,1)S(1)} collective-permute-done((bf16[128,1024]{1,0:T(8,128)(2,1)S(1)}, bf16[128,1024]{1,0:T(8,128)(2,1)S(1)}, u32[]{:S(2)}, u32[]{:S(2)}) %collective-permute-start.21) | collective-permute-done | bytes 262176 | tf_op jit(solution)/shard_map/ppermute | solution.py:642
  232.2 2.9 %collective-permute-done.25 = bf16[128,1024]{1,0:T(8,128)(2,1)} collective-permute-done((bf16[128,1024]{1,0:T(8,128)(2,1)}, bf16[128,1024]{1,0:T(8,128)(2,1)}, u32[]{:S(2)}, u32[]{:S(2)}) %collective-permute-start.25) | collective-permute-done | bytes 262176 | tf_op jit(solution)/shard_map/ppermute | solution.py:642
  237.3 3.0 %collective-permute-start.27 = (bf16[128,1024]{1,0:T(8,128)(2,1)S(1)}, bf16[128,1024]{1,0:T(8,128)(2,1)S(1)}, u32[]{:S(2)}, u32[]{:S(2)}) collective-permute-start(bf16[128,1024]{1,0:T(8,128)(2,1)S(1)} %add_convert_fusion.2), channel_id=1, source_target_pairs={{2,4},{4,2},{3,5},{5,3},{10,12},{12,10},{11,13},{13,11},{18,20},{2... | collective-permute-start | bytes 786440 | tf_op jit(solution)/shard_map/ppermute | solution.py:642
  240.3 2.9 %collective-permute-start.28 = (bf16[128,1024]{1,0:T(8,128)(2,1)S(1)}, bf16[128,1024]{1,0:T(8,128)(2,1)S(1)}, u32[]{:S(2)}, u32[]{:S(2)}) collective-permute-start(bf16[128,1024]{1,0:T(8,128)(2,1)S(1)} %add_convert_fusion.1), channel_id=1, source_target_pairs={{2,4},{4,2},{3,5},{5,3},{10,12},{12,10},{11,13},{13,11},{18,20},{2... | collective-permute-start | bytes 786440 | tf_op jit(solution)/shard_map/ppermute | solution.py:642
  244.6 3.8 %collective-permute-done.27.refs_2_ = bf16[128,1024]{1,0:T(8,128)(2,1)S(1)} collective-permute-done((bf16[128,1024]{1,0:T(8,128)(2,1)S(1)}, bf16[128,1024]{1,0:T(8,128)(2,1)S(1)}, u32[]{:S(2)}, u32[]{:S(2)}) %collective-permute-start.27) | collective-permute-done | bytes 262176 | tf_op jit(solution)/shard_map/ppermute | solution.py:642
  248.4 3.1 %collective-permute-done.28.refs_3_ = bf16[128,1024]{1,0:T(8,128)(2,1)S(1)} collective-permute-done((bf16[128,1024]{1,0:T(8,128)(2,1)S(1)}, bf16[128,1024]{1,0:T(8,128)(2,1)S(1)}, u32[]{:S(2)}, u32[]{:S(2)}) %collective-permute-start.28) | collective-permute-done | bytes 262176 | tf_op jit(solution)/shard_map/ppermute | solution.py:642
  (118 shorter events, 61.2 us)
Async XLA Ops:
  6.0 11.0 %collective-permute-start = (bf16[592,256]{1,0:T(8,128)(2,1)}, bf16[592,256]{1,0:T(8,128)(2,1)S(1)}, u32[]{:S(2)}, u32[]{:S(2)}) collective-permute-start(bf16[592,256]{1,0:T(8,128)(2,1)} %get-tuple-element.56.refs_4_), channel_id=1, source_target_pairs={{2,4},{4,2},{3,5},{5,3},{10,12},{12,10},{11,13},{13,11},{18,20},{2... | collective-permute-start | bytes 909320 | tf_op jit(solution)/shard_map/ppermute | solution.py:531
  9.5 9.5 %collective-permute-start.3 = (bf16[592,256]{1,0:T(8,128)(2,1)}, bf16[592,256]{1,0:T(8,128)(2,1)S(1)}, u32[]{:S(2)}, u32[]{:S(2)}) collective-permute-start(bf16[592,256]{1,0:T(8,128)(2,1)} %get-tuple-element.56.refs_4_), channel_id=1, source_target_pairs={{0,2},{2,0},{4,6},{6,4},{1,3},{3,1},{5,7},{7,5},{8,10},{10,8},{12,... | collective-permute-start | bytes 909320 | tf_op jit(solution)/shard_map/ppermute | solution.py:530
  9.5 20.6 %collective-permute-start.7 = (bf16[592,256]{1,0:T(8,128)(2,1)}, bf16[592,256]{1,0:T(8,128)(2,1)S(1)}, u32[]{:S(2)}, u32[]{:S(2)}) collective-permute-start(bf16[592,256]{1,0:T(8,128)(2,1)} %get-tuple-element.56.refs_4_), channel_id=1, source_target_pairs={{0,1},{1,0},{2,3},{3,2},{4,5},{5,4},{6,7},{7,6},{8,9},{9,8},{10,11... | collective-permute-start | bytes 909320 | tf_op jit(solution)/shard_map/ppermute | solution.py:35
  17.0 9.0 %collective-permute-start.1 = (bf16[592,256]{1,0:T(8,128)(2,1)S(1)}, bf16[592,256]{1,0:T(8,128)(2,1)S(1)}, u32[]{:S(2)}, u32[]{:S(2)}) collective-permute-start(bf16[592,256]{1,0:T(8,128)(2,1)S(1)} %collective-permute-done), channel_id=1, source_target_pairs={{2,0},{4,6},{3,1},{5,7},{10,8},{12,14},{11,9},{13,15},{18,16},{20,... | collective-permute-start | bytes 909320 | tf_op jit(solution)/shard_map/ppermute | solution.py:533
  18.9 9.7 %collective-permute-start.4 = (bf16[592,256]{1,0:T(8,128)(2,1)S(1)}, bf16[592,256]{1,0:T(8,128)(2,1)S(1)}, u32[]{:S(2)}, u32[]{:S(2)}) collective-permute-start(bf16[592,256]{1,0:T(8,128)(2,1)S(1)} %collective-permute-done.3.refs_6_), channel_id=1, source_target_pairs={{2,4},{4,2},{3,5},{5,3},{10,12},{12,10},{11,13},{13,11},{18,20},{2... | collective-permute-start | bytes 909320 | tf_op jit(solution)/shard_map/ppermute | solution.py:532
  21.9 10.3 %collective-permute-start.8 = (bf16[592,256]{1,0:T(8,128)(2,1)S(1)}, bf16[592,256]{1,0:T(8,128)(2,1)}, u32[]{:S(2)}, u32[]{:S(2)}) collective-permute-start(bf16[592,256]{1,0:T(8,128)(2,1)S(1)} %collective-permute-done.3.refs_6_), channel_id=1, source_target_pairs={{0,1},{1,0},{2,3},{3,2},{4,5},{5,4},{6,7},{7,6},{8,9},{9,8},{10,11... | collective-permute-start | bytes 909320 | tf_op jit(solution)/shard_map/ppermute | solution.py:35
  26.0 18.8 %collective-permute-start.2 = (bf16[592,256]{1,0:T(8,128)(2,1)S(1)}, bf16[592,256]{1,0:T(8,128)(2,1)S(1)}, u32[]{:S(2)}, u32[]{:S(2)}) collective-permute-start(bf16[592,256]{1,0:T(8,128)(2,1)S(1)} %broadcast_select_fusion.1.refs_4_), channel_id=1, source_target_pairs={{0,1},{1,0},{2,3},{3,2},{4,5},{5,4},{6,7},{7,6},{8,9},{9,8},{10,11... | collective-permute-start | bytes 909320 | tf_op jit(solution)/shard_map/ppermute | solution.py:35
  28.6 14.6 %collective-permute-start.5 = (bf16[592,256]{1,0:T(8,128)(2,1)S(1)}, bf16[592,256]{1,0:T(8,128)(2,1)S(1)}, u32[]{:S(2)}, u32[]{:S(2)}) collective-permute-start(bf16[592,256]{1,0:T(8,128)(2,1)S(1)} %collective-permute-done.4), channel_id=1, source_target_pairs={{2,0},{4,6},{3,1},{5,7},{10,8},{12,14},{11,9},{13,15},{18,16},{20,... | collective-permute-start | bytes 909320 | tf_op jit(solution)/shard_map/ppermute | solution.py:534
  43.3 13.5 %collective-permute-start.6 = (bf16[592,256]{1,0:T(8,128)(2,1)S(1)}, bf16[592,256]{1,0:T(8,128)(2,1)S(1)}, u32[]{:S(2)}, u32[]{:S(2)}) collective-permute-start(bf16[592,256]{1,0:T(8,128)(2,1)S(1)} %broadcast_select_fusion.refs_4_), channel_id=1, source_target_pairs={{0,1},{1,0},{2,3},{3,2},{4,5},{5,4},{6,7},{7,6},{8,9},{9,8},{10,11... | collective-permute-start | bytes 909320 | tf_op jit(solution)/shard_map/ppermute | solution.py:35
  71.7 10.7 %collective-permute-start.11 = (bf16[128,1024]{1,0:T(8,128)(2,1)}, bf16[128,1024]{1,0:T(8,128)(2,1)S(1)}, u32[]{:S(2)}, u32[]{:S(2)}) collective-permute-start(bf16[128,1024]{1,0:T(8,128)(2,1)} %get-tuple-element.74.refs_0_), channel_id=1, source_target_pairs={{2,4},{4,2},{3,5},{5,3},{10,12},{12,10},{11,13},{13,11},{18,20},{2... | collective-permute-start | bytes 786440 | tf_op jit(solution)/shard_map/ppermute | solution.py:531
  74.2 8.2 %collective-permute-start.10 = (bf16[128,1024]{1,0:T(8,128)(2,1)}, bf16[128,1024]{1,0:T(8,128)(2,1)S(1)}, u32[]{:S(2)}, u32[]{:S(2)}) collective-permute-start(bf16[128,1024]{1,0:T(8,128)(2,1)} %get-tuple-element.75.refs_1_), channel_id=1, source_target_pairs={{0,2},{2,0},{4,6},{6,4},{1,3},{3,1},{5,7},{7,5},{8,10},{10,8},{12,... | collective-permute-start | bytes 786440 | tf_op jit(solution)/shard_map/ppermute | solution.py:530
  74.5 9.8 %collective-permute-start.12 = (bf16[128,1024]{1,0:T(8,128)(2,1)}, bf16[128,1024]{1,0:T(8,128)(2,1)S(1)}, u32[]{:S(2)}, u32[]{:S(2)}) collective-permute-start(bf16[128,1024]{1,0:T(8,128)(2,1)} %get-tuple-element.75.refs_1_), channel_id=1, source_target_pairs={{2,4},{4,2},{3,5},{5,3},{10,12},{12,10},{11,13},{13,11},{18,20},{2... | collective-permute-start | bytes 786440 | tf_op jit(solution)/shard_map/ppermute | solution.py:531
  86.2 34.3 %all-to-all-start = ((bf16[8,56,2048]{2,1,0:T(8,128)(2,1)}), bf16[8,56,2048]{2,1,0:T(8,128)(2,1)}, u32[]{:S(2)}, u32[]{:S(2)}) async-start(bf16[8,56,2048]{2,1,0:T(8,128)(2,1)} %bitcast.19), calls=%async_computation | async-start | bytes 3670016 | tf_op jit(solution)/shard_map/all_to_all | solution.py:621
  90.5 11.0 %collective-permute-start.15 = (bf16[128,1024]{1,0:T(8,128)(2,1)S(1)}, bf16[128,1024]{1,0:T(8,128)(2,1)S(1)}, u32[]{:S(2)}, u32[]{:S(2)}) collective-permute-start(bf16[128,1024]{1,0:T(8,128)(2,1)S(1)} %collective-permute-done.9.refs_2_), channel_id=1, source_target_pairs={{2,4},{4,2},{3,5},{5,3},{10,12},{12,10},{11,13},{13,11},{18,20},{2... | collective-permute-start | bytes 786440 | tf_op jit(solution)/shard_map/ppermute | solution.py:532
  93.6 13.1 %collective-permute-start.16 = (bf16[128,1024]{1,0:T(8,128)(2,1)S(1)}, bf16[128,1024]{1,0:T(8,128)(2,1)S(1)}, u32[]{:S(2)}, u32[]{:S(2)}) collective-permute-start(bf16[128,1024]{1,0:T(8,128)(2,1)S(1)} %collective-permute-done.10.refs_3_), channel_id=1, source_target_pairs={{2,4},{4,2},{3,5},{5,3},{10,12},{12,10},{11,13},{13,11},{18,20},{2... | collective-permute-start | bytes 786440 | tf_op jit(solution)/shard_map/ppermute | solution.py:532
  96.6 12.2 %collective-permute-start.13 = (bf16[128,1024]{1,0:T(8,128)(2,1)S(1)}, bf16[128,1024]{1,0:T(8,128)(2,1)S(1)}, u32[]{:S(2)}, u32[]{:S(2)}) collective-permute-start(bf16[128,1024]{1,0:T(8,128)(2,1)S(1)} %collective-permute-done.11.refs_0_), channel_id=1, source_target_pairs={{2,0},{4,6},{3,1},{5,7},{10,8},{12,14},{11,9},{13,15},{18,16},{20,... | collective-permute-start | bytes 786440 | tf_op jit(solution)/shard_map/ppermute | solution.py:533
  97.9 12.3 %collective-permute-start.14 = (bf16[128,1024]{1,0:T(8,128)(2,1)S(1)}, bf16[128,1024]{1,0:T(8,128)(2,1)S(1)}, u32[]{:S(2)}, u32[]{:S(2)}) collective-permute-start(bf16[128,1024]{1,0:T(8,128)(2,1)S(1)} %collective-permute-done.12.refs_1_), channel_id=1, source_target_pairs={{2,0},{4,6},{3,1},{5,7},{10,8},{12,14},{11,9},{13,15},{18,16},{20,... | collective-permute-start | bytes 786440 | tf_op jit(solution)/shard_map/ppermute | solution.py:533
  101.6 14.2 %collective-permute-start.17 = (bf16[128,1024]{1,0:T(8,128)(2,1)S(1)}, bf16[128,1024]{1,0:T(8,128)(2,1)S(1)}, u32[]{:S(2)}, u32[]{:S(2)}) collective-permute-start(bf16[128,1024]{1,0:T(8,128)(2,1)S(1)} %collective-permute-done.15.refs_4_), channel_id=1, source_target_pairs={{2,0},{4,6},{3,1},{5,7},{10,8},{12,14},{11,9},{13,15},{18,16},{20,... | collective-permute-start | bytes 786440 | tf_op jit(solution)/shard_map/ppermute | solution.py:534
  106.6 13.8 %collective-permute-start.18 = (bf16[128,1024]{1,0:T(8,128)(2,1)S(1)}, bf16[128,1024]{1,0:T(8,128)(2,1)S(1)}, u32[]{:S(2)}, u32[]{:S(2)}) collective-permute-start(bf16[128,1024]{1,0:T(8,128)(2,1)S(1)} %collective-permute-done.16.refs_5_), channel_id=1, source_target_pairs={{2,0},{4,6},{3,1},{5,7},{10,8},{12,14},{11,9},{13,15},{18,16},{20,... | collective-permute-start | bytes 786440 | tf_op jit(solution)/shard_map/ppermute | solution.py:534
  122.4 26.8 %all-to-all-start.1 = ((bf16[8,56,2048]{2,1,0:T(8,128)(2,1)}), bf16[8,56,2048]{2,1,0:T(8,128)(2,1)S(1)}, u32[]{:S(2)}, u32[]{:S(2)}) async-start(bf16[8,56,2048]{2,1,0:T(8,128)(2,1)} %bitcast.21), calls=%async_computation.1 | async-start | bytes 3670016 | tf_op jit(solution)/shard_map/all_to_all | solution.py:621
  171.5 26.5 %all-to-all-start.2 = ((bf16[8,56,2048]{2,1,0:T(8,128)(2,1)}), bf16[8,56,2048]{2,1,0:T(8,128)(2,1)S(1)}, u32[]{:S(2)}, u32[]{:S(2)}) async-start(bf16[8,56,2048]{2,1,0:T(8,128)(2,1)} %bitcast.48), calls=%async_computation.2 | async-start | bytes 3670016 | tf_op jit(solution)/shard_map/all_to_all | solution.py:621
  198.7 27.6 %all-to-all-start.3 = ((bf16[8,56,2048]{2,1,0:T(8,128)(2,1)}), bf16[8,56,2048]{2,1,0:T(8,128)(2,1)S(1)}, u32[]{:S(2)}, u32[]{:S(2)}) async-start(bf16[8,56,2048]{2,1,0:T(8,128)(2,1)} %bitcast.47), calls=%async_computation.3 | async-start | bytes 3670016 | tf_op jit(solution)/shard_map/all_to_all | solution.py:621
  202.3 11.0 %collective-permute-start.19 = (bf16[128,1024]{1,0:T(8,128)(2,1)S(1)}, bf16[128,1024]{1,0:T(8,128)(2,1)S(1)}, u32[]{:S(2)}, u32[]{:S(2)}) collective-permute-start(bf16[128,1024]{1,0:T(8,128)(2,1)S(1)} %get-tuple-element.97), channel_id=1, source_target_pairs={{0,2},{6,4},{1,3},{7,5},{8,10},{14,12},{9,11},{15,13},{16,18},{22,... | collective-permute-start | bytes 786440 | tf_op jit(solution)/shard_map/ppermute | solution.py:642
  203.6 15.3 %collective-permute-start.22 = (bf16[128,1024]{1,0:T(8,128)(2,1)S(1)}, bf16[128,1024]{1,0:T(8,128)(2,1)S(1)}, u32[]{:S(2)}, u32[]{:S(2)}) collective-permute-start(bf16[128,1024]{1,0:T(8,128)(2,1)S(1)} %get-tuple-element.102), channel_id=1, source_target_pairs={{0,2},{6,4},{1,3},{7,5},{8,10},{14,12},{9,11},{15,13},{16,18},{22,... | collective-permute-start | bytes 786440 | tf_op jit(solution)/shard_map/ppermute | solution.py:642
  213.3 13.7 %collective-permute-start.20 = (bf16[128,1024]{1,0:T(8,128)(2,1)S(1)}, bf16[128,1024]{1,0:T(8,128)(2,1)}, u32[]{:S(2)}, u32[]{:S(2)}) collective-permute-start(bf16[128,1024]{1,0:T(8,128)(2,1)S(1)} %get-tuple-element.105), channel_id=1, source_target_pairs={{0,2},{6,4},{1,3},{7,5},{8,10},{14,12},{9,11},{15,13},{16,18},{22,... | collective-permute-start | bytes 786440 | tf_op jit(solution)/shard_map/ppermute | solution.py:642
  214.6 15.2 %collective-permute-start.21 = (bf16[128,1024]{1,0:T(8,128)(2,1)S(1)}, bf16[128,1024]{1,0:T(8,128)(2,1)S(1)}, u32[]{:S(2)}, u32[]{:S(2)}) collective-permute-start(bf16[128,1024]{1,0:T(8,128)(2,1)S(1)} %get-tuple-element.107), channel_id=1, source_target_pairs={{0,2},{6,4},{1,3},{7,5},{8,10},{14,12},{9,11},{15,13},{16,18},{22,... | collective-permute-start | bytes 786440 | tf_op jit(solution)/shard_map/ppermute | solution.py:642
  219.7 11.4 %collective-permute-start.23 = (bf16[128,1024]{1,0:T(8,128)(2,1)}, bf16[128,1024]{1,0:T(8,128)(2,1)}, u32[]{:S(2)}, u32[]{:S(2)}) collective-permute-start(bf16[128,1024]{1,0:T(8,128)(2,1)} %add_convert_fusion.6), channel_id=1, source_target_pairs={{2,4},{4,2},{3,5},{5,3},{10,12},{12,10},{11,13},{13,11},{18,20},{2... | collective-permute-start | bytes 786440 | tf_op jit(solution)/shard_map/ppermute | solution.py:642
  223.5 11.6 %collective-permute-start.25 = (bf16[128,1024]{1,0:T(8,128)(2,1)}, bf16[128,1024]{1,0:T(8,128)(2,1)}, u32[]{:S(2)}, u32[]{:S(2)}) collective-permute-start(bf16[128,1024]{1,0:T(8,128)(2,1)} %add_convert_fusion.4), channel_id=1, source_target_pairs={{2,4},{4,2},{3,5},{5,3},{10,12},{12,10},{11,13},{13,11},{18,20},{2... | collective-permute-start | bytes 786440 | tf_op jit(solution)/shard_map/ppermute | solution.py:642
  232.2 11.0 %collective-permute-start.24 = (bf16[128,1024]{1,0:T(8,128)(2,1)S(1)}, bf16[128,1024]{1,0:T(8,128)(2,1)S(1)}, u32[]{:S(2)}, u32[]{:S(2)}) collective-permute-start(bf16[128,1024]{1,0:T(8,128)(2,1)S(1)} %add_convert_fusion.5), channel_id=1, source_target_pairs={{0,2},{2,0},{4,6},{6,4},{1,3},{3,1},{5,7},{7,5},{8,10},{10,8},{12,... | collective-permute-start | bytes 786440 | tf_op jit(solution)/shard_map/ppermute | solution.py:642
  236.2 8.4 %collective-permute-start.26 = (bf16[128,1024]{1,0:T(8,128)(2,1)S(1)}, bf16[128,1024]{1,0:T(8,128)(2,1)S(1)}, u32[]{:S(2)}, u32[]{:S(2)}) collective-permute-start(bf16[128,1024]{1,0:T(8,128)(2,1)S(1)} %add_convert_fusion.3), channel_id=1, source_target_pairs={{0,2},{2,0},{4,6},{6,4},{1,3},{3,1},{5,7},{7,5},{8,10},{10,8},{12,... | collective-permute-start | bytes 786440 | tf_op jit(solution)/shard_map/ppermute | solution.py:642
  237.3 11.1 %collective-permute-start.27 = (bf16[128,1024]{1,0:T(8,128)(2,1)S(1)}, bf16[128,1024]{1,0:T(8,128)(2,1)S(1)}, u32[]{:S(2)}, u32[]{:S(2)}) collective-permute-start(bf16[128,1024]{1,0:T(8,128)(2,1)S(1)} %add_convert_fusion.2), channel_id=1, source_target_pairs={{2,4},{4,2},{3,5},{5,3},{10,12},{12,10},{11,13},{13,11},{18,20},{2... | collective-permute-start | bytes 786440 | tf_op jit(solution)/shard_map/ppermute | solution.py:642
  240.3 11.2 %collective-permute-start.28 = (bf16[128,1024]{1,0:T(8,128)(2,1)S(1)}, bf16[128,1024]{1,0:T(8,128)(2,1)S(1)}, u32[]{:S(2)}, u32[]{:S(2)}) collective-permute-start(bf16[128,1024]{1,0:T(8,128)(2,1)S(1)} %add_convert_fusion.1), channel_id=1, source_target_pairs={{2,4},{4,2},{3,5},{5,3},{10,12},{12,10},{11,13},{13,11},{18,20},{2... | collective-permute-start | bytes 786440 | tf_op jit(solution)/shard_map/ppermute | solution.py:642
  (12 other events, 117.5 us)

commit v2 on v1

--- a/solution.py
+++ b/solution.py
@@ -27,6 +27,9 @@
 NEAR = [(0, 1), (1, 0), (2, 3), (3, 2)]
 MIDDLE = [(1, 2), (2, 1)]
 OUTWARD = [(1, 0), (2, 3)]
+ACROSS = [(0, 3), (3, 0)]
+FROM_END = [(3, 1), (0, 2)]
+TO_END = [(1, 3), (2, 0)]
 INWARD = [(0, 1), (3, 2)]
 
 
@@ -151,7 +154,7 @@
 def first_attention_kernel(score_scale, first_slot, y_count, block_count, *refs):
     facts_ref, nope_ref, rotated_ref, up_ref = refs[:4]
     block_refs = refs[4 : 4 + block_count]
-    *old_refs, highest_ref, totals_ref, mixed_ref, keys_ref, marks_ref = refs[4 + block_count :]
+    highest_ref, totals_ref, mixed_ref, keys_ref, marks_ref = refs[-5:]
 
     @pl.when(pl.program_id(0) == 0)
     def _():
@@ -160,10 +163,7 @@
         )
 
     results = attend(nope_ref, rotated_ref, up_ref, facts_ref, marks_ref, keys_ref, score_scale)
-    for group, result in enumerate(results):
-        if old_refs:
-            result = merged(result, group, old_refs, score_scale)
-        highest, totals, mixed = result
+    for group, (highest, totals, mixed) in enumerate(results):
         highest_ref[group] = highest
         totals_ref[group] = totals
         mixed_ref[group] = mixed
@@ -218,7 +218,7 @@
         right_ref[...] = normed[:, left_ref.shape[1] :]
 
 
-def attention_call(score_scale, first_slot, y_count, queries, blocks, old, tail):
+def attention_call(score_scale, first_slot, y_count, queries, blocks, old, tail, part=None):
     facts, nope, rotated, up = queries
     rows = nope.shape[0]
     latent_width = up.shape[0]
@@ -227,21 +227,28 @@
     rotary_width = rotated.shape[2]
     heads = PAIR * GROUPS
     whole = lambda *shape: pl.BlockSpec(shape, lambda s: (0,) * len(shape))
+    index, count = part or (0, 1)
+    steps = H // heads // count
+    start = index * steps
     state_specs = [
-        pl.BlockSpec((GROUPS, PAIR * rows, size), lambda s: (s, 0, 0))
+        pl.BlockSpec((GROUPS, PAIR * rows, size), lambda s: (s + start, 0, 0))
         for size in (1, 1, latent_width)
     ]
     in_specs = [
         pl.BlockSpec(memory_space=pltpu.SMEM),
-        pl.BlockSpec((rows, heads * NOPE), lambda s: (0, s)),
-        pl.BlockSpec((heads, rows, rotary_width), lambda s: (s, 0, 0)),
-        pl.BlockSpec((latent_width, heads * (NOPE + VD)), lambda s: (0, s)),
+        pl.BlockSpec((rows, heads * NOPE), lambda s: (0, s + start)),
+        pl.BlockSpec((heads, rows, rotary_width), lambda s: (s + start, 0, 0)),
+        pl.BlockSpec((latent_width, heads * (NOPE + VD)), lambda s: (0, s + start)),
     ] + [whole(block_height, width)] * len(blocks)
     scratch = [
         pltpu.VMEM((latent_width + rotary_width, keys), jnp.bfloat16),
         pltpu.VMEM((1, keys), jnp.int32),
     ]
-    if old:
+    aliases = {}
+    if old and part:
+        aliases = {len(in_specs) + i: i for i in range(len(old))}
+        in_specs += [pl.BlockSpec(memory_space=pl.ANY)] * len(old)
+    elif old:
         in_specs += state_specs
     if tail:
         proj, hidden, gain = tail
@@ -268,16 +275,17 @@
         ]
     return pl.pallas_call(
         functools.partial(kernel, score_scale, first_slot, y_count, len(blocks)),
-        grid=(H // heads,),
+        grid=(steps,),
         in_specs=in_specs,
         out_specs=out_specs,
         out_shape=out_shape,
         scratch_shapes=scratch,
+        input_output_aliases=aliases,
         compiler_params=pltpu.CompilerParams(vmem_limit_bytes=56 * MIB),
         cost_estimate=pl.CostEstimate(
-            flops=2 * H * rows * keys * (2 * latent_width + rotary_width),
-            bytes_accessed=16 * MIB,
-            transcendentals=H * rows * keys,
+            flops=2 * H * rows * keys * (2 * latent_width + rotary_width) // count,
+            bytes_accessed=16 * MIB // count,
+            transcendentals=H * rows * keys // count,
         ),
     )(facts, nope, rotated, up, *blocks, *old, *tail)
 
@@ -459,12 +467,14 @@
 
 def finish_kernel(residual_ref, own_ref, *refs):
     *part_refs, out_ref = refs
-    width = part_refs[0].shape[1]
+    halves, wholes = part_refs[:2], part_refs[2:]
+    width = halves[0].shape[1]
     for side in range(2):
         columns = slice(side * width, (side + 1) * width)
         value = residual_ref[:, columns] + own_ref[:, columns]
-        for part_ref in part_refs[side::2]:
-            value = value + part_ref[...].astype(jnp.float32)
+        value = value + halves[side][...].astype(jnp.float32)
+        for part_ref in wholes:
+            value = value + part_ref[:, columns].astype(jnp.float32)
         out_ref[:, columns] = value.astype(out_ref.dtype)
 
 
@@ -507,8 +517,14 @@
     sine = jnp.sin(angles)
     page_size = latent_cache.shape[2]
     top_count = routes.shape[2]
-    own_facts = jnp.concatenate([routes[0].astype(jnp.bfloat16), route_gates[0].astype(jnp.bfloat16)], axis=1).T
-    own_facts = jnp.pad(own_facts, ((0, FACT_ROWS - 2 * top_count), (0, 0)))
+    own_facts = jnp.concatenate(
+        [
+            routes[0].T.astype(jnp.bfloat16),
+            route_gates[0].T.astype(jnp.bfloat16),
+            jnp.zeros((FACT_ROWS - 2 * top_count, row_count), jnp.bfloat16),
+        ],
+        axis=0,
+    )
     own_block, new_entries = pl.pallas_call(
         entries_kernel,
         out_shape=[
@@ -556,22 +572,20 @@
         [length, z_index.astype(jnp.int32), y_index.astype(jnp.int32), jnp.int32(y_count)]
     )
     prepared = (jnp.concatenate([places, page_table[0]]), nope, rotated, kv_up)
-    own_blocks, middle_blocks, last_blocks = (
-        blocks[: 2 * y_count],
-        blocks[2 * y_count : 3 * y_count],
-        blocks[3 * y_count :],
-    )
-    state = attention_call(score_scale, 0, y_count, prepared, own_blocks, (), ())
-    middle_blocks, last_blocks[0] = lax.optimization_barrier((middle_blocks, last_blocks[0]))
-    state = attention_call(score_scale, 2, y_count, prepared, middle_blocks, state, ())
+    early = 2 * y_count
+    first_blocks = blocks[:early]
+    state = attention_call(score_scale, 0, y_count, prepared, first_blocks, (), (), (0, 2))
+    state, blocks[-y_count] = lax.optimization_barrier((state, blocks[-y_count]))
+    state = attention_call(score_scale, 0, y_count, prepared, first_blocks, state, (), (1, 2))
+
     column_facts = [block[entry_width:, page_size:] for block in z_blocks]
     column_facts, state = lax.optimization_barrier((column_facts, state))
     residual, *normed = attention_call(
         score_scale,
-        3,
+        2,
         y_count,
         prepared,
-        last_blocks,
+        blocks[early:],
         state,
         (out_proj, hidden[0], norm_gain[None, :]),
     )
@@ -624,45 +638,48 @@
         rows = rows.reshape(plane_devices, experts_here * group, model_width)
         return exchanged(rows).reshape(expert_places * group, model_width)
 
-    near, *far = zip(*[along_z(half) for half in normed])
-    near, middle = lax.optimization_barrier((near, [layers[0] for layers in far[0]]))
-    far[0] = [(value, layers[1]) for value, layers in zip(middle, far[0])]
+    def added(first, second):
+        value = first.astype(jnp.float32) + second.astype(jnp.float32)
+        return value.astype(jnp.bfloat16)
+
+    def moved(value, pairs):
+        return lax.ppermute(value, "z", pairs)
+
+    near = [moved(half, NEAR) for half in normed]
+    middle = [moved(half, MIDDLE) for half in normed]
+    outward = [moved(half, OUTWARD) for half in middle]
+    sent, near[0] = lax.optimization_barrier((normed, near[0]))
+    far = [
+        [middle, outward],
+        [[moved(half, FROM_END) for half in sent], [moved(half, ACROSS) for half in sent]],
+    ]
     near_rows = all_exchanged(pack(near_matrices[0], [[normed], [near]]))
-    far = [list(zip(*block)) for block in far]
     near_rows, far = lax.optimization_barrier((near_rows, far))
     far_rows = all_exchanged(pack(far_matrices[0], far))
     near_rows = experts(near_rows, expert_in, expert_out, experts_here, group)
+    near_rows, far_rows = lax.optimization_barrier((near_rows, far_rows))
+    near_rows = all_exchanged(near_rows)
     far_rows = experts(far_rows, expert_in, expert_out, experts_here, group)
-
-    def added(first, second):
-        value = first.astype(jnp.float32) + second.astype(jnp.float32)
-        return value.astype(jnp.bfloat16)
-
-    def moved(value, pairs):
-        return lax.ppermute(value, "z", pairs)
+    near_rows, far_rows = lax.optimization_barrier((near_rows, far_rows))
+    far_rows = all_exchanged(far_rows)
 
     half_shape = jax.ShapeDtypeStruct((row_count, model_width // 2), jnp.bfloat16)
     whole_shape = jax.ShapeDtypeStruct((row_count, model_width), jnp.float32)
-    returned = combine(far_matrices[1], all_exchanged(far_rows), [half_shape] * 4)
-    returned, near_rows = lax.optimization_barrier((returned, near_rows))
-    middle_parts, far_parts = returned[:2], returned[2:]
-    far_arrived = [moved(part, INWARD) for part in far_parts]
-    middle_parts, far_arrived[1] = lax.optimization_barrier((middle_parts, far_arrived[1]))
-    far_parts = [moved(added(*pair), MIDDLE) for pair in zip(far_parts, far_arrived)]
-    middle_arrived = [moved(part, INWARD) for part in middle_parts]
     own_part, *near_parts = combine(
-        near_matrices[1], all_exchanged(near_rows), [whole_shape] + [half_shape] * 2
+        near_matrices[1], near_rows, [whole_shape] + [half_shape] * 2
     )
-    own_part, middle_parts, middle_arrived = lax.optimization_barrier(
-        (own_part, middle_parts, middle_arrived)
-    )
-    middle_arrived = [moved(added(*pair), MIDDLE) for pair in zip(middle_parts, middle_arrived)]
-    near_arrived = [moved(added(*pair), NEAR) for pair in zip(near_parts, far_parts)]
+    near_arrived = [moved(part, NEAR) for part in near_parts]
+    near_arrived, far_rows = lax.optimization_barrier((near_arrived, far_rows))
+    part_shape = jax.ShapeDtypeStruct((row_count, model_width), jnp.bfloat16)
+    middle_part, far_part = combine(far_matrices[1], far_rows, [part_shape] * 2)
+    middle_arrived = moved(middle_part, INWARD)
+    far_arrived = [moved(far_part, TO_END), moved(far_part, ACROSS)]
+    middle_arrived = moved(added(middle_part, middle_arrived), MIDDLE)
     layer_out = pl.pallas_call(
         finish_kernel,
         out_shape=jax.ShapeDtypeStruct((row_count, model_width), jnp.bfloat16),
         compiler_params=pltpu.CompilerParams(vmem_limit_bytes=40 * MIB),
-    )(residual, own_part, *near_arrived, *middle_arrived)
+    )(residual, own_part, *near_arrived, middle_arrived, *far_arrived)
     return (layer_out[None], new_entries.T[None])
 
 

time: 254 us -> 261 us (1.028)
  waiting for transfers between devices: 78.6 us -> 99.5 us
  starting transfers between devices: 64.8 us -> 57.9 us
  Pallas kernels: 86.2 us -> 79.9 us
  other arithmetic: 10.3 us -> 6.49 us
  local copies, waits for them, and re-layouts: 8.59 us -> 12.2 us
    ppermute x10 -> x16, waiting for transfers between devices: 26.3 us -> 89.5 us  [moved(): return lax.ppermute(value, 'z', pairs)]
    all_to_all x4, waiting for transfers between devices: 22.5 us -> 6.48 us  [exchanged(): lax.all_to_all(values, PLANE_AXES, split_axis=0, concat_axis=0, tiled=True)]
    ppermute x10 -> x16, starting transfers between devices: 17 us -> 28.2 us  [moved(): return lax.ppermute(value, 'z', pairs)]
    ppermute x3 -> x1, waiting for transfers between devices: 10.4 us -> 0.01 us  [along_z(): outward_far = lax.ppermute(middle_far, 'z', OUTWARD)]
    ppermute x3 -> x1, starting transfers between devices: 8.77 us -> 2.12 us  [along_z(): middle_far = lax.ppermute(near, 'z', MIDDLE)]
    pallas_call x3, Pallas kernels: 36.1 us -> 29.5 us  [attention_call(): pl.pallas_call(functools.partial(kernel, score_scale, first_slot, y_count...]
    ppermute x3 -> x1, waiting for transfers between devices: 8.19 us -> 2.44 us  [along_z(): middle_far = lax.ppermute(near, 'z', MIDDLE)]
    ppermute x3 -> x1, starting transfers between devices: 9.28 us -> 4.6 us  [along_z(): middle = lax.ppermute(values, 'z', MIDDLE)]
  transfers between devices with their start and end apart: 33 -> 29, of which waited for: 21 -> 17; matrix products, arithmetic and copies ran while one was open for 6% -> 4% of each run, Pallas kernels for 17% -> 22%
where the time goes in v2:
time: 261 us; the launch traced here: 260 us
  waiting for transfers between devices  99.5 us (38%)
  Pallas kernels  79.9 us (31%)
  starting transfers between devices  57.9 us (22%)
  local copies, waits for them, and re-layouts  12.2 us (5%)
  other arithmetic  6.49 us (2%)
    ppermute x16, waiting for transfers between devices, moved(): return lax.ppermute(value, 'z', pairs)  89.5 us
    pallas_call x2, Pallas kernels, experts(): pl.pallas_call(functools.partial(experts_kernel, slabs_each, sorting), gr...  42.1 us
    pallas_call x3, Pallas kernels, attention_call(): pl.pallas_call(functools.partial(kernel, score_scale, first_slot, y_count...  29.5 us
    ppermute x16, starting transfers between devices, moved(): return lax.ppermute(value, 'z', pairs)  28.2 us
    all_to_all x4, starting transfers between devices, exchanged(): lax.all_to_all(values, PLANE_AXES, split_axis=0, concat_axis=0, tiled=True)  15.7 us
    unnamed x35, local copies, waits for them, and re-layouts  9.35 us
    all_to_all x4, waiting for transfers between devices, exchanged(): lax.all_to_all(values, PLANE_AXES, split_axis=0, concat_axis=0, tiled=True)  6.48 us
  transfers between devices with their start and end apart: 29, of which 17 were waited for; matrix products, arithmetic and copies ran while one was open for 4% of the time, Pallas kernels for 22%

profile of v2, /device:TPU:8, one launch (start us, length us, event | category | flops | bytes accessed | tf_op | source)
XLA Modules:
  0.0 259.8 jit_solution(8017005172351791603)
XLA Ops:
  4.2 1.9 shard_map.149
  6.1 2.0 collective-permute-start.3
  8.1 4.6 %collective-permute-start = (bf16[592,256]{1,0:T(8,128)(2,1)}, bf16[592,256]{1,0:T(8,128)(2,1)S(1)}, u32[]{:S(2)}, u32[]{:S(2)}) collective-permute-start(bf16[592,256]{1,0:T(8,128)(2,1)} %get-tuple-element.48.refs_4_), channel_id=1, source_target_pairs={{2,4},{4,2},{3,5},{5,3},{10,12},{12,10},{11,13},{13,11},{18,20},{2... | collective-permute-start | bytes 909320 | tf_op jit(solution)/shard_map/ppermute | solution.py:547
  16.6 2.1 collective-permute-start.6
  24.1 2.4 collective-permute-done.6
  30.0 6.9 %shard_map.150 = (f32[8,256,1]{2,1,0:T(8,128)}, f32[8,256,1]{2,1,0:T(8,128)}, f32[8,256,512]{2,1,0:T(8,128)}) custom-call(s32[12]{0:T(128)} %concatenate.26.refs_0_, bf16[128,2048]{1,0:T(8,128)(2,1)} %copy.59.refs_1_, bf16[16,128,64]{2,1,0:T(8,128)(2,1)} %pad_maximum_fusion.refs_2_, bf16[512,4096]{1,0:T(8,128)(2,1)} %refs_3_.7, ...), custom_call_target="tpu_custom_call" | custom-call | flops 2281701376 | bytes 8388608 | tf_op jit(solution)/shard_map/pallas_call | solution.py:276
  38.5 6.9 %shard_map.151 = (f32[8,256,1]{2,1,0:T(8,128)}, f32[8,256,1]{2,1,0:T(8,128)}, f32[8,256,512]{2,1,0:T(8,128)}) custom-call(s32[12]{0:T(128)} %concatenate.26.refs_0_, bf16[128,2048]{1,0:T(8,128)(2,1)} %copy.59.refs_1_, bf16[16,128,64]{2,1,0:T(8,128)(2,1)} %pad_maximum_fusion.refs_2_, ...), custom_call_target="tpu_custom_call", output_to_operand_aliasing={{0}: (8, {}), {1}: (9, {}), {2}: (10, {})} | custom-call | flops 2281701376 | bytes 8388608 | tf_op jit(solution)/shard_map/pallas_call | solution.py:276
  46.5 15.8 %shard_map.152 = (f32[128,2048]{1,0:T(8,128)}, bf16[128,1024]{1,0:T(8,128)(2,1)}, bf16[128,1024]{1,0:T(8,128)(2,1)}) custom-call(s32[12]{0:T(128)} %concatenate.26.refs_0_, bf16[128,2048]{1,0:T(8,128)(2,1)} %copy.59.refs_1_, bf16[16,128,64]{2,1,0:T(8,128)(2,1)} %pad_maximum_fusion.refs_2_, bf16[512,4096]{1,0:T(8,128)(2,1)} %refs_3_.7, ...), custom_call_target="tpu_custom_call" | custom-call | flops 4563402752 | bytes 16777216 | tf_op jit(solution)/shard_map/pallas_call | solution.py:276
  65.1 6.0 %collective-permute-done.9.refs_2_ = bf16[128,1024]{1,0:T(8,128)(2,1)S(1)} collective-permute-done((bf16[128,1024]{1,0:T(8,128)(2,1)}, bf16[128,1024]{1,0:T(8,128)(2,1)S(1)}, u32[]{:S(2)}, u32[]{:S(2)}) %collective-permute-start.9) | collective-permute-done | bytes 262176 | tf_op jit(solution)/shard_map/ppermute | solution.py:646
  71.1 2.8 %collective-permute-done.10.refs_3_ = bf16[128,1024]{1,0:T(8,128)(2,1)S(1)} collective-permute-done((bf16[128,1024]{1,0:T(8,128)(2,1)}, bf16[128,1024]{1,0:T(8,128)(2,1)S(1)}, u32[]{:S(2)}, u32[]{:S(2)}) %collective-permute-start.10) | collective-permute-done | bytes 262176 | tf_op jit(solution)/shard_map/ppermute | solution.py:646
  75.8 4.3 %all-to-all-start = ((bf16[8,56,2048]{2,1,0:T(8,128)(2,1)}), bf16[8,56,2048]{2,1,0:T(8,128)(2,1)}, u32[]{:S(2)}, u32[]{:S(2)}) async-start(bf16[8,56,2048]{2,1,0:T(8,128)(2,1)} %bitcast.19), calls=%async_computation | async-start | bytes 3670016 | tf_op jit(solution)/shard_map/all_to_all | solution.py:635
  80.1 4.0 %collective-permute-start.11 = (bf16[128,1024]{1,0:T(8,128)(2,1)S(1)}, bf16[128,1024]{1,0:T(8,128)(2,1)S(1)}, u32[]{:S(2)}, u32[]{:S(2)}) collective-permute-start(bf16[128,1024]{1,0:T(8,128)(2,1)S(1)} %copy-done.4), channel_id=1, source_target_pairs={{2,4},{4,2},{3,5},{5,3},{10,12},{12,10},{11,13},{13,11},{18,20},{2... | collective-permute-start | bytes 786440 | tf_op jit(solution)/shard_map/ppermute | solution.py:646
  84.2 1.9 collective-permute-start.12
  92.0 27.1 %collective-permute-done.12.refs_1_ = bf16[128,1024]{1,0:T(8,128)(2,1)S(1)} collective-permute-done((bf16[128,1024]{1,0:T(8,128)(2,1)S(1)}, bf16[128,1024]{1,0:T(8,128)(2,1)S(1)}, u32[]{:S(2)}, u32[]{:S(2)}) %collective-permute-start.12) | collective-permute-done | bytes 262176 | tf_op jit(solution)/shard_map/ppermute | solution.py:646
  122.6 4.4 %collective-permute-done.13.refs_2_ = bf16[128,1024]{1,0:T(8,128)(2,1)S(1)} collective-permute-done((bf16[128,1024]{1,0:T(8,128)(2,1)S(1)}, bf16[128,1024]{1,0:T(8,128)(2,1)S(1)}, u32[]{:S(2)}, u32[]{:S(2)}) %collective-permute-start.13) | collective-permute-done | bytes 262176 | tf_op jit(solution)/shard_map/ppermute | solution.py:646
  127.0 4.7 %collective-permute-done.14.refs_3_ = bf16[128,1024]{1,0:T(8,128)(2,1)S(1)} collective-permute-done((bf16[128,1024]{1,0:T(8,128)(2,1)S(1)}, bf16[128,1024]{1,0:T(8,128)(2,1)S(1)}, u32[]{:S(2)}, u32[]{:S(2)}) %collective-permute-start.14) | collective-permute-done | bytes 262176 | tf_op jit(solution)/shard_map/ppermute | solution.py:646
  131.8 1.9 shard_map.155
  133.7 3.7 %all-to-all-start.1 = ((bf16[8,56,2048]{2,1,0:T(8,128)(2,1)}), bf16[8,56,2048]{2,1,0:T(8,128)(2,1)S(1)}, u32[]{:S(2)}, u32[]{:S(2)}) async-start(bf16[8,56,2048]{2,1,0:T(8,128)(2,1)} %bitcast.21), calls=%async_computation.1 | async-start | bytes 3670016 | tf_op jit(solution)/shard_map/all_to_all | solution.py:635
  139.2 21.1 %shard_map.154 = bf16[448,2048]{1,0:T(8,128)(2,1)} custom-call(bf16[448,2048]{1,0:T(8,128)(2,1)} %bitcast.20.x_ref, bf16[2,224,448]{2,1,0:T(8,128)(2,1)} %fusion.8.refs_0_, bf16[2,448,224]{2,1,0:T(8,128)(2,1)} %fusion.9.refs_1_, bf16[4,2048,1408]{2,1,0:T(8,128)(2,1)} %refs_3_.9, bf16[4,2048,1408]{2,1,0:T(8,128)(2,1)} %refs_3_.9, ...), custom_call_target="tpu_custom_call" | custom-call | flops 7751073792 | bytes 34603008 | tf_op jit(solution)/shard_map/pallas_call | solution.py:391
  161.6 4.1 %all-to-all-start.2 = ((bf16[8,56,2048]{2,1,0:T(8,128)(2,1)}), bf16[8,56,2048]{2,1,0:T(8,128)(2,1)S(1)}, u32[]{:S(2)}, u32[]{:S(2)}) async-start(bf16[8,56,2048]{2,1,0:T(8,128)(2,1)} %bitcast.51), calls=%async_computation.2 | async-start | bytes 3670016 | tf_op jit(solution)/shard_map/all_to_all | solution.py:635
  165.7 21.1 %shard_map.156 = bf16[448,2048]{1,0:T(8,128)(2,1)} custom-call(bf16[448,2048]{1,0:T(8,128)(2,1)} %bitcast.50, bf16[2,224,448]{2,1,0:T(8,128)(2,1)} %fusion.8.refs_0_, bf16[2,448,224]{2,1,0:T(8,128)(2,1)} %fusion.9.refs_1_, bf16[4,2048,1408]{2,1,0:T(8,128)(2,1)} %refs_3_.9, bf16[4,2048,1408]{2,1,0:T(8,128)(2,1)} %refs_3_.9, bf16[4,704,2048]{2,1,0:T(8,128)(2,1)} %refs_5_.3, ...), custom_call_target="tpu_custom_call" | custom-call | flops 7751073792 | bytes 34603008 | tf_op jit(solution)/shard_map/pallas_call | solution.py:391
  186.8 1.9 all-to-all-done.2
  190.0 3.6 %all-to-all-start.3 = ((bf16[8,56,2048]{2,1,0:T(8,128)(2,1)}), bf16[8,56,2048]{2,1,0:T(8,128)(2,1)S(1)}, u32[]{:S(2)}, u32[]{:S(2)}) async-start(bf16[8,56,2048]{2,1,0:T(8,128)(2,1)} %bitcast.49), calls=%async_computation.3 | async-start | bytes 3670016 | tf_op jit(solution)/shard_map/all_to_all | solution.py:635
  196.2 2.6 collective-permute-start.19
  199.2 6.7 %collective-permute-done.19.refs_0_ = bf16[128,1024]{1,0:T(8,128)(2,1)S(1)} collective-permute-done((bf16[128,1024]{1,0:T(8,128)(2,1)S(1)}, bf16[128,1024]{1,0:T(8,128)(2,1)S(1)}, u32[]{:S(2)}, u32[]{:S(2)}) %collective-permute-start.19) | collective-permute-done | bytes 262176 | tf_op jit(solution)/shard_map/ppermute | solution.py:646
  205.9 5.3 %collective-permute-done.20.refs_1_ = bf16[128,1024]{1,0:T(8,128)(2,1)S(1)} collective-permute-done((bf16[128,1024]{1,0:T(8,128)(2,1)S(1)}, bf16[128,1024]{1,0:T(8,128)(2,1)S(1)}, u32[]{:S(2)}, u32[]{:S(2)}) %collective-permute-start.20) | collective-permute-done | bytes 262176 | tf_op jit(solution)/shard_map/ppermute | solution.py:646
  212.0 4.5 %all-to-all-done.3 = bf16[8,56,2048]{2,1,0:T(8,128)(2,1)S(1)} async-done(((bf16[8,56,2048]{2,1,0:T(8,128)(2,1)}), bf16[8,56,2048]{2,1,0:T(8,128)(2,1)S(1)}, u32[]{:S(2)}, u32[]{:S(2)}) %all-to-all-start.3) | async-done | bytes 1835040 | tf_op jit(solution)/shard_map/all_to_all | solution.py:635
  218.5 5.5 %collective-permute-start.23 = (bf16[128,2048]{1,0:T(8,128)(2,1)S(1)}, bf16[128,2048]{1,0:T(8,128)(2,1)S(1)}, u32[]{:S(2)}, u32[]{:S(2)}) collective-permute-start(bf16[128,2048]{1,0:T(8,128)(2,1)S(1)} %get-tuple-element.92), channel_id=1, source_target_pairs={{2,6},{4,0},{3,7},{5,1},{10,14},{12,8},{11,15},{13,9},{18,22},{20,... | collective-permute-start | bytes 1572872 | tf_op jit(solution)/shard_map/ppermute | solution.py:646
  224.7 9.2 %collective-permute-done.21 = bf16[128,2048]{1,0:T(8,128)(2,1)S(1)} collective-permute-done((bf16[128,2048]{1,0:T(8,128)(2,1)S(1)}, bf16[128,2048]{1,0:T(8,128)(2,1)S(1)}, u32[]{:S(2)}, u32[]{:S(2)}) %collective-permute-start.21) | collective-permute-done | bytes 524320 | tf_op jit(solution)/shard_map/ppermute | solution.py:646
  234.0 3.3 %collective-permute-start.22 = (bf16[128,2048]{1,0:T(8,128)(2,1)S(1)}, bf16[128,2048]{1,0:T(8,128)(2,1)S(1)}, u32[]{:S(2)}, u32[]{:S(2)}) collective-permute-start(bf16[128,2048]{1,0:T(8,128)(2,1)S(1)} %add_convert_fusion), channel_id=1, source_target_pairs={{2,4},{4,2},{3,5},{5,3},{10,12},{12,10},{11,13},{13,11},{18,20},{2... | collective-permute-start | bytes 1572872 | tf_op jit(solution)/shard_map/ppermute | solution.py:646
  237.3 10.2 %collective-permute-done.23.refs_3_ = bf16[128,2048]{1,0:T(8,128)(2,1)S(1)} collective-permute-done((bf16[128,2048]{1,0:T(8,128)(2,1)S(1)}, bf16[128,2048]{1,0:T(8,128)(2,1)S(1)}, u32[]{:S(2)}, u32[]{:S(2)}) %collective-permute-start.23) | collective-permute-done | bytes 524320 | tf_op jit(solution)/shard_map/ppermute | solution.py:646
  247.5 11.2 %collective-permute-done.22.refs_2_ = bf16[128,2048]{1,0:T(8,128)(2,1)S(1)} collective-permute-done((bf16[128,2048]{1,0:T(8,128)(2,1)S(1)}, bf16[128,2048]{1,0:T(8,128)(2,1)S(1)}, u32[]{:S(2)}, u32[]{:S(2)}) %collective-permute-start.22) | collective-permute-done | bytes 524320 | tf_op jit(solution)/shard_map/ppermute | solution.py:646
  (116 shorter events, 44.2 us)
Async XLA Ops:
  6.1 10.5 %collective-permute-start.4 = (bf16[592,256]{1,0:T(8,128)(2,1)}, bf16[592,256]{1,0:T(8,128)(2,1)S(1)}, u32[]{:S(2)}, u32[]{:S(2)}) collective-permute-start(bf16[592,256]{1,0:T(8,128)(2,1)} %get-tuple-element.48.refs_4_), channel_id=1, source_target_pairs={{0,2},{2,0},{4,6},{6,4},{1,3},{3,1},{5,7},{7,5},{8,10},{10,8},{12,... | collective-permute-start | bytes 909320 | tf_op jit(solution)/shard_map/ppermute | solution.py:546
  6.1 22.4 %collective-permute-start.3 = (bf16[592,256]{1,0:T(8,128)(2,1)}, bf16[592,256]{1,0:T(8,128)(2,1)S(1)}, u32[]{:S(2)}, u32[]{:S(2)}) collective-permute-start(bf16[592,256]{1,0:T(8,128)(2,1)} %get-tuple-element.48.refs_4_), channel_id=1, source_target_pairs={{0,1},{1,0},{2,3},{3,2},{4,5},{5,4},{6,7},{7,6},{8,9},{9,8},{10,11... | collective-permute-start | bytes 909320 | tf_op jit(solution)/shard_map/ppermute | solution.py:38
  8.1 11.6 %collective-permute-start = (bf16[592,256]{1,0:T(8,128)(2,1)}, bf16[592,256]{1,0:T(8,128)(2,1)S(1)}, u32[]{:S(2)}, u32[]{:S(2)}) collective-permute-start(bf16[592,256]{1,0:T(8,128)(2,1)} %get-tuple-element.48.refs_4_), channel_id=1, source_target_pairs={{2,4},{4,2},{3,5},{5,3},{10,12},{12,10},{11,13},{13,11},{18,20},{2... | collective-permute-start | bytes 909320 | tf_op jit(solution)/shard_map/ppermute | solution.py:547
  16.6 12.0 %copy-start.10 = (bf16[592,256]{1,0:T(8,128)(2,1)}, bf16[592,256]{1,0:T(8,128)(2,1)S(1)}, u32[]{:S(2)}) copy-start(bf16[592,256]{1,0:T(8,128)(2,1)S(1)} %collective-permute-done.4.refs_6_) | copy-start | bytes 909316
  16.6 10.0 %collective-permute-start.6 = (bf16[592,256]{1,0:T(8,128)(2,1)S(1)}, bf16[592,256]{1,0:T(8,128)(2,1)S(1)}, u32[]{:S(2)}, u32[]{:S(2)}) collective-permute-start(bf16[592,256]{1,0:T(8,128)(2,1)S(1)} %collective-permute-done.4.refs_6_), channel_id=1, source_target_pairs={{2,4},{4,2},{3,5},{5,3},{10,12},{12,10},{11,13},{13,11},{18,20},{2... | collective-permute-start | bytes 909320 | tf_op jit(solution)/shard_map/ppermute | solution.py:548
  19.7 8.2 %collective-permute-start.1 = (bf16[592,256]{1,0:T(8,128)(2,1)S(1)}, bf16[592,256]{1,0:T(8,128)(2,1)S(1)}, u32[]{:S(2)}, u32[]{:S(2)}) collective-permute-start(bf16[592,256]{1,0:T(8,128)(2,1)S(1)} %collective-permute-done), channel_id=1, source_target_pairs={{2,0},{4,6},{3,1},{5,7},{10,8},{12,14},{11,9},{13,15},{18,16},{20,... | collective-permute-start | bytes 909320 | tf_op jit(solution)/shard_map/ppermute | solution.py:549
  21.1 7.6 %collective-permute-start.5 = (bf16[592,256]{1,0:T(8,128)(2,1)S(1)}, bf16[592,256]{1,0:T(8,128)(2,1)S(1)}, u32[]{:S(2)}, u32[]{:S(2)}) collective-permute-start(bf16[592,256]{1,0:T(8,128)(2,1)S(1)} %collective-permute-done.4.refs_6_), channel_id=1, source_target_pairs={{0,1},{1,0},{2,3},{3,2},{4,5},{5,4},{6,7},{7,6},{8,9},{9,8},{10,11... | collective-permute-start | bytes 909320 | tf_op jit(solution)/shard_map/ppermute | solution.py:38
  26.6 10.3 %collective-permute-start.7 = (bf16[592,256]{1,0:T(8,128)(2,1)S(1)}, bf16[592,256]{1,0:T(8,128)(2,1)S(1)}, u32[]{:S(2)}, u32[]{:S(2)}) collective-permute-start(bf16[592,256]{1,0:T(8,128)(2,1)S(1)} %collective-permute-done.6), channel_id=1, source_target_pairs={{2,0},{4,6},{3,1},{5,7},{10,8},{12,14},{11,9},{13,15},{18,16},{20,... | collective-permute-start | bytes 909320 | tf_op jit(solution)/shard_map/ppermute | solution.py:550
  27.9 17.7 %collective-permute-start.2 = (bf16[592,256]{1,0:T(8,128)(2,1)S(1)}, bf16[592,256]{1,0:T(8,128)(2,1)S(1)}, u32[]{:S(2)}, u32[]{:S(2)}) collective-permute-start(bf16[592,256]{1,0:T(8,128)(2,1)S(1)} %broadcast_select_fusion.1.refs_4_), channel_id=1, source_target_pairs={{0,1},{1,0},{2,3},{3,2},{4,5},{5,4},{6,7},{7,6},{8,9},{9,8},{10,11... | collective-permute-start | bytes 909320 | tf_op jit(solution)/shard_map/ppermute | solution.py:38
  36.9 8.8 %collective-permute-start.8 = (bf16[592,256]{1,0:T(8,128)(2,1)S(1)}, bf16[592,256]{1,0:T(8,128)(2,1)S(1)}, u32[]{:S(2)}, u32[]{:S(2)}) collective-permute-start(bf16[592,256]{1,0:T(8,128)(2,1)S(1)} %broadcast_select_fusion.refs_6_), channel_id=1, source_target_pairs={{0,1},{1,0},{2,3},{3,2},{4,5},{5,4},{6,7},{7,6},{8,9},{9,8},{10,11... | collective-permute-start | bytes 909320 | tf_op jit(solution)/shard_map/ppermute | solution.py:38
  62.3 8.8 %collective-permute-start.9 = (bf16[128,1024]{1,0:T(8,128)(2,1)}, bf16[128,1024]{1,0:T(8,128)(2,1)S(1)}, u32[]{:S(2)}, u32[]{:S(2)}) collective-permute-start(bf16[128,1024]{1,0:T(8,128)(2,1)} %get-tuple-element.68.refs_0_), channel_id=1, source_target_pairs={{0,2},{2,0},{4,6},{6,4},{1,3},{3,1},{5,7},{7,5},{8,10},{10,8},{12,... | collective-permute-start | bytes 786440 | tf_op jit(solution)/shard_map/ppermute | solution.py:646
  63.3 10.6 %collective-permute-start.10 = (bf16[128,1024]{1,0:T(8,128)(2,1)}, bf16[128,1024]{1,0:T(8,128)(2,1)S(1)}, u32[]{:S(2)}, u32[]{:S(2)}) collective-permute-start(bf16[128,1024]{1,0:T(8,128)(2,1)} %get-tuple-element.69.refs_1_), channel_id=1, source_target_pairs={{0,2},{2,0},{4,6},{6,4},{1,3},{3,1},{5,7},{7,5},{8,10},{10,8},{12,... | collective-permute-start | bytes 786440 | tf_op jit(solution)/shard_map/ppermute | solution.py:646
  75.8 56.0 %all-to-all-start = ((bf16[8,56,2048]{2,1,0:T(8,128)(2,1)}), bf16[8,56,2048]{2,1,0:T(8,128)(2,1)}, u32[]{:S(2)}, u32[]{:S(2)}) async-start(bf16[8,56,2048]{2,1,0:T(8,128)(2,1)} %bitcast.19), calls=%async_computation | async-start | bytes 3670016 | tf_op jit(solution)/shard_map/all_to_all | solution.py:635
  80.1 11.2 %collective-permute-start.11 = (bf16[128,1024]{1,0:T(8,128)(2,1)S(1)}, bf16[128,1024]{1,0:T(8,128)(2,1)S(1)}, u32[]{:S(2)}, u32[]{:S(2)}) collective-permute-start(bf16[128,1024]{1,0:T(8,128)(2,1)S(1)} %copy-done.4), channel_id=1, source_target_pairs={{2,4},{4,2},{3,5},{5,3},{10,12},{12,10},{11,13},{13,11},{18,20},{2... | collective-permute-start | bytes 786440 | tf_op jit(solution)/shard_map/ppermute | solution.py:646
  84.2 34.9 %collective-permute-start.12 = (bf16[128,1024]{1,0:T(8,128)(2,1)S(1)}, bf16[128,1024]{1,0:T(8,128)(2,1)S(1)}, u32[]{:S(2)}, u32[]{:S(2)}) collective-permute-start(bf16[128,1024]{1,0:T(8,128)(2,1)S(1)} %copy-done.3), channel_id=1, source_target_pairs={{2,4},{4,2},{3,5},{5,3},{10,12},{12,10},{11,13},{13,11},{18,20},{2... | collective-permute-start | bytes 786440 | tf_op jit(solution)/shard_map/ppermute | solution.py:646
  86.1 34.5 %collective-permute-start.15 = (bf16[128,1024]{1,0:T(8,128)(2,1)S(1)}, bf16[128,1024]{1,0:T(8,128)(2,1)S(1)}, u32[]{:S(2)}, u32[]{:S(2)}) collective-permute-start(bf16[128,1024]{1,0:T(8,128)(2,1)S(1)} %copy-done.4), channel_id=1, source_target_pairs={{6,2},{0,4},{7,3},{1,5},{14,10},{8,12},{15,11},{9,13},{22,18},{16,... | collective-permute-start | bytes 786440 | tf_op jit(solution)/shard_map/ppermute | solution.py:646
  87.5 35.0 %collective-permute-start.17 = (bf16[128,1024]{1,0:T(8,128)(2,1)S(1)}, bf16[128,1024]{1,0:T(8,128)(2,1)S(1)}, u32[]{:S(2)}, u32[]{:S(2)}) collective-permute-start(bf16[128,1024]{1,0:T(8,128)(2,1)S(1)} %copy-done.4), channel_id=1, source_target_pairs={{0,6},{6,0},{1,7},{7,1},{8,14},{14,8},{9,15},{15,9},{16,22},{22,16... | collective-permute-start | bytes 786440 | tf_op jit(solution)/shard_map/ppermute | solution.py:646
  88.2 34.3 %collective-permute-start.16 = (bf16[128,1024]{1,0:T(8,128)(2,1)S(1)}, bf16[128,1024]{1,0:T(8,128)(2,1)S(1)}, u32[]{:S(2)}, u32[]{:S(2)}) collective-permute-start(bf16[128,1024]{1,0:T(8,128)(2,1)S(1)} %copy-done.3), channel_id=1, source_target_pairs={{6,2},{0,4},{7,3},{1,5},{14,10},{8,12},{15,11},{9,13},{22,18},{16,... | collective-permute-start | bytes 786440 | tf_op jit(solution)/shard_map/ppermute | solution.py:646
  91.3 31.3 %collective-permute-start.18 = (bf16[128,1024]{1,0:T(8,128)(2,1)S(1)}, bf16[128,1024]{1,0:T(8,128)(2,1)S(1)}, u32[]{:S(2)}, u32[]{:S(2)}) collective-permute-start(bf16[128,1024]{1,0:T(8,128)(2,1)S(1)} %copy-done.3), channel_id=1, source_target_pairs={{0,6},{6,0},{1,7},{7,1},{8,14},{14,8},{9,15},{15,9},{16,22},{22,16... | collective-permute-start | bytes 786440 | tf_op jit(solution)/shard_map/ppermute | solution.py:646
  119.1 7.9 %collective-permute-start.13 = (bf16[128,1024]{1,0:T(8,128)(2,1)S(1)}, bf16[128,1024]{1,0:T(8,128)(2,1)S(1)}, u32[]{:S(2)}, u32[]{:S(2)}) collective-permute-start(bf16[128,1024]{1,0:T(8,128)(2,1)S(1)} %collective-permute-done.11.refs_0_), channel_id=1, source_target_pairs={{2,0},{4,6},{3,1},{5,7},{10,8},{12,14},{11,9},{13,15},{18,16},{20,... | collective-permute-start | bytes 786440 | tf_op jit(solution)/shard_map/ppermute | solution.py:646
  120.6 11.2 %collective-permute-start.14 = (bf16[128,1024]{1,0:T(8,128)(2,1)S(1)}, bf16[128,1024]{1,0:T(8,128)(2,1)S(1)}, u32[]{:S(2)}, u32[]{:S(2)}) collective-permute-start(bf16[128,1024]{1,0:T(8,128)(2,1)S(1)} %collective-permute-done.12.refs_1_), channel_id=1, source_target_pairs={{2,0},{4,6},{3,1},{5,7},{10,8},{12,14},{11,9},{13,15},{18,16},{20,... | collective-permute-start | bytes 786440 | tf_op jit(solution)/shard_map/ppermute | solution.py:646
  133.7 26.7 %all-to-all-start.1 = ((bf16[8,56,2048]{2,1,0:T(8,128)(2,1)}), bf16[8,56,2048]{2,1,0:T(8,128)(2,1)S(1)}, u32[]{:S(2)}, u32[]{:S(2)}) async-start(bf16[8,56,2048]{2,1,0:T(8,128)(2,1)} %bitcast.21), calls=%async_computation.1 | async-start | bytes 3670016 | tf_op jit(solution)/shard_map/all_to_all | solution.py:635
  161.6 27.1 %all-to-all-start.2 = ((bf16[8,56,2048]{2,1,0:T(8,128)(2,1)}), bf16[8,56,2048]{2,1,0:T(8,128)(2,1)S(1)}, u32[]{:S(2)}, u32[]{:S(2)}) async-start(bf16[8,56,2048]{2,1,0:T(8,128)(2,1)} %bitcast.51), calls=%async_computation.2 | async-start | bytes 3670016 | tf_op jit(solution)/shard_map/all_to_all | solution.py:635
  190.0 26.5 %all-to-all-start.3 = ((bf16[8,56,2048]{2,1,0:T(8,128)(2,1)}), bf16[8,56,2048]{2,1,0:T(8,128)(2,1)S(1)}, u32[]{:S(2)}, u32[]{:S(2)}) async-start(bf16[8,56,2048]{2,1,0:T(8,128)(2,1)} %bitcast.49), calls=%async_computation.3 | async-start | bytes 3670016 | tf_op jit(solution)/shard_map/all_to_all | solution.py:635
  196.2 9.7 %collective-permute-start.19 = (bf16[128,1024]{1,0:T(8,128)(2,1)S(1)}, bf16[128,1024]{1,0:T(8,128)(2,1)S(1)}, u32[]{:S(2)}, u32[]{:S(2)}) collective-permute-start(bf16[128,1024]{1,0:T(8,128)(2,1)S(1)} %get-tuple-element.85), channel_id=1, source_target_pairs={{0,2},{2,0},{4,6},{6,4},{1,3},{3,1},{5,7},{7,5},{8,10},{10,8},{12,... | collective-permute-start | bytes 786440 | tf_op jit(solution)/shard_map/ppermute | solution.py:646
  198.8 12.5 %collective-permute-start.20 = (bf16[128,1024]{1,0:T(8,128)(2,1)S(1)}, bf16[128,1024]{1,0:T(8,128)(2,1)S(1)}, u32[]{:S(2)}, u32[]{:S(2)}) collective-permute-start(bf16[128,1024]{1,0:T(8,128)(2,1)S(1)} %get-tuple-element.86), channel_id=1, source_target_pairs={{0,2},{2,0},{4,6},{6,4},{1,3},{3,1},{5,7},{7,5},{8,10},{10,8},{12,... | collective-permute-start | bytes 786440 | tf_op jit(solution)/shard_map/ppermute | solution.py:646
  216.5 42.2 %copy-start.2 = (f32[128,2048]{1,0:T(8,128)S(1)}, f32[128,2048]{1,0:T(8,128)}, u32[]{:S(2)}) copy-start(f32[128,2048]{1,0:T(8,128)} %get-tuple-element.62.residual_ref) | copy-start | bytes 3145732
  216.5 42.2 %copy-start.6 = (bf16[128,1024]{1,0:T(8,128)(2,1)S(1)}, bf16[128,1024]{1,0:T(8,128)(2,1)}, u32[]{:S(2)}) copy-start(bf16[128,1024]{1,0:T(8,128)(2,1)} %copy-done.5) | copy-start | bytes 786436
  217.2 16.7 %collective-permute-start.21 = (bf16[128,2048]{1,0:T(8,128)(2,1)S(1)}, bf16[128,2048]{1,0:T(8,128)(2,1)S(1)}, u32[]{:S(2)}, u32[]{:S(2)}) collective-permute-start(bf16[128,2048]{1,0:T(8,128)(2,1)S(1)} %get-tuple-element.91), channel_id=1, source_target_pairs={{0,2},{6,4},{1,3},{7,5},{8,10},{14,12},{9,11},{15,13},{16,18},{22,... | collective-permute-start | bytes 1572872 | tf_op jit(solution)/shard_map/ppermute | solution.py:646
  218.5 29.0 %collective-permute-start.23 = (bf16[128,2048]{1,0:T(8,128)(2,1)S(1)}, bf16[128,2048]{1,0:T(8,128)(2,1)S(1)}, u32[]{:S(2)}, u32[]{:S(2)}) collective-permute-start(bf16[128,2048]{1,0:T(8,128)(2,1)S(1)} %get-tuple-element.92), channel_id=1, source_target_pairs={{2,6},{4,0},{3,7},{5,1},{10,14},{12,8},{11,15},{13,9},{18,22},{20,... | collective-permute-start | bytes 1572872 | tf_op jit(solution)/shard_map/ppermute | solution.py:646
  224.0 23.5 %collective-permute-start.24 = (bf16[128,2048]{1,0:T(8,128)(2,1)S(1)}, bf16[128,2048]{1,0:T(8,128)(2,1)S(1)}, u32[]{:S(2)}, u32[]{:S(2)}) collective-permute-start(bf16[128,2048]{1,0:T(8,128)(2,1)S(1)} %get-tuple-element.92), channel_id=1, source_target_pairs={{0,6},{6,0},{1,7},{7,1},{8,14},{14,8},{9,15},{15,9},{16,22},{22,16... | collective-permute-start | bytes 1572872 | tf_op jit(solution)/shard_map/ppermute | solution.py:646
  234.0 24.7 %collective-permute-start.22 = (bf16[128,2048]{1,0:T(8,128)(2,1)S(1)}, bf16[128,2048]{1,0:T(8,128)(2,1)S(1)}, u32[]{:S(2)}, u32[]{:S(2)}) collective-permute-start(bf16[128,2048]{1,0:T(8,128)(2,1)S(1)} %add_convert_fusion), channel_id=1, source_target_pairs={{2,4},{4,2},{3,5},{5,3},{10,12},{12,10},{11,13},{13,11},{18,20},{2... | collective-permute-start | bytes 1572872 | tf_op jit(solution)/shard_map/ppermute | solution.py:646
  (13 other events, 56.4 us)

commit v3 on v2

--- a/solution.py
+++ b/solution.py
@@ -27,9 +27,6 @@
 NEAR = [(0, 1), (1, 0), (2, 3), (3, 2)]
 MIDDLE = [(1, 2), (2, 1)]
 OUTWARD = [(1, 0), (2, 3)]
-ACROSS = [(0, 3), (3, 0)]
-FROM_END = [(3, 1), (0, 2)]
-TO_END = [(1, 3), (2, 0)]
 INWARD = [(0, 1), (3, 2)]
 
 
@@ -467,14 +464,12 @@
 
 def finish_kernel(residual_ref, own_ref, *refs):
     *part_refs, out_ref = refs
-    halves, wholes = part_refs[:2], part_refs[2:]
-    width = halves[0].shape[1]
+    width = part_refs[0].shape[1]
     for side in range(2):
         columns = slice(side * width, (side + 1) * width)
         value = residual_ref[:, columns] + own_ref[:, columns]
-        value = value + halves[side][...].astype(jnp.float32)
-        for part_ref in wholes:
-            value = value + part_ref[:, columns].astype(jnp.float32)
+        for part_ref in part_refs[side::2]:
+            value = value + part_ref[...].astype(jnp.float32)
         out_ref[:, columns] = value.astype(out_ref.dtype)
 
 
@@ -638,22 +633,16 @@
         rows = rows.reshape(plane_devices, experts_here * group, model_width)
         return exchanged(rows).reshape(expert_places * group, model_width)
 
-    def added(first, second):
-        value = first.astype(jnp.float32) + second.astype(jnp.float32)
-        return value.astype(jnp.bfloat16)
-
-    def moved(value, pairs):
-        return lax.ppermute(value, "z", pairs)
-
-    near = [moved(half, NEAR) for half in normed]
-    middle = [moved(half, MIDDLE) for half in normed]
-    outward = [moved(half, OUTWARD) for half in middle]
-    sent, near[0] = lax.optimization_barrier((normed, near[0]))
-    far = [
-        [middle, outward],
-        [[moved(half, FROM_END) for half in sent], [moved(half, ACROSS) for half in sent]],
-    ]
+    near, *far = zip(*[along_z(half) for half in normed])
+    (middle, outward), (other_middle, other_outward) = far[0]
+    middle_far = far[1][0][0]
+    near, middle, other_middle, outward, middle_far = lax.optimization_barrier(
+        (near, middle, other_middle, outward, middle_far)
+    )
+    far[1] = [(middle_far, far[1][0][1]), far[1][1]]
+    far[0] = [(middle, outward), (other_middle, other_outward)]
     near_rows = all_exchanged(pack(near_matrices[0], [[normed], [near]]))
+    far = [list(zip(*block)) for block in far]
     near_rows, far = lax.optimization_barrier((near_rows, far))
     far_rows = all_exchanged(pack(far_matrices[0], far))
     near_rows = experts(near_rows, expert_in, expert_out, experts_here, group)
@@ -663,6 +652,13 @@
     near_rows, far_rows = lax.optimization_barrier((near_rows, far_rows))
     far_rows = all_exchanged(far_rows)
 
+    def added(first, second):
+        value = first.astype(jnp.float32) + second.astype(jnp.float32)
+        return value.astype(jnp.bfloat16)
+
+    def moved(value, pairs):
+        return lax.ppermute(value, "z", pairs)
+
     half_shape = jax.ShapeDtypeStruct((row_count, model_width // 2), jnp.bfloat16)
     whole_shape = jax.ShapeDtypeStruct((row_count, model_width), jnp.float32)
     own_part, *near_parts = combine(
@@ -670,16 +666,19 @@
     )
     near_arrived = [moved(part, NEAR) for part in near_parts]
     near_arrived, far_rows = lax.optimization_barrier((near_arrived, far_rows))
-    part_shape = jax.ShapeDtypeStruct((row_count, model_width), jnp.bfloat16)
-    middle_part, far_part = combine(far_matrices[1], far_rows, [part_shape] * 2)
-    middle_arrived = moved(middle_part, INWARD)
-    far_arrived = [moved(far_part, TO_END), moved(far_part, ACROSS)]
-    middle_arrived = moved(added(middle_part, middle_arrived), MIDDLE)
+    returned = combine(far_matrices[1], far_rows, [half_shape] * 4)
+    middle_parts, far_parts = returned[:2], returned[2:]
+    far_arrived = [moved(part, INWARD) for part in far_parts]
+    middle_parts, far_arrived[1] = lax.optimization_barrier((middle_parts, far_arrived[1]))
+    middle_arrived = [moved(part, INWARD) for part in middle_parts]
+    far_arrived = [moved(added(*pair), MIDDLE) for pair in zip(far_parts, far_arrived)]
+    middle_arrived = [moved(added(*pair), MIDDLE) for pair in zip(middle_parts, middle_arrived)]
+    far_arrived = [moved(part, OUTWARD) for part in far_arrived]
     layer_out = pl.pallas_call(
         finish_kernel,
         out_shape=jax.ShapeDtypeStruct((row_count, model_width), jnp.bfloat16),
         compiler_params=pltpu.CompilerParams(vmem_limit_bytes=40 * MIB),
-    )(residual, own_part, *near_arrived, middle_arrived, *far_arrived)
+    )(residual, own_part, *near_arrived, *middle_arrived, *far_arrived)
     return (layer_out[None], new_entries.T[None])
 
 

time: 261 us -> 239 us (0.916)
  waiting for transfers between devices: 99.5 us -> 65.2 us
  starting transfers between devices: 57.9 us -> 68.6 us
    ppermute x16 -> x12, waiting for transfers between devices: 89.5 us -> 30.6 us  [moved(): return lax.ppermute(value, 'z', pairs)]
    ppermute x1 -> x3, waiting for transfers between devices: 0.01 us -> 8.82 us  [along_z(): outward_far = lax.ppermute(middle_far, 'z', OUTWARD)]
    ppermute x16 -> x12, starting transfers between devices: 28.2 us -> 20.7 us  [moved(): return lax.ppermute(value, 'z', pairs)]
    ppermute x1 -> x3, waiting for transfers between devices: 2.44 us -> 9.66 us  [along_z(): middle_far = lax.ppermute(near, 'z', MIDDLE)]
    ppermute x1 -> x3, starting transfers between devices: 4.6 us -> 10.6 us  [along_z(): middle = lax.ppermute(values, 'z', MIDDLE)]
    ppermute x1 -> x3, starting transfers between devices: 2.12 us -> 7.18 us  [along_z(): middle_far = lax.ppermute(near, 'z', MIDDLE)]
  transfers between devices with their start and end apart: 29 -> 35, of which waited for: 17 -> 24; matrix products, arithmetic and copies ran while one was open for 4% -> 5% of each run, Pallas kernels for 22% -> 24%
where the time goes in v3:
time: 239 us; the launch traced here: 236 us
  Pallas kernels  79.9 us (33%)
  starting transfers between devices  68.6 us (29%)
  waiting for transfers between devices  65.2 us (27%)
  local copies, waits for them, and re-layouts  12.1 us (5%)
  other arithmetic  6.59 us (3%)
    pallas_call x2, Pallas kernels, experts(): pl.pallas_call(functools.partial(experts_kernel, slabs_each, sorting), gr...  42.1 us
    ppermute x12, waiting for transfers between devices, moved(): return lax.ppermute(value, 'z', pairs)  30.6 us
    pallas_call x3, Pallas kernels, attention_call(): pl.pallas_call(functools.partial(kernel, score_scale, first_slot, y_count...  29.6 us
    ppermute x12, starting transfers between devices, moved(): return lax.ppermute(value, 'z', pairs)  20.7 us
    all_to_all x4, starting transfers between devices, exchanged(): lax.all_to_all(values, PLANE_AXES, split_axis=0, concat_axis=0, tiled=True)  15.6 us
    ppermute x3, starting transfers between devices, along_z(): middle = lax.ppermute(values, 'z', MIDDLE)  10.6 us
    ppermute x3, waiting for transfers between devices, along_z(): middle_far = lax.ppermute(near, 'z', MIDDLE)  9.66 us
    unnamed x35, local copies, waits for them, and re-layouts  9.36 us
  transfers between devices with their start and end apart: 35, of which 24 were waited for; matrix products, arithmetic and copies ran while one was open for 5% of the time, Pallas kernels for 24%

profile of v3, /device:TPU:8, one launch (start us, length us, event | category | flops | bytes accessed | tf_op | source)
XLA Modules:
  0.0 236.4 jit_solution(17005784971274469140)
XLA Ops:
  6.1 2.0 collective-permute-start.3
  8.1 4.6 %collective-permute-start = (bf16[592,256]{1,0:T(8,128)(2,1)}, bf16[592,256]{1,0:T(8,128)(2,1)S(1)}, u32[]{:S(2)}, u32[]{:S(2)}) collective-permute-start(bf16[592,256]{1,0:T(8,128)(2,1)} %get-tuple-element.56.refs_4_), channel_id=1, source_target_pairs={{2,4},{4,2},{3,5},{5,3},{10,12},{12,10},{11,13},{13,11},{18,20},{2... | collective-permute-start | bytes 909320 | tf_op jit(solution)/shard_map/ppermute | solution.py:542
  16.6 2.1 collective-permute-start.6
  24.1 2.4 %collective-permute-done.6 = bf16[592,256]{1,0:T(8,128)(2,1)S(1)} collective-permute-done((bf16[592,256]{1,0:T(8,128)(2,1)S(1)}, bf16[592,256]{1,0:T(8,128)(2,1)S(1)}, u32[]{:S(2)}, u32[]{:S(2)}) %collective-permute-start.6) | collective-permute-done | bytes 303136 | tf_op jit(solution)/shard_map/ppermute | solution.py:543
  29.9 6.9 %shard_map.150 = (f32[8,256,1]{2,1,0:T(8,128)}, f32[8,256,1]{2,1,0:T(8,128)}, f32[8,256,512]{2,1,0:T(8,128)}) custom-call(s32[12]{0:T(128)} %concatenate.26.refs_0_, bf16[128,2048]{1,0:T(8,128)(2,1)} %copy.59.refs_1_, bf16[16,128,64]{2,1,0:T(8,128)(2,1)} %pad_maximum_fusion.refs_2_, bf16[512,4096]{1,0:T(8,128)(2,1)} %refs_3_.7, ...), custom_call_target="tpu_custom_call" | custom-call | flops 2281701376 | bytes 8388608 | tf_op jit(solution)/shard_map/pallas_call | solution.py:273
  38.5 6.9 %shard_map.151 = (f32[8,256,1]{2,1,0:T(8,128)}, f32[8,256,1]{2,1,0:T(8,128)}, f32[8,256,512]{2,1,0:T(8,128)}) custom-call(s32[12]{0:T(128)} %concatenate.26.refs_0_, bf16[128,2048]{1,0:T(8,128)(2,1)} %copy.59.refs_1_, bf16[16,128,64]{2,1,0:T(8,128)(2,1)} %pad_maximum_fusion.refs_2_, ...), custom_call_target="tpu_custom_call", output_to_operand_aliasing={{0}: (8, {}), {1}: (9, {}), {2}: (10, {})} | custom-call | flops 2281701376 | bytes 8388608 | tf_op jit(solution)/shard_map/pallas_call | solution.py:273
  46.2 15.8 %shard_map.152 = (f32[128,2048]{1,0:T(8,128)}, bf16[128,1024]{1,0:T(8,128)(2,1)}, bf16[128,1024]{1,0:T(8,128)(2,1)}) custom-call(s32[12]{0:T(128)} %concatenate.26.refs_0_, bf16[128,2048]{1,0:T(8,128)(2,1)} %copy.59.refs_1_, bf16[16,128,64]{2,1,0:T(8,128)(2,1)} %pad_maximum_fusion.refs_2_, bf16[512,4096]{1,0:T(8,128)(2,1)} %refs_3_.7, ...), custom_call_target="tpu_custom_call" | custom-call | flops 4563402752 | bytes 16777216 | tf_op jit(solution)/shard_map/pallas_call | solution.py:273
  62.1 3.2 %collective-permute-start.11 = (bf16[128,1024]{1,0:T(8,128)(2,1)}, bf16[128,1024]{1,0:T(8,128)(2,1)S(1)}, u32[]{:S(2)}, u32[]{:S(2)}) collective-permute-start(bf16[128,1024]{1,0:T(8,128)(2,1)} %get-tuple-element.73.refs_0_), channel_id=1, source_target_pairs={{2,4},{4,2},{3,5},{5,3},{10,12},{12,10},{11,13},{13,11},{18,20},{2... | collective-permute-start | bytes 786440 | tf_op jit(solution)/shard_map/ppermute | solution.py:542
  65.6 2.0 collective-permute-start.10
  67.7 2.7 %collective-permute-start.12 = (bf16[128,1024]{1,0:T(8,128)(2,1)}, bf16[128,1024]{1,0:T(8,128)(2,1)S(1)}, u32[]{:S(2)}, u32[]{:S(2)}) collective-permute-start(bf16[128,1024]{1,0:T(8,128)(2,1)} %get-tuple-element.74.refs_1_), channel_id=1, source_target_pairs={{2,4},{4,2},{3,5},{5,3},{10,12},{12,10},{11,13},{13,11},{18,20},{2... | collective-permute-start | bytes 786440 | tf_op jit(solution)/shard_map/ppermute | solution.py:542
  74.8 2.5 %collective-permute-start.14 = (bf16[128,1024]{1,0:T(8,128)(2,1)S(1)}, bf16[128,1024]{1,0:T(8,128)(2,1)S(1)}, u32[]{:S(2)}, u32[]{:S(2)}) collective-permute-start(bf16[128,1024]{1,0:T(8,128)(2,1)S(1)} %collective-permute-done.9.refs_2_), channel_id=1, source_target_pairs={{2,4},{4,2},{3,5},{5,3},{10,12},{12,10},{11,13},{13,11},{18,20},{2... | collective-permute-start | bytes 786440 | tf_op jit(solution)/shard_map/ppermute | solution.py:543
  78.8 2.3 collective-permute-done.13.refs_2_
  81.1 2.0 collective-permute-done.14.refs_4_
  85.0 4.3 %all-to-all-start = ((bf16[8,56,2048]{2,1,0:T(8,128)(2,1)}), bf16[8,56,2048]{2,1,0:T(8,128)(2,1)}, u32[]{:S(2)}, u32[]{:S(2)}) async-start(bf16[8,56,2048]{2,1,0:T(8,128)(2,1)} %bitcast.19), calls=%async_computation | async-start | bytes 3670016 | tf_op jit(solution)/shard_map/all_to_all | solution.py:630
  89.3 2.5 %collective-permute-start.16 = (bf16[128,1024]{1,0:T(8,128)(2,1)S(1)}, bf16[128,1024]{1,0:T(8,128)(2,1)S(1)}, u32[]{:S(2)}, u32[]{:S(2)}) collective-permute-start(bf16[128,1024]{1,0:T(8,128)(2,1)S(1)} %collective-permute-done.10.refs_3_), channel_id=1, source_target_pairs={{2,4},{4,2},{3,5},{5,3},{10,12},{12,10},{11,13},{13,11},{18,20},{2... | collective-permute-start | bytes 786440 | tf_op jit(solution)/shard_map/ppermute | solution.py:543
  94.6 5.2 %collective-permute-done.16.refs_5_ = bf16[128,1024]{1,0:T(8,128)(2,1)S(1)} collective-permute-done((bf16[128,1024]{1,0:T(8,128)(2,1)S(1)}, bf16[128,1024]{1,0:T(8,128)(2,1)S(1)}, u32[]{:S(2)}, u32[]{:S(2)}) %collective-permute-start.16) | collective-permute-done | bytes 262176 | tf_op jit(solution)/shard_map/ppermute | solution.py:543
  101.8 3.8 %collective-permute-done.17.refs_6_ = bf16[128,1024]{1,0:T(8,128)(2,1)S(1)} collective-permute-done((bf16[128,1024]{1,0:T(8,128)(2,1)S(1)}, bf16[128,1024]{1,0:T(8,128)(2,1)S(1)}, u32[]{:S(2)}, u32[]{:S(2)}) %collective-permute-start.17) | collective-permute-done | bytes 262176 | tf_op jit(solution)/shard_map/ppermute | solution.py:545
  105.6 5.1 %collective-permute-done.18.refs_7_ = bf16[128,1024]{1,0:T(8,128)(2,1)S(1)} collective-permute-done((bf16[128,1024]{1,0:T(8,128)(2,1)S(1)}, bf16[128,1024]{1,0:T(8,128)(2,1)S(1)}, u32[]{:S(2)}, u32[]{:S(2)}) %collective-permute-start.18) | collective-permute-done | bytes 262176 | tf_op jit(solution)/shard_map/ppermute | solution.py:545
  114.2 3.6 %all-to-all-start.1 = ((bf16[8,56,2048]{2,1,0:T(8,128)(2,1)}), bf16[8,56,2048]{2,1,0:T(8,128)(2,1)S(1)}, u32[]{:S(2)}, u32[]{:S(2)}) async-start(bf16[8,56,2048]{2,1,0:T(8,128)(2,1)} %bitcast.21), calls=%async_computation.1 | async-start | bytes 3670016 | tf_op jit(solution)/shard_map/all_to_all | solution.py:630
  119.7 21.1 %shard_map.154 = bf16[448,2048]{1,0:T(8,128)(2,1)} custom-call(bf16[448,2048]{1,0:T(8,128)(2,1)} %bitcast.20.x_ref, bf16[2,224,448]{2,1,0:T(8,128)(2,1)} %fusion.8.refs_0_, bf16[2,448,224]{2,1,0:T(8,128)(2,1)} %fusion.9.refs_1_, bf16[4,2048,1408]{2,1,0:T(8,128)(2,1)} %refs_3_.9, bf16[4,2048,1408]{2,1,0:T(8,128)(2,1)} %refs_3_.9, ...), custom_call_target="tpu_custom_call" | custom-call | flops 7751073792 | bytes 34603008 | tf_op jit(solution)/shard_map/pallas_call | solution.py:388
  142.0 4.1 %all-to-all-start.2 = ((bf16[8,56,2048]{2,1,0:T(8,128)(2,1)}), bf16[8,56,2048]{2,1,0:T(8,128)(2,1)S(1)}, u32[]{:S(2)}, u32[]{:S(2)}) async-start(bf16[8,56,2048]{2,1,0:T(8,128)(2,1)} %bitcast.51), calls=%async_computation.2 | async-start | bytes 3670016 | tf_op jit(solution)/shard_map/all_to_all | solution.py:630
  146.1 21.1 %shard_map.156 = bf16[448,2048]{1,0:T(8,128)(2,1)} custom-call(bf16[448,2048]{1,0:T(8,128)(2,1)} %bitcast.50, bf16[2,224,448]{2,1,0:T(8,128)(2,1)} %fusion.8.refs_0_, bf16[2,448,224]{2,1,0:T(8,128)(2,1)} %fusion.9.refs_1_, bf16[4,2048,1408]{2,1,0:T(8,128)(2,1)} %refs_3_.9, bf16[4,2048,1408]{2,1,0:T(8,128)(2,1)} %refs_3_.9, bf16[4,704,2048]{2,1,0:T(8,128)(2,1)} %refs_5_.3, ...), custom_call_target="tpu_custom_call" | custom-call | flops 7751073792 | bytes 34603008 | tf_op jit(solution)/shard_map/pallas_call | solution.py:388
  170.4 3.6 %all-to-all-start.3 = ((bf16[8,56,2048]{2,1,0:T(8,128)(2,1)}), bf16[8,56,2048]{2,1,0:T(8,128)(2,1)S(1)}, u32[]{:S(2)}, u32[]{:S(2)}) async-start(bf16[8,56,2048]{2,1,0:T(8,128)(2,1)} %bitcast.49), calls=%async_computation.3 | async-start | bytes 3670016 | tf_op jit(solution)/shard_map/all_to_all | solution.py:630
  179.0 6.8 %collective-permute-done.19.refs_0_ = bf16[128,1024]{1,0:T(8,128)(2,1)S(1)} collective-permute-done((bf16[128,1024]{1,0:T(8,128)(2,1)S(1)}, bf16[128,1024]{1,0:T(8,128)(2,1)S(1)}, u32[]{:S(2)}, u32[]{:S(2)}) %collective-permute-start.19) | collective-permute-done | bytes 262176 | tf_op jit(solution)/shard_map/ppermute | solution.py:660
  185.8 5.1 %collective-permute-done.20.refs_1_ = bf16[128,1024]{1,0:T(8,128)(2,1)S(1)} collective-permute-done((bf16[128,1024]{1,0:T(8,128)(2,1)S(1)}, bf16[128,1024]{1,0:T(8,128)(2,1)S(1)}, u32[]{:S(2)}, u32[]{:S(2)}) %collective-permute-start.20) | collective-permute-done | bytes 262176 | tf_op jit(solution)/shard_map/ppermute | solution.py:660
  191.6 5.2 %all-to-all-done.3 = bf16[8,56,2048]{2,1,0:T(8,128)(2,1)S(1)} async-done(((bf16[8,56,2048]{2,1,0:T(8,128)(2,1)}), bf16[8,56,2048]{2,1,0:T(8,128)(2,1)S(1)}, u32[]{:S(2)}, u32[]{:S(2)}) %all-to-all-start.3) | async-done | bytes 1835040 | tf_op jit(solution)/shard_map/all_to_all | solution.py:630
  200.3 8.5 %collective-permute-done.21 = bf16[128,1024]{1,0:T(8,128)(2,1)S(1)} collective-permute-done((bf16[128,1024]{1,0:T(8,128)(2,1)S(1)}, bf16[128,1024]{1,0:T(8,128)(2,1)S(1)}, u32[]{:S(2)}, u32[]{:S(2)}) %collective-permute-start.21) | collective-permute-done | bytes 262176 | tf_op jit(solution)/shard_map/ppermute | solution.py:660
  210.2 2.5 %collective-permute-start.29 = (bf16[128,1024]{1,0:T(8,128)(2,1)S(1)}, bf16[128,1024]{1,0:T(8,128)(2,1)S(1)}, u32[]{:S(2)}, u32[]{:S(2)}) collective-permute-start(bf16[128,1024]{1,0:T(8,128)(2,1)S(1)} %add_convert_fusion.1), channel_id=1, source_target_pairs={{2,4},{4,2},{3,5},{5,3},{10,12},{12,10},{11,13},{13,11},{18,20},{2... | collective-permute-start | bytes 786440 | tf_op jit(solution)/shard_map/ppermute | solution.py:660
  214.5 2.5 %collective-permute-start.27 = (bf16[128,1024]{1,0:T(8,128)(2,1)S(1)}, bf16[128,1024]{1,0:T(8,128)(2,1)S(1)}, u32[]{:S(2)}, u32[]{:S(2)}) collective-permute-start(bf16[128,1024]{1,0:T(8,128)(2,1)S(1)} %add_convert_fusion.2), channel_id=1, source_target_pairs={{2,4},{4,2},{3,5},{5,3},{10,12},{12,10},{11,13},{13,11},{18,20},{2... | collective-permute-start | bytes 786440 | tf_op jit(solution)/shard_map/ppermute | solution.py:660
  219.1 2.6 %collective-permute-start.25 = (bf16[128,1024]{1,0:T(8,128)(2,1)S(1)}, bf16[128,1024]{1,0:T(8,128)(2,1)S(1)}, u32[]{:S(2)}, u32[]{:S(2)}) collective-permute-start(bf16[128,1024]{1,0:T(8,128)(2,1)S(1)} %add_convert_fusion.3), channel_id=1, source_target_pairs={{2,4},{4,2},{3,5},{5,3},{10,12},{12,10},{11,13},{13,11},{18,20},{2... | collective-permute-start | bytes 786440 | tf_op jit(solution)/shard_map/ppermute | solution.py:660
  226.7 2.5 %collective-permute-start.23 = (bf16[128,1024]{1,0:T(8,128)(2,1)S(1)}, bf16[128,1024]{1,0:T(8,128)(2,1)S(1)}, u32[]{:S(2)}, u32[]{:S(2)}) collective-permute-start(bf16[128,1024]{1,0:T(8,128)(2,1)S(1)} %add_convert_fusion.4), channel_id=1, source_target_pairs={{2,4},{4,2},{3,5},{5,3},{10,12},{12,10},{11,13},{13,11},{18,20},{2... | collective-permute-start | bytes 786440 | tf_op jit(solution)/shard_map/ppermute | solution.py:660
  230.4 3.0 %collective-permute-done.28.refs_4_ = bf16[128,1024]{1,0:T(8,128)(2,1)S(1)} collective-permute-done((bf16[128,1024]{1,0:T(8,128)(2,1)S(1)}, bf16[128,1024]{1,0:T(8,128)(2,1)S(1)}, u32[]{:S(2)}, u32[]{:S(2)}) %collective-permute-start.28) | collective-permute-done | bytes 262176 | tf_op jit(solution)/shard_map/ppermute | solution.py:660
  (131 shorter events, 65.9 us)
Async XLA Ops:
  6.1 10.5 %collective-permute-start.4 = (bf16[592,256]{1,0:T(8,128)(2,1)}, bf16[592,256]{1,0:T(8,128)(2,1)S(1)}, u32[]{:S(2)}, u32[]{:S(2)}) collective-permute-start(bf16[592,256]{1,0:T(8,128)(2,1)} %get-tuple-element.56.refs_4_), channel_id=1, source_target_pairs={{0,2},{2,0},{4,6},{6,4},{1,3},{3,1},{5,7},{7,5},{8,10},{10,8},{12,... | collective-permute-start | bytes 909320 | tf_op jit(solution)/shard_map/ppermute | solution.py:541
  6.1 22.4 %collective-permute-start.3 = (bf16[592,256]{1,0:T(8,128)(2,1)}, bf16[592,256]{1,0:T(8,128)(2,1)S(1)}, u32[]{:S(2)}, u32[]{:S(2)}) collective-permute-start(bf16[592,256]{1,0:T(8,128)(2,1)} %get-tuple-element.56.refs_4_), channel_id=1, source_target_pairs={{0,1},{1,0},{2,3},{3,2},{4,5},{5,4},{6,7},{7,6},{8,9},{9,8},{10,11... | collective-permute-start | bytes 909320 | tf_op jit(solution)/shard_map/ppermute | solution.py:35
  8.1 11.6 %collective-permute-start = (bf16[592,256]{1,0:T(8,128)(2,1)}, bf16[592,256]{1,0:T(8,128)(2,1)S(1)}, u32[]{:S(2)}, u32[]{:S(2)}) collective-permute-start(bf16[592,256]{1,0:T(8,128)(2,1)} %get-tuple-element.56.refs_4_), channel_id=1, source_target_pairs={{2,4},{4,2},{3,5},{5,3},{10,12},{12,10},{11,13},{13,11},{18,20},{2... | collective-permute-start | bytes 909320 | tf_op jit(solution)/shard_map/ppermute | solution.py:542
  16.6 10.0 %collective-permute-start.6 = (bf16[592,256]{1,0:T(8,128)(2,1)S(1)}, bf16[592,256]{1,0:T(8,128)(2,1)S(1)}, u32[]{:S(2)}, u32[]{:S(2)}) collective-permute-start(bf16[592,256]{1,0:T(8,128)(2,1)S(1)} %collective-permute-done.4.refs_6_), channel_id=1, source_target_pairs={{2,4},{4,2},{3,5},{5,3},{10,12},{12,10},{11,13},{13,11},{18,20},{2... | collective-permute-start | bytes 909320 | tf_op jit(solution)/shard_map/ppermute | solution.py:543
  26.5 10.3 %collective-permute-start.7 = (bf16[592,256]{1,0:T(8,128)(2,1)S(1)}, bf16[592,256]{1,0:T(8,128)(2,1)S(1)}, u32[]{:S(2)}, u32[]{:S(2)}) collective-permute-start(bf16[592,256]{1,0:T(8,128)(2,1)S(1)} %collective-permute-done.6), channel_id=1, source_target_pairs={{2,0},{4,6},{3,1},{5,7},{10,8},{12,14},{11,9},{13,15},{18,16},{20,... | collective-permute-start | bytes 909320 | tf_op jit(solution)/shard_map/ppermute | solution.py:545
  27.9 17.5 %collective-permute-start.2 = (bf16[592,256]{1,0:T(8,128)(2,1)S(1)}, bf16[592,256]{1,0:T(8,128)(2,1)S(1)}, u32[]{:S(2)}, u32[]{:S(2)}) collective-permute-start(bf16[592,256]{1,0:T(8,128)(2,1)S(1)} %broadcast_select_fusion.1.refs_4_), channel_id=1, source_target_pairs={{0,1},{1,0},{2,3},{3,2},{4,5},{5,4},{6,7},{7,6},{8,9},{9,8},{10,11... | collective-permute-start | bytes 909320 | tf_op jit(solution)/shard_map/ppermute | solution.py:35
  36.9 8.5 %collective-permute-start.8 = (bf16[592,256]{1,0:T(8,128)(2,1)S(1)}, bf16[592,256]{1,0:T(8,128)(2,1)S(1)}, u32[]{:S(2)}, u32[]{:S(2)}) collective-permute-start(bf16[592,256]{1,0:T(8,128)(2,1)S(1)} %broadcast_select_fusion.refs_6_), channel_id=1, source_target_pairs={{0,1},{1,0},{2,3},{3,2},{4,5},{5,4},{6,7},{7,6},{8,9},{9,8},{10,11... | collective-permute-start | bytes 909320 | tf_op jit(solution)/shard_map/ppermute | solution.py:35
  62.1 9.6 %collective-permute-start.11 = (bf16[128,1024]{1,0:T(8,128)(2,1)}, bf16[128,1024]{1,0:T(8,128)(2,1)S(1)}, u32[]{:S(2)}, u32[]{:S(2)}) collective-permute-start(bf16[128,1024]{1,0:T(8,128)(2,1)} %get-tuple-element.73.refs_0_), channel_id=1, source_target_pairs={{2,4},{4,2},{3,5},{5,3},{10,12},{12,10},{11,13},{13,11},{18,20},{2... | collective-permute-start | bytes 786440 | tf_op jit(solution)/shard_map/ppermute | solution.py:542
  65.3 9.5 %collective-permute-start.9 = (bf16[128,1024]{1,0:T(8,128)(2,1)}, bf16[128,1024]{1,0:T(8,128)(2,1)S(1)}, u32[]{:S(2)}, u32[]{:S(2)}) collective-permute-start(bf16[128,1024]{1,0:T(8,128)(2,1)} %get-tuple-element.73.refs_0_), channel_id=1, source_target_pairs={{0,2},{2,0},{4,6},{6,4},{1,3},{3,1},{5,7},{7,5},{8,10},{10,8},{12,... | collective-permute-start | bytes 786440 | tf_op jit(solution)/shard_map/ppermute | solution.py:541
  65.6 12.4 %collective-permute-start.10 = (bf16[128,1024]{1,0:T(8,128)(2,1)}, bf16[128,1024]{1,0:T(8,128)(2,1)S(1)}, u32[]{:S(2)}, u32[]{:S(2)}) collective-permute-start(bf16[128,1024]{1,0:T(8,128)(2,1)} %get-tuple-element.74.refs_1_), channel_id=1, source_target_pairs={{0,2},{2,0},{4,6},{6,4},{1,3},{3,1},{5,7},{7,5},{8,10},{10,8},{12,... | collective-permute-start | bytes 786440 | tf_op jit(solution)/shard_map/ppermute | solution.py:541
  67.7 11.1 %collective-permute-start.12 = (bf16[128,1024]{1,0:T(8,128)(2,1)}, bf16[128,1024]{1,0:T(8,128)(2,1)S(1)}, u32[]{:S(2)}, u32[]{:S(2)}) collective-permute-start(bf16[128,1024]{1,0:T(8,128)(2,1)} %get-tuple-element.74.refs_1_), channel_id=1, source_target_pairs={{2,4},{4,2},{3,5},{5,3},{10,12},{12,10},{11,13},{13,11},{18,20},{2... | collective-permute-start | bytes 786440 | tf_op jit(solution)/shard_map/ppermute | solution.py:542
  71.7 9.3 %collective-permute-start.13 = (bf16[128,1024]{1,0:T(8,128)(2,1)S(1)}, bf16[128,1024]{1,0:T(8,128)(2,1)S(1)}, u32[]{:S(2)}, u32[]{:S(2)}) collective-permute-start(bf16[128,1024]{1,0:T(8,128)(2,1)S(1)} %collective-permute-done.11.refs_0_), channel_id=1, source_target_pairs={{2,0},{4,6},{3,1},{5,7},{10,8},{12,14},{11,9},{13,15},{18,16},{20,... | collective-permute-start | bytes 786440 | tf_op jit(solution)/shard_map/ppermute | solution.py:544
  74.8 8.3 %collective-permute-start.14 = (bf16[128,1024]{1,0:T(8,128)(2,1)S(1)}, bf16[128,1024]{1,0:T(8,128)(2,1)S(1)}, u32[]{:S(2)}, u32[]{:S(2)}) collective-permute-start(bf16[128,1024]{1,0:T(8,128)(2,1)S(1)} %collective-permute-done.9.refs_2_), channel_id=1, source_target_pairs={{2,4},{4,2},{3,5},{5,3},{10,12},{12,10},{11,13},{13,11},{18,20},{2... | collective-permute-start | bytes 786440 | tf_op jit(solution)/shard_map/ppermute | solution.py:543
  85.0 27.3 %all-to-all-start = ((bf16[8,56,2048]{2,1,0:T(8,128)(2,1)}), bf16[8,56,2048]{2,1,0:T(8,128)(2,1)}, u32[]{:S(2)}, u32[]{:S(2)}) async-start(bf16[8,56,2048]{2,1,0:T(8,128)(2,1)} %bitcast.19), calls=%async_computation | async-start | bytes 3670016 | tf_op jit(solution)/shard_map/all_to_all | solution.py:630
  89.3 10.5 %collective-permute-start.16 = (bf16[128,1024]{1,0:T(8,128)(2,1)S(1)}, bf16[128,1024]{1,0:T(8,128)(2,1)S(1)}, u32[]{:S(2)}, u32[]{:S(2)}) collective-permute-start(bf16[128,1024]{1,0:T(8,128)(2,1)S(1)} %collective-permute-done.10.refs_3_), channel_id=1, source_target_pairs={{2,4},{4,2},{3,5},{5,3},{10,12},{12,10},{11,13},{13,11},{18,20},{2... | collective-permute-start | bytes 786440 | tf_op jit(solution)/shard_map/ppermute | solution.py:543
  92.0 9.8 %collective-permute-start.15 = (bf16[128,1024]{1,0:T(8,128)(2,1)S(1)}, bf16[128,1024]{1,0:T(8,128)(2,1)S(1)}, u32[]{:S(2)}, u32[]{:S(2)}) collective-permute-start(bf16[128,1024]{1,0:T(8,128)(2,1)S(1)} %collective-permute-done.12.refs_1_), channel_id=1, source_target_pairs={{2,0},{4,6},{3,1},{5,7},{10,8},{12,14},{11,9},{13,15},{18,16},{20,... | collective-permute-start | bytes 786440 | tf_op jit(solution)/shard_map/ppermute | solution.py:544
  93.3 12.2 %collective-permute-start.17 = (bf16[128,1024]{1,0:T(8,128)(2,1)S(1)}, bf16[128,1024]{1,0:T(8,128)(2,1)S(1)}, u32[]{:S(2)}, u32[]{:S(2)}) collective-permute-start(bf16[128,1024]{1,0:T(8,128)(2,1)S(1)} %collective-permute-done.14.refs_4_), channel_id=1, source_target_pairs={{2,0},{4,6},{3,1},{5,7},{10,8},{12,14},{11,9},{13,15},{18,16},{20,... | collective-permute-start | bytes 786440 | tf_op jit(solution)/shard_map/ppermute | solution.py:545
  99.8 10.8 %collective-permute-start.18 = (bf16[128,1024]{1,0:T(8,128)(2,1)S(1)}, bf16[128,1024]{1,0:T(8,128)(2,1)S(1)}, u32[]{:S(2)}, u32[]{:S(2)}) collective-permute-start(bf16[128,1024]{1,0:T(8,128)(2,1)S(1)} %collective-permute-done.16.refs_5_), channel_id=1, source_target_pairs={{2,0},{4,6},{3,1},{5,7},{10,8},{12,14},{11,9},{13,15},{18,16},{20,... | collective-permute-start | bytes 786440 | tf_op jit(solution)/shard_map/ppermute | solution.py:545
  114.2 26.5 %all-to-all-start.1 = ((bf16[8,56,2048]{2,1,0:T(8,128)(2,1)}), bf16[8,56,2048]{2,1,0:T(8,128)(2,1)S(1)}, u32[]{:S(2)}, u32[]{:S(2)}) async-start(bf16[8,56,2048]{2,1,0:T(8,128)(2,1)} %bitcast.21), calls=%async_computation.1 | async-start | bytes 3670016 | tf_op jit(solution)/shard_map/all_to_all | solution.py:630
  142.0 27.1 %all-to-all-start.2 = ((bf16[8,56,2048]{2,1,0:T(8,128)(2,1)}), bf16[8,56,2048]{2,1,0:T(8,128)(2,1)S(1)}, u32[]{:S(2)}, u32[]{:S(2)}) async-start(bf16[8,56,2048]{2,1,0:T(8,128)(2,1)} %bitcast.51), calls=%async_computation.2 | async-start | bytes 3670016 | tf_op jit(solution)/shard_map/all_to_all | solution.py:630
  170.4 26.5 %all-to-all-start.3 = ((bf16[8,56,2048]{2,1,0:T(8,128)(2,1)}), bf16[8,56,2048]{2,1,0:T(8,128)(2,1)S(1)}, u32[]{:S(2)}, u32[]{:S(2)}) async-start(bf16[8,56,2048]{2,1,0:T(8,128)(2,1)} %bitcast.49), calls=%async_computation.3 | async-start | bytes 3670016 | tf_op jit(solution)/shard_map/all_to_all | solution.py:630
  176.6 9.2 %collective-permute-start.19 = (bf16[128,1024]{1,0:T(8,128)(2,1)S(1)}, bf16[128,1024]{1,0:T(8,128)(2,1)S(1)}, u32[]{:S(2)}, u32[]{:S(2)}) collective-permute-start(bf16[128,1024]{1,0:T(8,128)(2,1)S(1)} %get-tuple-element.96), channel_id=1, source_target_pairs={{0,2},{2,0},{4,6},{6,4},{1,3},{3,1},{5,7},{7,5},{8,10},{10,8},{12,... | collective-permute-start | bytes 786440 | tf_op jit(solution)/shard_map/ppermute | solution.py:660
  177.8 13.2 %collective-permute-start.20 = (bf16[128,1024]{1,0:T(8,128)(2,1)S(1)}, bf16[128,1024]{1,0:T(8,128)(2,1)S(1)}, u32[]{:S(2)}, u32[]{:S(2)}) collective-permute-start(bf16[128,1024]{1,0:T(8,128)(2,1)S(1)} %get-tuple-element.97), channel_id=1, source_target_pairs={{0,2},{2,0},{4,6},{6,4},{1,3},{3,1},{5,7},{7,5},{8,10},{10,8},{12,... | collective-permute-start | bytes 786440 | tf_op jit(solution)/shard_map/ppermute | solution.py:660
  197.6 11.2 %collective-permute-start.21 = (bf16[128,1024]{1,0:T(8,128)(2,1)S(1)}, bf16[128,1024]{1,0:T(8,128)(2,1)S(1)}, u32[]{:S(2)}, u32[]{:S(2)}) collective-permute-start(bf16[128,1024]{1,0:T(8,128)(2,1)S(1)} %get-tuple-element.104), channel_id=1, source_target_pairs={{0,2},{6,4},{1,3},{7,5},{8,10},{14,12},{9,11},{15,13},{16,18},{22,... | collective-permute-start | bytes 786440 | tf_op jit(solution)/shard_map/ppermute | solution.py:660
  199.0 15.4 %collective-permute-start.26 = (bf16[128,1024]{1,0:T(8,128)(2,1)S(1)}, bf16[128,1024]{1,0:T(8,128)(2,1)S(1)}, u32[]{:S(2)}, u32[]{:S(2)}) collective-permute-start(bf16[128,1024]{1,0:T(8,128)(2,1)S(1)} %get-tuple-element.107), channel_id=1, source_target_pairs={{0,2},{6,4},{1,3},{7,5},{8,10},{14,12},{9,11},{15,13},{16,18},{22,... | collective-permute-start | bytes 786440 | tf_op jit(solution)/shard_map/ppermute | solution.py:660
  208.8 10.3 %collective-permute-start.24 = (bf16[128,1024]{1,0:T(8,128)(2,1)S(1)}, bf16[128,1024]{1,0:T(8,128)(2,1)S(1)}, u32[]{:S(2)}, u32[]{:S(2)}) collective-permute-start(bf16[128,1024]{1,0:T(8,128)(2,1)S(1)} %get-tuple-element.106), channel_id=1, source_target_pairs={{0,2},{6,4},{1,3},{7,5},{8,10},{14,12},{9,11},{15,13},{16,18},{22,... | collective-permute-start | bytes 786440 | tf_op jit(solution)/shard_map/ppermute | solution.py:660
  210.2 11.6 %collective-permute-start.29 = (bf16[128,1024]{1,0:T(8,128)(2,1)S(1)}, bf16[128,1024]{1,0:T(8,128)(2,1)S(1)}, u32[]{:S(2)}, u32[]{:S(2)}) collective-permute-start(bf16[128,1024]{1,0:T(8,128)(2,1)S(1)} %add_convert_fusion.1), channel_id=1, source_target_pairs={{2,4},{4,2},{3,5},{5,3},{10,12},{12,10},{11,13},{13,11},{18,20},{2... | collective-permute-start | bytes 786440 | tf_op jit(solution)/shard_map/ppermute | solution.py:660
  214.5 10.8 %collective-permute-start.27 = (bf16[128,1024]{1,0:T(8,128)(2,1)S(1)}, bf16[128,1024]{1,0:T(8,128)(2,1)S(1)}, u32[]{:S(2)}, u32[]{:S(2)}) collective-permute-start(bf16[128,1024]{1,0:T(8,128)(2,1)S(1)} %add_convert_fusion.2), channel_id=1, source_target_pairs={{2,4},{4,2},{3,5},{5,3},{10,12},{12,10},{11,13},{13,11},{18,20},{2... | collective-permute-start | bytes 786440 | tf_op jit(solution)/shard_map/ppermute | solution.py:660
  217.0 9.6 %collective-permute-start.22 = (bf16[128,1024]{1,0:T(8,128)(2,1)S(1)}, bf16[128,1024]{1,0:T(8,128)(2,1)S(1)}, u32[]{:S(2)}, u32[]{:S(2)}) collective-permute-start(bf16[128,1024]{1,0:T(8,128)(2,1)S(1)} %get-tuple-element.105), channel_id=1, source_target_pairs={{0,2},{6,4},{1,3},{7,5},{8,10},{14,12},{9,11},{15,13},{16,18},{22,... | collective-permute-start | bytes 786440 | tf_op jit(solution)/shard_map/ppermute | solution.py:660
  219.1 14.3 %collective-permute-start.25 = (bf16[128,1024]{1,0:T(8,128)(2,1)S(1)}, bf16[128,1024]{1,0:T(8,128)(2,1)S(1)}, u32[]{:S(2)}, u32[]{:S(2)}) collective-permute-start(bf16[128,1024]{1,0:T(8,128)(2,1)S(1)} %add_convert_fusion.3), channel_id=1, source_target_pairs={{2,4},{4,2},{3,5},{5,3},{10,12},{12,10},{11,13},{13,11},{18,20},{2... | collective-permute-start | bytes 786440 | tf_op jit(solution)/shard_map/ppermute | solution.py:660
  221.7 8.7 %collective-permute-start.30 = (bf16[128,1024]{1,0:T(8,128)(2,1)S(1)}, bf16[128,1024]{1,0:T(8,128)(2,1)S(1)}, u32[]{:S(2)}, u32[]{:S(2)}) collective-permute-start(bf16[128,1024]{1,0:T(8,128)(2,1)S(1)} %collective-permute-done.29), channel_id=1, source_target_pairs={{2,0},{4,6},{3,1},{5,7},{10,8},{12,14},{11,9},{13,15},{18,16},{20,... | collective-permute-start | bytes 786440 | tf_op jit(solution)/shard_map/ppermute | solution.py:660
  226.7 8.6 %collective-permute-start.23 = (bf16[128,1024]{1,0:T(8,128)(2,1)S(1)}, bf16[128,1024]{1,0:T(8,128)(2,1)S(1)}, u32[]{:S(2)}, u32[]{:S(2)}) collective-permute-start(bf16[128,1024]{1,0:T(8,128)(2,1)S(1)} %add_convert_fusion.4), channel_id=1, source_target_pairs={{2,4},{4,2},{3,5},{5,3},{10,12},{12,10},{11,13},{13,11},{18,20},{2... | collective-permute-start | bytes 786440 | tf_op jit(solution)/shard_map/ppermute | solution.py:660
  (19 other events, 186.5 us)

commit v4 on v3

--- a/solution.py
+++ b/solution.py
@@ -278,7 +278,7 @@
         out_shape=out_shape,
         scratch_shapes=scratch,
         input_output_aliases=aliases,
-        compiler_params=pltpu.CompilerParams(vmem_limit_bytes=56 * MIB),
+        compiler_params=pltpu.CompilerParams(vmem_limit_bytes=28 * MIB),
         cost_estimate=pl.CostEstimate(
             flops=2 * H * rows * keys * (2 * latent_width + rotary_width) // count,
             bytes_accessed=16 * MIB // count,
@@ -395,7 +395,7 @@
             pltpu.VMEM((each, width), jnp.bfloat16),
             pltpu.VMEM((each, width), jnp.float32),
         ],
-        compiler_params=pltpu.CompilerParams(vmem_limit_bytes=58 * MIB),
+        compiler_params=pltpu.CompilerParams(vmem_limit_bytes=44 * MIB),
         cost_estimate=pl.CostEstimate(
             flops=6 * rows * width * half * slabs_each,
             bytes_accessed=2 * 3 * width * half * experts_here * slabs_each,
@@ -430,7 +430,7 @@
     return pl.pallas_call(
         functools.partial(pack_kernel, layers),
         out_shape=jax.ShapeDtypeStruct((rows, width), jnp.bfloat16),
-        compiler_params=pltpu.CompilerParams(vmem_limit_bytes=40 * MIB),
+        compiler_params=pltpu.CompilerParams(vmem_limit_bytes=24 * MIB),
         cost_estimate=pl.CostEstimate(
             flops=2 * rows * tokens * width, bytes_accessed=6 * rows * width, transcendentals=0
         ),
@@ -453,7 +453,7 @@
     return pl.pallas_call(
         combine_kernel,
         out_shape=out_shape,
-        compiler_params=pltpu.CompilerParams(vmem_limit_bytes=40 * MIB),
+        compiler_params=pltpu.CompilerParams(vmem_limit_bytes=24 * MIB),
         cost_estimate=pl.CostEstimate(
             flops=2 * weights.shape[0] * rows.size,
             bytes_accessed=4 * rows.size,
@@ -677,7 +677,7 @@
     layer_out = pl.pallas_call(
         finish_kernel,
         out_shape=jax.ShapeDtypeStruct((row_count, model_width), jnp.bfloat16),
-        compiler_params=pltpu.CompilerParams(vmem_limit_bytes=40 * MIB),
+        compiler_params=pltpu.CompilerParams(vmem_limit_bytes=24 * MIB),
     )(residual, own_part, *near_arrived, *middle_arrived, *far_arrived)
     return (layer_out[None], new_entries.T[None])
 

time: 239 us -> 235 us (0.983)
  Pallas kernels: 79.9 us -> 70.2 us
  starting transfers between devices: 68.6 us -> 74 us
  waiting for transfers between devices: 65.2 us -> 62 us
  local copies, waits for them, and re-layouts: 12.1 us -> 15.2 us
    pallas_call x3, Pallas kernels: 29.6 us -> 21.8 us  [attention_call(): pl.pallas_call(functools.partial(kernel, score_scale, first_slot, y_count...]
    pallas_call x2, Pallas kernels: 42.1 us -> 39.1 us  [experts(): pl.pallas_call(functools.partial(experts_kernel, slabs_each, sorting), gr...]
    ppermute x4, waiting for transfers between devices: 0.13 us -> 2.53 us  [shifted(): lax.ppermute(values, axis, [(i, (i + step) % count) for i in range(count)])]
    unnamed x35 -> x37, local copies, waits for them, and re-layouts: 9.36 us -> 11.6 us
  transfers between devices with their start and end apart: 35 -> 35, of which waited for: 24 -> 24; matrix products, arithmetic and copies ran while one was open for 5% -> 5% of each run, Pallas kernels for 24% -> 21%
where the time goes in v4:
time: 235 us; the launch traced here: 231 us
  starting transfers between devices  74 us (31%)
  Pallas kernels  70.2 us (30%)
  waiting for transfers between devices  62 us (26%)
  local copies, waits for them, and re-layouts  15.2 us (6%)
  other arithmetic  5.18 us (2%)
  matrix products  2.68 us (1%)
    pallas_call x2, Pallas kernels, experts(): pl.pallas_call(functools.partial(experts_kernel, slabs_each, sorting), gr...  39.1 us
    ppermute x12, waiting for transfers between devices, moved(): return lax.ppermute(value, 'z', pairs)  28.6 us
    ppermute x12, starting transfers between devices, moved(): return lax.ppermute(value, 'z', pairs)  22.6 us
    pallas_call x3, Pallas kernels, attention_call(): pl.pallas_call(functools.partial(kernel, score_scale, first_slot, y_count...  21.8 us
    all_to_all x4, starting transfers between devices, exchanged(): lax.all_to_all(values, PLANE_AXES, split_axis=0, concat_axis=0, tiled=True)  15.2 us
    unnamed x37, local copies, waits for them, and re-layouts  11.6 us
    ppermute x3, starting transfers between devices, along_z(): middle = lax.ppermute(values, 'z', MIDDLE)  10.4 us
    all_to_all x4, waiting for transfers between devices, exchanged(): lax.all_to_all(values, PLANE_AXES, split_axis=0, concat_axis=0, tiled=True)  10.2 us
  transfers between devices with their start and end apart: 35, of which 24 were waited for; matrix products, arithmetic and copies ran while one was open for 5% of the time, Pallas kernels for 21%

profile of v4, /device:TPU:8, one launch (start us, length us, event | category | flops | bytes accessed | tf_op | source)
XLA Modules:
  0.0 231.2 jit_solution(763266472617663100)
XLA Ops:
  8.1 4.6 %collective-permute-start = (bf16[592,256]{1,0:T(8,128)(2,1)}, bf16[592,256]{1,0:T(8,128)(2,1)S(1)}, u32[]{:S(2)}, u32[]{:S(2)}) collective-permute-start(bf16[592,256]{1,0:T(8,128)(2,1)} %get-tuple-element.56.refs_4_), channel_id=1, source_target_pairs={{2,4},{4,2},{3,5},{5,3},{10,12},{12,10},{11,13},{13,11},{18,20},{2... | collective-permute-start | bytes 909320 | tf_op jit(solution)/shard_map/ppermute | solution.py:542
  15.7 3.0 %collective-permute-start.6 = (bf16[592,256]{1,0:T(8,128)(2,1)S(1)}, bf16[592,256]{1,0:T(8,128)(2,1)}, u32[]{:S(2)}, u32[]{:S(2)}) collective-permute-start(bf16[592,256]{1,0:T(8,128)(2,1)S(1)} %collective-permute-done.4.refs_6_), channel_id=1, source_target_pairs={{2,4},{4,2},{3,5},{5,3},{10,12},{12,10},{11,13},{13,11},{18,20},{2... | collective-permute-start | bytes 909320 | tf_op jit(solution)/shard_map/ppermute | solution.py:543
  30.1 2.2 copy-done
  32.3 4.8 %shard_map.150 = (f32[8,256,1]{2,1,0:T(8,128)S(1)}, f32[8,256,1]{2,1,0:T(8,128)S(1)}, f32[8,256,512]{2,1,0:T(8,128)S(1)}) custom-call(s32[12]{0:T(128)S(1)} %concatenate.26.refs_0_, bf16[128,2048]{1,0:T(8,128)(2,1)S(1)} %copy.59.refs_1_, bf16[16,128,64]{2,1,0:T(8,128)(2,1)S(1)} %pad_maximum_fusion.refs_2_, bf16[512,4096]{1,0:T(8,128)(2,1)S(1)} %copy-done, ...), custom_call_target="tpu_custom_call" | custom-call | flops 2281701376 | bytes 8388608 | tf_op jit(solution)/shard_map/pallas_call | solution.py:273
  39.4 4.8 %shard_map.151 = (f32[8,256,1]{2,1,0:T(8,128)S(1)}, f32[8,256,1]{2,1,0:T(8,128)S(1)}, f32[8,256,512]{2,1,0:T(8,128)S(1)}) custom-call(s32[12]{0:T(128)S(1)} %concatenate.26.refs_0_, bf16[128,2048]{1,0:T(8,128)(2,1)S(1)} %copy.59.refs_1_, ...), custom_call_target="tpu_custom_call", output_to_operand_aliasing={{0}: (8, {}), {1}: (9, {}), {2}: (10, {})} | custom-call | flops 2281701376 | bytes 8388608 | tf_op jit(solution)/shard_map/pallas_call | solution.py:273
  45.0 12.2 %shard_map.152 = (f32[128,2048]{1,0:T(8,128)S(1)}, bf16[128,1024]{1,0:T(8,128)(2,1)S(1)}, bf16[128,1024]{1,0:T(8,128)(2,1)S(1)}) custom-call(s32[12]{0:T(128)S(1)} %concatenate.26.refs_0_, bf16[128,2048]{1,0:T(8,128)(2,1)S(1)} %copy.59.refs_1_, bf16[16,128,64]{2,1,0:T(8,128)(2,1)S(1)} %pad_maximum_fusion.refs_2_, bf16[512,4096]{1,0:T(8,128)(2,1)S(1)} %copy-done.1, ...), custom_call_target="tpu_custom_call" | custom-call | flops 4563402752 | bytes 16777216 | tf_op jit(solution)/shard_map/pallas_call | solution.py:273
  58.2 3.0 %collective-permute-start.11 = (bf16[128,1024]{1,0:T(8,128)(2,1)S(1)}, bf16[128,1024]{1,0:T(8,128)(2,1)S(1)}, u32[]{:S(2)}, u32[]{:S(2)}) collective-permute-start(bf16[128,1024]{1,0:T(8,128)(2,1)S(1)} %get-tuple-element.73.refs_0_), channel_id=1, source_target_pairs={{2,4},{4,2},{3,5},{5,3},{10,12},{12,10},{11,13},{13,11},{18,20},{2... | collective-permute-start | bytes 786440 | tf_op jit(solution)/shard_map/ppermute | solution.py:542
  63.5 2.9 %collective-permute-start.12 = (bf16[128,1024]{1,0:T(8,128)(2,1)S(1)}, bf16[128,1024]{1,0:T(8,128)(2,1)S(1)}, u32[]{:S(2)}, u32[]{:S(2)}) collective-permute-start(bf16[128,1024]{1,0:T(8,128)(2,1)S(1)} %get-tuple-element.74.refs_1_), channel_id=1, source_target_pairs={{2,4},{4,2},{3,5},{5,3},{10,12},{12,10},{11,13},{13,11},{18,20},{2... | collective-permute-start | bytes 786440 | tf_op jit(solution)/shard_map/ppermute | solution.py:542
  66.4 2.7 %collective-permute-done.11.refs_0_ = bf16[128,1024]{1,0:T(8,128)(2,1)S(1)} collective-permute-done((bf16[128,1024]{1,0:T(8,128)(2,1)S(1)}, bf16[128,1024]{1,0:T(8,128)(2,1)S(1)}, u32[]{:S(2)}, u32[]{:S(2)}) %collective-permute-start.11) | collective-permute-done | bytes 262176 | tf_op jit(solution)/shard_map/ppermute | solution.py:542
  70.4 3.1 %collective-permute-start.14 = (bf16[128,1024]{1,0:T(8,128)(2,1)S(1)}, bf16[128,1024]{1,0:T(8,128)(2,1)S(1)}, u32[]{:S(2)}, u32[]{:S(2)}) collective-permute-start(bf16[128,1024]{1,0:T(8,128)(2,1)S(1)} %collective-permute-done.9.refs_2_), channel_id=1, source_target_pairs={{2,4},{4,2},{3,5},{5,3},{10,12},{12,10},{11,13},{13,11},{18,20},{2... | collective-permute-start | bytes 786440 | tf_op jit(solution)/shard_map/ppermute | solution.py:543
  74.9 3.7 %collective-permute-done.14.refs_4_ = bf16[128,1024]{1,0:T(8,128)(2,1)S(1)} collective-permute-done((bf16[128,1024]{1,0:T(8,128)(2,1)S(1)}, bf16[128,1024]{1,0:T(8,128)(2,1)S(1)}, u32[]{:S(2)}, u32[]{:S(2)}) %collective-permute-start.14) | collective-permute-done | bytes 262176 | tf_op jit(solution)/shard_map/ppermute | solution.py:543
  80.5 3.6 %all-to-all-start = ((bf16[8,56,2048]{2,1,0:T(8,128)(2,1)}), bf16[8,56,2048]{2,1,0:T(8,128)(2,1)S(1)}, u32[]{:S(2)}, u32[]{:S(2)}) async-start(bf16[8,56,2048]{2,1,0:T(8,128)(2,1)} %bitcast.19), calls=%async_computation | async-start | bytes 3670016 | tf_op jit(solution)/shard_map/all_to_all | solution.py:630
  84.2 3.1 %collective-permute-start.16 = (bf16[128,1024]{1,0:T(8,128)(2,1)S(1)}, bf16[128,1024]{1,0:T(8,128)(2,1)}, u32[]{:S(2)}, u32[]{:S(2)}) collective-permute-start(bf16[128,1024]{1,0:T(8,128)(2,1)S(1)} %collective-permute-done.10.refs_3_), channel_id=1, source_target_pairs={{2,4},{4,2},{3,5},{5,3},{10,12},{12,10},{11,13},{13,11},{18,20},{2... | collective-permute-start | bytes 786440 | tf_op jit(solution)/shard_map/ppermute | solution.py:543
  91.5 3.3 %collective-permute-done.16.refs_5_ = bf16[128,1024]{1,0:T(8,128)(2,1)} collective-permute-done((bf16[128,1024]{1,0:T(8,128)(2,1)S(1)}, bf16[128,1024]{1,0:T(8,128)(2,1)}, u32[]{:S(2)}, u32[]{:S(2)}) %collective-permute-start.16) | collective-permute-done | bytes 262176 | tf_op jit(solution)/shard_map/ppermute | solution.py:543
  98.5 2.4 %collective-permute-done.17.refs_6_ = bf16[128,1024]{1,0:T(8,128)(2,1)} collective-permute-done((bf16[128,1024]{1,0:T(8,128)(2,1)S(1)}, bf16[128,1024]{1,0:T(8,128)(2,1)}, u32[]{:S(2)}, u32[]{:S(2)}) %collective-permute-start.17) | collective-permute-done | bytes 262176 | tf_op jit(solution)/shard_map/ppermute | solution.py:545
  100.9 5.3 %collective-permute-done.18.refs_7_ = bf16[128,1024]{1,0:T(8,128)(2,1)S(1)} collective-permute-done((bf16[128,1024]{1,0:T(8,128)(2,1)}, bf16[128,1024]{1,0:T(8,128)(2,1)S(1)}, u32[]{:S(2)}, u32[]{:S(2)}) %collective-permute-start.18) | collective-permute-done | bytes 262176 | tf_op jit(solution)/shard_map/ppermute | solution.py:545
  107.2 3.0 %shard_map.155 = bf16[448,2048]{1,0:T(8,128)(2,1)} custom-call(bf16[448,256]{1,0:T(8,128)(2,1)S(1)} %copy.66.place_ref, bf16[128,1024]{1,0:T(8,128)(2,1)S(1)} %collective-permute-done.11.refs_0_, bf16[128,1024]{1,0:T(8,128)(2,1)S(1)} %collective-permute-done.12.refs_1_, bf16[128,1024]{1,0:T(8,128)(2,1)S(1)} %collective-permute-done.13.refs_2_, ...), custom_call_target="tpu_custom_call" | custom-call | flops 469762048 | bytes 5505024 | tf_op jit(solution)/shard_map/pallas_call | solution.py:430
  110.2 4.3 %all-to-all-start.1 = ((bf16[8,56,2048]{2,1,0:T(8,128)(2,1)}), bf16[8,56,2048]{2,1,0:T(8,128)(2,1)}, u32[]{:S(2)}, u32[]{:S(2)}) async-start(bf16[8,56,2048]{2,1,0:T(8,128)(2,1)} %bitcast.21), calls=%async_computation.1 | async-start | bytes 3670016 | tf_op jit(solution)/shard_map/all_to_all | solution.py:630
  114.8 18.2 %shard_map.154 = bf16[448,2048]{1,0:T(8,128)(2,1)S(1)} custom-call(bf16[448,2048]{1,0:T(8,128)(2,1)S(1)} %bitcast.51, bf16[2,224,448]{2,1,0:T(8,128)(2,1)S(1)} %fusion.8.refs_0_, bf16[2,448,224]{2,1,0:T(8,128)(2,1)S(1)} %fusion.9.refs_1_, bf16[4,2048,1408]{2,1,0:T(8,128)(2,1)} %refs_3_.9, bf16[4,2048,1408]{2,1,0:T(8,128)(2,1)} %refs_3_.9, ...), custom_call_target="tpu_custom_call" | custom-call | flops 7751073792 | bytes 34603008 | tf_op jit(solution)/shard_map/pallas_call | solution.py:388
  134.3 3.2 %all-to-all-done.1 = bf16[8,56,2048]{2,1,0:T(8,128)(2,1)} async-done(((bf16[8,56,2048]{2,1,0:T(8,128)(2,1)}), bf16[8,56,2048]{2,1,0:T(8,128)(2,1)}, u32[]{:S(2)}, u32[]{:S(2)}) %all-to-all-start.1) | async-done | bytes 1835040 | tf_op jit(solution)/shard_map/all_to_all | solution.py:630
  137.5 3.6 %all-to-all-start.2 = ((bf16[8,56,2048]{2,1,0:T(8,128)(2,1)}), bf16[8,56,2048]{2,1,0:T(8,128)(2,1)S(1)}, u32[]{:S(2)}, u32[]{:S(2)}) async-start(bf16[8,56,2048]{2,1,0:T(8,128)(2,1)} %bitcast.53), calls=%async_computation.2 | async-start | bytes 3670016 | tf_op jit(solution)/shard_map/all_to_all | solution.py:630
  141.1 20.9 %shard_map.156 = bf16[448,2048]{1,0:T(8,128)(2,1)S(1)} custom-call(bf16[448,2048]{1,0:T(8,128)(2,1)} %bitcast.22.x_ref, bf16[2,224,448]{2,1,0:T(8,128)(2,1)S(1)} %fusion.8.refs_0_, bf16[2,448,224]{2,1,0:T(8,128)(2,1)S(1)} %fusion.9.refs_1_, bf16[4,2048,1408]{2,1,0:T(8,128)(2,1)} %refs_3_.9, bf16[4,2048,1408]{2,1,0:T(8,128)(2,1)} %refs_3_.9, ...), custom_call_target="tpu_custom_call" | custom-call | flops 7751073792 | bytes 34603008 | tf_op jit(solution)/shard_map/pallas_call | solution.py:388
  165.2 3.6 %all-to-all-start.3 = ((bf16[8,56,2048]{2,1,0:T(8,128)(2,1)}), bf16[8,56,2048]{2,1,0:T(8,128)(2,1)S(1)}, u32[]{:S(2)}, u32[]{:S(2)}) async-start(bf16[8,56,2048]{2,1,0:T(8,128)(2,1)} %bitcast.52), calls=%async_computation.3 | async-start | bytes 3670016 | tf_op jit(solution)/shard_map/all_to_all | solution.py:630
  173.9 6.8 %collective-permute-done.19.refs_0_ = bf16[128,1024]{1,0:T(8,128)(2,1)S(1)} collective-permute-done((bf16[128,1024]{1,0:T(8,128)(2,1)S(1)}, bf16[128,1024]{1,0:T(8,128)(2,1)S(1)}, u32[]{:S(2)}, u32[]{:S(2)}) %collective-permute-start.19) | collective-permute-done | bytes 262176 | tf_op jit(solution)/shard_map/ppermute | solution.py:660
  180.7 5.1 %collective-permute-done.20.refs_1_ = bf16[128,1024]{1,0:T(8,128)(2,1)S(1)} collective-permute-done((bf16[128,1024]{1,0:T(8,128)(2,1)S(1)}, bf16[128,1024]{1,0:T(8,128)(2,1)S(1)}, u32[]{:S(2)}, u32[]{:S(2)}) %collective-permute-start.20) | collective-permute-done | bytes 262176 | tf_op jit(solution)/shard_map/ppermute | solution.py:660
  186.5 5.3 %all-to-all-done.3 = bf16[8,56,2048]{2,1,0:T(8,128)(2,1)S(1)} async-done(((bf16[8,56,2048]{2,1,0:T(8,128)(2,1)}), bf16[8,56,2048]{2,1,0:T(8,128)(2,1)S(1)}, u32[]{:S(2)}, u32[]{:S(2)}) %all-to-all-start.3) | async-done | bytes 1835040 | tf_op jit(solution)/shard_map/all_to_all | solution.py:630
  195.2 8.5 %collective-permute-done.21 = bf16[128,1024]{1,0:T(8,128)(2,1)S(1)} collective-permute-done((bf16[128,1024]{1,0:T(8,128)(2,1)S(1)}, bf16[128,1024]{1,0:T(8,128)(2,1)S(1)}, u32[]{:S(2)}, u32[]{:S(2)}) %collective-permute-start.21) | collective-permute-done | bytes 262176 | tf_op jit(solution)/shard_map/ppermute | solution.py:660
  205.0 3.0 %collective-permute-start.29 = (bf16[128,1024]{1,0:T(8,128)(2,1)S(1)}, bf16[128,1024]{1,0:T(8,128)(2,1)S(1)}, u32[]{:S(2)}, u32[]{:S(2)}) collective-permute-start(bf16[128,1024]{1,0:T(8,128)(2,1)S(1)} %add_convert_fusion.1), channel_id=1, source_target_pairs={{2,4},{4,2},{3,5},{5,3},{10,12},{12,10},{11,13},{13,11},{18,20},{2... | collective-permute-start | bytes 786440 | tf_op jit(solution)/shard_map/ppermute | solution.py:660
  209.4 3.0 %collective-permute-start.27 = (bf16[128,1024]{1,0:T(8,128)(2,1)S(1)}, bf16[128,1024]{1,0:T(8,128)(2,1)S(1)}, u32[]{:S(2)}, u32[]{:S(2)}) collective-permute-start(bf16[128,1024]{1,0:T(8,128)(2,1)S(1)} %add_convert_fusion.2), channel_id=1, source_target_pairs={{2,4},{4,2},{3,5},{5,3},{10,12},{12,10},{11,13},{13,11},{18,20},{2... | collective-permute-start | bytes 786440 | tf_op jit(solution)/shard_map/ppermute | solution.py:660
  214.0 3.0 %collective-permute-start.25 = (bf16[128,1024]{1,0:T(8,128)(2,1)S(1)}, bf16[128,1024]{1,0:T(8,128)(2,1)S(1)}, u32[]{:S(2)}, u32[]{:S(2)}) collective-permute-start(bf16[128,1024]{1,0:T(8,128)(2,1)S(1)} %add_convert_fusion.3), channel_id=1, source_target_pairs={{2,4},{4,2},{3,5},{5,3},{10,12},{12,10},{11,13},{13,11},{18,20},{2... | collective-permute-start | bytes 786440 | tf_op jit(solution)/shard_map/ppermute | solution.py:660
  221.6 3.0 %collective-permute-start.23 = (bf16[128,1024]{1,0:T(8,128)(2,1)S(1)}, bf16[128,1024]{1,0:T(8,128)(2,1)S(1)}, u32[]{:S(2)}, u32[]{:S(2)}) collective-permute-start(bf16[128,1024]{1,0:T(8,128)(2,1)S(1)} %add_convert_fusion.4), channel_id=1, source_target_pairs={{2,4},{4,2},{3,5},{5,3},{10,12},{12,10},{11,13},{13,11},{18,20},{2... | collective-permute-start | bytes 786440 | tf_op jit(solution)/shard_map/ppermute | solution.py:660
  225.7 3.1 %collective-permute-done.28.refs_4_ = bf16[128,1024]{1,0:T(8,128)(2,1)S(1)} collective-permute-done((bf16[128,1024]{1,0:T(8,128)(2,1)S(1)}, bf16[128,1024]{1,0:T(8,128)(2,1)S(1)}, u32[]{:S(2)}, u32[]{:S(2)}) %collective-permute-start.28) | collective-permute-done | bytes 262176 | tf_op jit(solution)/shard_map/ppermute | solution.py:660
  (134 shorter events, 67.3 us)
Async XLA Ops:
  6.1 9.6 %collective-permute-start.4 = (bf16[592,256]{1,0:T(8,128)(2,1)}, bf16[592,256]{1,0:T(8,128)(2,1)S(1)}, u32[]{:S(2)}, u32[]{:S(2)}) collective-permute-start(bf16[592,256]{1,0:T(8,128)(2,1)} %get-tuple-element.56.refs_4_), channel_id=1, source_target_pairs={{0,2},{2,0},{4,6},{6,4},{1,3},{3,1},{5,7},{7,5},{8,10},{10,8},{12,... | collective-permute-start | bytes 909320 | tf_op jit(solution)/shard_map/ppermute | solution.py:541
  6.1 22.1 %collective-permute-start.3 = (bf16[592,256]{1,0:T(8,128)(2,1)}, bf16[592,256]{1,0:T(8,128)(2,1)S(1)}, u32[]{:S(2)}, u32[]{:S(2)}) collective-permute-start(bf16[592,256]{1,0:T(8,128)(2,1)} %get-tuple-element.56.refs_4_), channel_id=1, source_target_pairs={{0,1},{1,0},{2,3},{3,2},{4,5},{5,4},{6,7},{7,6},{8,9},{9,8},{10,11... | collective-permute-start | bytes 909320 | tf_op jit(solution)/shard_map/ppermute | solution.py:35
  8.1 11.7 %collective-permute-start = (bf16[592,256]{1,0:T(8,128)(2,1)}, bf16[592,256]{1,0:T(8,128)(2,1)S(1)}, u32[]{:S(2)}, u32[]{:S(2)}) collective-permute-start(bf16[592,256]{1,0:T(8,128)(2,1)} %get-tuple-element.56.refs_4_), channel_id=1, source_target_pairs={{2,4},{4,2},{3,5},{5,3},{10,12},{12,10},{11,13},{13,11},{18,20},{2... | collective-permute-start | bytes 909320 | tf_op jit(solution)/shard_map/ppermute | solution.py:542
  15.7 10.4 %collective-permute-start.6 = (bf16[592,256]{1,0:T(8,128)(2,1)S(1)}, bf16[592,256]{1,0:T(8,128)(2,1)}, u32[]{:S(2)}, u32[]{:S(2)}) collective-permute-start(bf16[592,256]{1,0:T(8,128)(2,1)S(1)} %collective-permute-done.4.refs_6_), channel_id=1, source_target_pairs={{2,4},{4,2},{3,5},{5,3},{10,12},{12,10},{11,13},{13,11},{18,20},{2... | collective-permute-start | bytes 909320 | tf_op jit(solution)/shard_map/ppermute | solution.py:543
  21.9 8.2 %collective-permute-start.5 = (bf16[592,256]{1,0:T(8,128)(2,1)S(1)}, bf16[592,256]{1,0:T(8,128)(2,1)S(1)}, u32[]{:S(2)}, u32[]{:S(2)}) collective-permute-start(bf16[592,256]{1,0:T(8,128)(2,1)S(1)} %collective-permute-done.4.refs_6_), channel_id=1, source_target_pairs={{0,1},{1,0},{2,3},{3,2},{4,5},{5,4},{6,7},{7,6},{8,9},{9,8},{10,11... | collective-permute-start | bytes 909320 | tf_op jit(solution)/shard_map/ppermute | solution.py:35
  26.1 10.9 %collective-permute-start.7 = (bf16[592,256]{1,0:T(8,128)(2,1)}, bf16[592,256]{1,0:T(8,128)(2,1)S(1)}, u32[]{:S(2)}, u32[]{:S(2)}) collective-permute-start(bf16[592,256]{1,0:T(8,128)(2,1)} %collective-permute-done.6), channel_id=1, source_target_pairs={{2,0},{4,6},{3,1},{5,7},{10,8},{12,14},{11,9},{13,15},{18,16},{20,... | collective-permute-start | bytes 909320 | tf_op jit(solution)/shard_map/ppermute | solution.py:545
  27.5 16.7 %collective-permute-start.2 = (bf16[592,256]{1,0:T(8,128)(2,1)S(1)}, bf16[592,256]{1,0:T(8,128)(2,1)S(1)}, u32[]{:S(2)}, u32[]{:S(2)}) collective-permute-start(bf16[592,256]{1,0:T(8,128)(2,1)S(1)} %broadcast_select_fusion.1.refs_4_), channel_id=1, source_target_pairs={{0,1},{1,0},{2,3},{3,2},{4,5},{5,4},{6,7},{7,6},{8,9},{9,8},{10,11... | collective-permute-start | bytes 909320 | tf_op jit(solution)/shard_map/ppermute | solution.py:35
  58.2 10.8 %collective-permute-start.11 = (bf16[128,1024]{1,0:T(8,128)(2,1)S(1)}, bf16[128,1024]{1,0:T(8,128)(2,1)S(1)}, u32[]{:S(2)}, u32[]{:S(2)}) collective-permute-start(bf16[128,1024]{1,0:T(8,128)(2,1)S(1)} %get-tuple-element.73.refs_0_), channel_id=1, source_target_pairs={{2,4},{4,2},{3,5},{5,3},{10,12},{12,10},{11,13},{13,11},{18,20},{2... | collective-permute-start | bytes 786440 | tf_op jit(solution)/shard_map/ppermute | solution.py:542
  61.2 9.2 %collective-permute-start.9 = (bf16[128,1024]{1,0:T(8,128)(2,1)S(1)}, bf16[128,1024]{1,0:T(8,128)(2,1)S(1)}, u32[]{:S(2)}, u32[]{:S(2)}) collective-permute-start(bf16[128,1024]{1,0:T(8,128)(2,1)S(1)} %get-tuple-element.73.refs_0_), channel_id=1, source_target_pairs={{0,2},{2,0},{4,6},{6,4},{1,3},{3,1},{5,7},{7,5},{8,10},{10,8},{12,... | collective-permute-start | bytes 786440 | tf_op jit(solution)/shard_map/ppermute | solution.py:541
  61.5 12.7 %collective-permute-start.10 = (bf16[128,1024]{1,0:T(8,128)(2,1)S(1)}, bf16[128,1024]{1,0:T(8,128)(2,1)S(1)}, u32[]{:S(2)}, u32[]{:S(2)}) collective-permute-start(bf16[128,1024]{1,0:T(8,128)(2,1)S(1)} %get-tuple-element.74.refs_1_), channel_id=1, source_target_pairs={{0,2},{2,0},{4,6},{6,4},{1,3},{3,1},{5,7},{7,5},{8,10},{10,8},{12,... | collective-permute-start | bytes 786440 | tf_op jit(solution)/shard_map/ppermute | solution.py:541
  63.5 11.2 %collective-permute-start.12 = (bf16[128,1024]{1,0:T(8,128)(2,1)S(1)}, bf16[128,1024]{1,0:T(8,128)(2,1)S(1)}, u32[]{:S(2)}, u32[]{:S(2)}) collective-permute-start(bf16[128,1024]{1,0:T(8,128)(2,1)S(1)} %get-tuple-element.74.refs_1_), channel_id=1, source_target_pairs={{2,4},{4,2},{3,5},{5,3},{10,12},{12,10},{11,13},{13,11},{18,20},{2... | collective-permute-start | bytes 786440 | tf_op jit(solution)/shard_map/ppermute | solution.py:542
  70.4 8.3 %collective-permute-start.14 = (bf16[128,1024]{1,0:T(8,128)(2,1)S(1)}, bf16[128,1024]{1,0:T(8,128)(2,1)S(1)}, u32[]{:S(2)}, u32[]{:S(2)}) collective-permute-start(bf16[128,1024]{1,0:T(8,128)(2,1)S(1)} %collective-permute-done.9.refs_2_), channel_id=1, source_target_pairs={{2,4},{4,2},{3,5},{5,3},{10,12},{12,10},{11,13},{13,11},{18,20},{2... | collective-permute-start | bytes 786440 | tf_op jit(solution)/shard_map/ppermute | solution.py:543
  80.5 26.6 %all-to-all-start = ((bf16[8,56,2048]{2,1,0:T(8,128)(2,1)}), bf16[8,56,2048]{2,1,0:T(8,128)(2,1)S(1)}, u32[]{:S(2)}, u32[]{:S(2)}) async-start(bf16[8,56,2048]{2,1,0:T(8,128)(2,1)} %bitcast.19), calls=%async_computation | async-start | bytes 3670016 | tf_op jit(solution)/shard_map/all_to_all | solution.py:630
  84.2 10.7 %collective-permute-start.16 = (bf16[128,1024]{1,0:T(8,128)(2,1)S(1)}, bf16[128,1024]{1,0:T(8,128)(2,1)}, u32[]{:S(2)}, u32[]{:S(2)}) collective-permute-start(bf16[128,1024]{1,0:T(8,128)(2,1)S(1)} %collective-permute-done.10.refs_3_), channel_id=1, source_target_pairs={{2,4},{4,2},{3,5},{5,3},{10,12},{12,10},{11,13},{13,11},{18,20},{2... | collective-permute-start | bytes 786440 | tf_op jit(solution)/shard_map/ppermute | solution.py:543
  87.4 11.1 %collective-permute-start.15 = (bf16[128,1024]{1,0:T(8,128)(2,1)S(1)}, bf16[128,1024]{1,0:T(8,128)(2,1)}, u32[]{:S(2)}, u32[]{:S(2)}) collective-permute-start(bf16[128,1024]{1,0:T(8,128)(2,1)S(1)} %collective-permute-done.12.refs_1_), channel_id=1, source_target_pairs={{2,0},{4,6},{3,1},{5,7},{10,8},{12,14},{11,9},{13,15},{18,16},{20,... | collective-permute-start | bytes 786440 | tf_op jit(solution)/shard_map/ppermute | solution.py:544
  89.4 11.5 %collective-permute-start.17 = (bf16[128,1024]{1,0:T(8,128)(2,1)S(1)}, bf16[128,1024]{1,0:T(8,128)(2,1)}, u32[]{:S(2)}, u32[]{:S(2)}) collective-permute-start(bf16[128,1024]{1,0:T(8,128)(2,1)S(1)} %collective-permute-done.14.refs_4_), channel_id=1, source_target_pairs={{2,0},{4,6},{3,1},{5,7},{10,8},{12,14},{11,9},{13,15},{18,16},{20,... | collective-permute-start | bytes 786440 | tf_op jit(solution)/shard_map/ppermute | solution.py:545
  94.9 11.3 %collective-permute-start.18 = (bf16[128,1024]{1,0:T(8,128)(2,1)}, bf16[128,1024]{1,0:T(8,128)(2,1)S(1)}, u32[]{:S(2)}, u32[]{:S(2)}) collective-permute-start(bf16[128,1024]{1,0:T(8,128)(2,1)} %collective-permute-done.16.refs_5_), channel_id=1, source_target_pairs={{2,0},{4,6},{3,1},{5,7},{10,8},{12,14},{11,9},{13,15},{18,16},{20,... | collective-permute-start | bytes 786440 | tf_op jit(solution)/shard_map/ppermute | solution.py:545
  110.2 27.3 %all-to-all-start.1 = ((bf16[8,56,2048]{2,1,0:T(8,128)(2,1)}), bf16[8,56,2048]{2,1,0:T(8,128)(2,1)}, u32[]{:S(2)}, u32[]{:S(2)}) async-start(bf16[8,56,2048]{2,1,0:T(8,128)(2,1)} %bitcast.21), calls=%async_computation.1 | async-start | bytes 3670016 | tf_op jit(solution)/shard_map/all_to_all | solution.py:630
  137.5 26.5 %all-to-all-start.2 = ((bf16[8,56,2048]{2,1,0:T(8,128)(2,1)}), bf16[8,56,2048]{2,1,0:T(8,128)(2,1)S(1)}, u32[]{:S(2)}, u32[]{:S(2)}) async-start(bf16[8,56,2048]{2,1,0:T(8,128)(2,1)} %bitcast.53), calls=%async_computation.2 | async-start | bytes 3670016 | tf_op jit(solution)/shard_map/all_to_all | solution.py:630
  165.2 26.5 %all-to-all-start.3 = ((bf16[8,56,2048]{2,1,0:T(8,128)(2,1)}), bf16[8,56,2048]{2,1,0:T(8,128)(2,1)S(1)}, u32[]{:S(2)}, u32[]{:S(2)}) async-start(bf16[8,56,2048]{2,1,0:T(8,128)(2,1)} %bitcast.52), calls=%async_computation.3 | async-start | bytes 3670016 | tf_op jit(solution)/shard_map/all_to_all | solution.py:630
  171.5 9.2 %collective-permute-start.19 = (bf16[128,1024]{1,0:T(8,128)(2,1)S(1)}, bf16[128,1024]{1,0:T(8,128)(2,1)S(1)}, u32[]{:S(2)}, u32[]{:S(2)}) collective-permute-start(bf16[128,1024]{1,0:T(8,128)(2,1)S(1)} %get-tuple-element.96), channel_id=1, source_target_pairs={{0,2},{2,0},{4,6},{6,4},{1,3},{3,1},{5,7},{7,5},{8,10},{10,8},{12,... | collective-permute-start | bytes 786440 | tf_op jit(solution)/shard_map/ppermute | solution.py:660
  172.9 12.8 %collective-permute-start.20 = (bf16[128,1024]{1,0:T(8,128)(2,1)S(1)}, bf16[128,1024]{1,0:T(8,128)(2,1)S(1)}, u32[]{:S(2)}, u32[]{:S(2)}) collective-permute-start(bf16[128,1024]{1,0:T(8,128)(2,1)S(1)} %get-tuple-element.97), channel_id=1, source_target_pairs={{0,2},{2,0},{4,6},{6,4},{1,3},{3,1},{5,7},{7,5},{8,10},{10,8},{12,... | collective-permute-start | bytes 786440 | tf_op jit(solution)/shard_map/ppermute | solution.py:660
  192.5 11.2 %collective-permute-start.21 = (bf16[128,1024]{1,0:T(8,128)(2,1)S(1)}, bf16[128,1024]{1,0:T(8,128)(2,1)S(1)}, u32[]{:S(2)}, u32[]{:S(2)}) collective-permute-start(bf16[128,1024]{1,0:T(8,128)(2,1)S(1)} %get-tuple-element.104), channel_id=1, source_target_pairs={{0,2},{6,4},{1,3},{7,5},{8,10},{14,12},{9,11},{15,13},{16,18},{22,... | collective-permute-start | bytes 786440 | tf_op jit(solution)/shard_map/ppermute | solution.py:660
  193.9 15.4 %collective-permute-start.26 = (bf16[128,1024]{1,0:T(8,128)(2,1)S(1)}, bf16[128,1024]{1,0:T(8,128)(2,1)S(1)}, u32[]{:S(2)}, u32[]{:S(2)}) collective-permute-start(bf16[128,1024]{1,0:T(8,128)(2,1)S(1)} %get-tuple-element.107), channel_id=1, source_target_pairs={{0,2},{6,4},{1,3},{7,5},{8,10},{14,12},{9,11},{15,13},{16,18},{22,... | collective-permute-start | bytes 786440 | tf_op jit(solution)/shard_map/ppermute | solution.py:660
  203.7 10.3 %collective-permute-start.24 = (bf16[128,1024]{1,0:T(8,128)(2,1)S(1)}, bf16[128,1024]{1,0:T(8,128)(2,1)S(1)}, u32[]{:S(2)}, u32[]{:S(2)}) collective-permute-start(bf16[128,1024]{1,0:T(8,128)(2,1)S(1)} %get-tuple-element.106), channel_id=1, source_target_pairs={{0,2},{6,4},{1,3},{7,5},{8,10},{14,12},{9,11},{15,13},{16,18},{22,... | collective-permute-start | bytes 786440 | tf_op jit(solution)/shard_map/ppermute | solution.py:660
  205.0 12.0 %collective-permute-start.29 = (bf16[128,1024]{1,0:T(8,128)(2,1)S(1)}, bf16[128,1024]{1,0:T(8,128)(2,1)S(1)}, u32[]{:S(2)}, u32[]{:S(2)}) collective-permute-start(bf16[128,1024]{1,0:T(8,128)(2,1)S(1)} %add_convert_fusion.1), channel_id=1, source_target_pairs={{2,4},{4,2},{3,5},{5,3},{10,12},{12,10},{11,13},{13,11},{18,20},{2... | collective-permute-start | bytes 786440 | tf_op jit(solution)/shard_map/ppermute | solution.py:660
  209.4 10.8 %collective-permute-start.27 = (bf16[128,1024]{1,0:T(8,128)(2,1)S(1)}, bf16[128,1024]{1,0:T(8,128)(2,1)S(1)}, u32[]{:S(2)}, u32[]{:S(2)}) collective-permute-start(bf16[128,1024]{1,0:T(8,128)(2,1)S(1)} %add_convert_fusion.2), channel_id=1, source_target_pairs={{2,4},{4,2},{3,5},{5,3},{10,12},{12,10},{11,13},{13,11},{18,20},{2... | collective-permute-start | bytes 786440 | tf_op jit(solution)/shard_map/ppermute | solution.py:660
  212.3 9.1 %collective-permute-start.22 = (bf16[128,1024]{1,0:T(8,128)(2,1)S(1)}, bf16[128,1024]{1,0:T(8,128)(2,1)S(1)}, u32[]{:S(2)}, u32[]{:S(2)}) collective-permute-start(bf16[128,1024]{1,0:T(8,128)(2,1)S(1)} %get-tuple-element.105), channel_id=1, source_target_pairs={{0,2},{6,4},{1,3},{7,5},{8,10},{14,12},{9,11},{15,13},{16,18},{22,... | collective-permute-start | bytes 786440 | tf_op jit(solution)/shard_map/ppermute | solution.py:660
  214.0 14.8 %collective-permute-start.25 = (bf16[128,1024]{1,0:T(8,128)(2,1)S(1)}, bf16[128,1024]{1,0:T(8,128)(2,1)S(1)}, u32[]{:S(2)}, u32[]{:S(2)}) collective-permute-start(bf16[128,1024]{1,0:T(8,128)(2,1)S(1)} %add_convert_fusion.3), channel_id=1, source_target_pairs={{2,4},{4,2},{3,5},{5,3},{10,12},{12,10},{11,13},{13,11},{18,20},{2... | collective-permute-start | bytes 786440 | tf_op jit(solution)/shard_map/ppermute | solution.py:660
  217.0 8.7 %collective-permute-start.30 = (bf16[128,1024]{1,0:T(8,128)(2,1)S(1)}, bf16[128,1024]{1,0:T(8,128)(2,1)S(1)}, u32[]{:S(2)}, u32[]{:S(2)}) collective-permute-start(bf16[128,1024]{1,0:T(8,128)(2,1)S(1)} %collective-permute-done.29), channel_id=1, source_target_pairs={{2,0},{4,6},{3,1},{5,7},{10,8},{12,14},{11,9},{13,15},{18,16},{20,... | collective-permute-start | bytes 786440 | tf_op jit(solution)/shard_map/ppermute | solution.py:660
  220.2 8.6 %collective-permute-start.28 = (bf16[128,1024]{1,0:T(8,128)(2,1)S(1)}, bf16[128,1024]{1,0:T(8,128)(2,1)S(1)}, u32[]{:S(2)}, u32[]{:S(2)}) collective-permute-start(bf16[128,1024]{1,0:T(8,128)(2,1)S(1)} %collective-permute-done.27), channel_id=1, source_target_pairs={{2,0},{4,6},{3,1},{5,7},{10,8},{12,14},{11,9},{13,15},{18,16},{20,... | collective-permute-start | bytes 786440 | tf_op jit(solution)/shard_map/ppermute | solution.py:660
  221.6 8.6 %collective-permute-start.23 = (bf16[128,1024]{1,0:T(8,128)(2,1)S(1)}, bf16[128,1024]{1,0:T(8,128)(2,1)S(1)}, u32[]{:S(2)}, u32[]{:S(2)}) collective-permute-start(bf16[128,1024]{1,0:T(8,128)(2,1)S(1)} %add_convert_fusion.4), channel_id=1, source_target_pairs={{2,4},{4,2},{3,5},{5,3},{10,12},{12,10},{11,13},{13,11},{18,20},{2... | collective-permute-start | bytes 786440 | tf_op jit(solution)/shard_map/ppermute | solution.py:660
  (20 other events, 161.8 us)

commit v5 on v4

--- a/solution.py
+++ b/solution.py
@@ -67,7 +67,7 @@
     block_ref[entry_width:, :rows] = facts_ref[...]
 
 
-def attend(nope_ref, rotated_ref, up_ref, facts_ref, marks_ref, keys_ref, score_scale):
+def attend(nope_ref, rotated_ref, up_ref, facts_ref, marks_ref, keys_ref, values_ref, score_scale):
     latent_width = up_ref.shape[0]
     head_width = NOPE + VD
     keys_latent = keys_ref[:latent_width, :]
@@ -81,11 +81,14 @@
         heads = range(group * PAIR, (group + 1) * PAIR)
         query_latent = jnp.concatenate(
             [
-                lax.dot_general(
-                    nope_ref[:, i * NOPE : (i + 1) * NOPE],
-                    up_ref[:, i * head_width : i * head_width + NOPE],
-                    (((1,), (1,)), ((), ())),
-                    preferred_element_type=jnp.float32,
+                (
+                    lax.dot_general(
+                        nope_ref[:, i * NOPE : (i + 1) * NOPE],
+                        up_ref[:, i * head_width : i * head_width + NOPE],
+                        (((1,), (1,)), ((), ())),
+                        preferred_element_type=jnp.float32,
+                    )
+                    * score_scale
                 ).astype(jnp.bfloat16)
                 for i in heads
             ],
@@ -98,19 +101,16 @@
     results = []
     for group in range(GROUPS):
         highest = jnp.max(scores[group], axis=1, keepdims=True)
-        soft = jnp.exp((scores[group] - highest) * score_scale)
+        soft = jnp.exp2(scores[group] - highest)
         totals = jnp.sum(soft, axis=1, keepdims=True)
-        mixed = lax.dot_general(
-            soft.astype(jnp.bfloat16),
-            keys_latent,
-            (((1,), (1,)), ((), ())),
-            preferred_element_type=jnp.float32,
+        mixed = jnp.dot(
+            soft.astype(jnp.bfloat16), values_ref[...], preferred_element_type=jnp.float32
         )
         results.append((highest, totals, mixed))
     return results
 
 
-def fill_keys(facts_ref, block_refs, keys_ref, marks_ref, first_slot, y_count, rows):
+def fill_keys(facts_ref, block_refs, keys_ref, values_ref, marks_ref, first_slot, y_count, rows):
     width = block_refs[0].shape[1]
     length, z_index, y_index = facts_ref[0], facts_ref[1], facts_ref[2]
     low = z_index < 2
@@ -118,6 +118,7 @@
     page_size = width - rows
     for index, block_ref in enumerate(block_refs):
         keys_ref[:, index * width : (index + 1) * width] = block_ref[: keys_ref.shape[0], :]
+        values_ref[index * width : (index + 1) * width, :] = block_ref[: values_ref.shape[1], :].T
         slot = first_slot + index // y_count
         z_source = (
             z_index,
@@ -139,27 +140,36 @@
         )
 
 
-def merged(result, group, old_refs, score_scale):
+def merged(result, group, old_refs):
     highest, totals, mixed = result
     old_highest, old_totals, old_mixed = [ref[group] for ref in old_refs]
     top = jnp.maximum(highest, old_highest)
-    fresh = jnp.exp((highest - top) * score_scale)
-    fading = jnp.exp((old_highest - top) * score_scale)
+    fresh = jnp.exp2(highest - top)
+    fading = jnp.exp2(old_highest - top)
     return top, totals * fresh + old_totals * fading, mixed * fresh + old_mixed * fading
 
 
 def first_attention_kernel(score_scale, first_slot, y_count, block_count, *refs):
     facts_ref, nope_ref, rotated_ref, up_ref = refs[:4]
     block_refs = refs[4 : 4 + block_count]
-    highest_ref, totals_ref, mixed_ref, keys_ref, marks_ref = refs[-5:]
+    highest_ref, totals_ref, mixed_ref, keys_ref, values_ref, marks_ref = refs[-6:]
 
     @pl.when(pl.program_id(0) == 0)
     def _():
         fill_keys(
-            facts_ref, block_refs, keys_ref, marks_ref, first_slot, y_count, nope_ref.shape[0]
+            facts_ref,
+            block_refs,
+            keys_ref,
+            values_ref,
+            marks_ref,
+            first_slot,
+            y_count,
+            nope_ref.shape[0],
         )
 
-    results = attend(nope_ref, rotated_ref, up_ref, facts_ref, marks_ref, keys_ref, score_scale)
+    results = attend(
+        nope_ref, rotated_ref, up_ref, facts_ref, marks_ref, keys_ref, values_ref, score_scale
+    )
     for group, (highest, totals, mixed) in enumerate(results):
         highest_ref[group] = highest
         totals_ref[group] = totals
@@ -171,19 +181,25 @@
     block_refs = refs[4 : 4 + block_count]
     old_refs = refs[4 + block_count : 7 + block_count]
     proj_ref, hidden_ref, gain_ref = refs[7 + block_count : 10 + block_count]
-    residual_ref, left_ref, right_ref, keys_ref, marks_ref, total_ref = refs[10 + block_count :]
+    residual_ref, left_ref, right_ref, keys_ref, values_ref, marks_ref, total_ref = refs[
+        10 + block_count :
+    ]
     step = pl.program_id(0)
     rows = hidden_ref.shape[0]
     head_width = NOPE + VD
 
     @pl.when(step == 0)
     def _():
-        fill_keys(facts_ref, block_refs, keys_ref, marks_ref, first_slot, y_count, rows)
-
-    results = attend(nope_ref, rotated_ref, up_ref, facts_ref, marks_ref, keys_ref, score_scale)
+        fill_keys(
+            facts_ref, block_refs, keys_ref, values_ref, marks_ref, first_slot, y_count, rows
+        )
+
+    results = attend(
+        nope_ref, rotated_ref, up_ref, facts_ref, marks_ref, keys_ref, values_ref, score_scale
+    )
     outs = []
     for group, result in enumerate(results):
-        _, totals, mixed = merged(result, group, old_refs, score_scale)
+        _, totals, mixed = merged(result, group, old_refs)
         mixed = (mixed / totals).astype(jnp.bfloat16)
         for i in range(PAIR):
             head = group * PAIR + i
@@ -239,6 +255,7 @@
     ] + [whole(block_height, width)] * len(blocks)
     scratch = [
         pltpu.VMEM((latent_width + rotary_width, keys), jnp.bfloat16),
+        pltpu.VMEM((keys, latent_width), jnp.bfloat16),
         pltpu.VMEM((1, keys), jnp.int32),
     ]
     aliases = {}
@@ -495,7 +512,7 @@
     entry_width = fresh_latent.shape[2]
     rotary_width = entry_width - latent_width
     half_rotary = rotary_width // 2
-    score_scale = 1.0 / math.sqrt(NOPE + rotary_width)
+    score_scale = math.log2(math.e) / math.sqrt(NOPE + rotary_width)
     length = cache_lengths[0]
     y_count = lax.axis_size("y")
     z_index = lax.axis_index("z")
@@ -558,10 +575,10 @@
     turning = query_rows[:, :, NOPE:].astype(jnp.float32).transpose(1, 0, 2)
     front, back = turning[:, :, :half_rotary], turning[:, :, half_rotary:]
     token_cosine, token_sine = cosine.T[None], sine.T[None]
-    rotated = jnp.concatenate(
+    rotated = (score_scale * jnp.concatenate(
         [front * token_cosine - back * token_sine, back * token_cosine + front * token_sine],
         axis=2,
-    ).astype(jnp.bfloat16)
+    )).astype(jnp.bfloat16)
 
     places = jnp.stack(
         [length, z_index.astype(jnp.int32), y_index.astype(jnp.int32), jnp.int32(y_count)]

time: 235 us -> 235 us (level)
  no operation moved by 1% of the time
where the time goes in v5:
time: 235 us; the launch traced here: 231 us
  starting transfers between devices  73.5 us (31%)
  Pallas kernels  70.5 us (30%)
  waiting for transfers between devices  62.3 us (27%)
  local copies, waits for them, and re-layouts  15.2 us (6%)
  other arithmetic  5.32 us (2%)
  matrix products  2.68 us (1%)
    pallas_call x2, Pallas kernels, experts(): pl.pallas_call(functools.partial(experts_kernel, slabs_each, sorting), gr...  39.1 us
    ppermute x12, waiting for transfers between devices, moved(): return lax.ppermute(value, 'z', pairs)  28.6 us
    ppermute x12, starting transfers between devices, moved(): return lax.ppermute(value, 'z', pairs)  22.5 us
    pallas_call x3, Pallas kernels, attention_call(): pl.pallas_call(functools.partial(kernel, score_scale, first_slot, y_count...  22.1 us
    all_to_all x4, starting transfers between devices, exchanged(): lax.all_to_all(values, PLANE_AXES, split_axis=0, concat_axis=0, tiled=True)  15.3 us
    unnamed x37, local copies, waits for them, and re-layouts  11.6 us
    ppermute x3, starting transfers between devices, along_z(): middle = lax.ppermute(values, 'z', MIDDLE)  10.4 us
    all_to_all x4, waiting for transfers between devices, exchanged(): lax.all_to_all(values, PLANE_AXES, split_axis=0, concat_axis=0, tiled=True)  10.2 us
  transfers between devices with their start and end apart: 35, of which 24 were waited for; matrix products, arithmetic and copies ran while one was open for 5% of the time, Pallas kernels for 21%

profile of v5, /device:TPU:8, one launch (start us, length us, event | category | flops | bytes accessed | tf_op | source)
XLA Modules:
  0.0 231.4 jit_solution(10417173146252498797)
XLA Ops:
  8.1 4.6 %collective-permute-start = (bf16[592,256]{1,0:T(8,128)(2,1)}, bf16[592,256]{1,0:T(8,128)(2,1)S(1)}, u32[]{:S(2)}, u32[]{:S(2)}) collective-permute-start(bf16[592,256]{1,0:T(8,128)(2,1)} %get-tuple-element.56.refs_4_), channel_id=1, source_target_pairs={{2,4},{4,2},{3,5},{5,3},{10,12},{12,10},{11,13},{13,11},{18,20},{2... | collective-permute-start | bytes 909320 | tf_op jit(solution)/shard_map/ppermute | solution.py:559
  15.9 2.9 %collective-permute-start.6 = (bf16[592,256]{1,0:T(8,128)(2,1)S(1)}, bf16[592,256]{1,0:T(8,128)(2,1)}, u32[]{:S(2)}, u32[]{:S(2)}) collective-permute-start(bf16[592,256]{1,0:T(8,128)(2,1)S(1)} %collective-permute-done.4.refs_6_), channel_id=1, source_target_pairs={{2,4},{4,2},{3,5},{5,3},{10,12},{12,10},{11,13},{13,11},{18,20},{2... | collective-permute-start | bytes 909320 | tf_op jit(solution)/shard_map/ppermute | solution.py:560
  30.2 2.2 copy-done
  32.4 4.9 %shard_map.150 = (f32[8,256,1]{2,1,0:T(8,128)S(1)}, f32[8,256,1]{2,1,0:T(8,128)S(1)}, f32[8,256,512]{2,1,0:T(8,128)S(1)}) custom-call(s32[12]{0:T(128)S(1)} %concatenate.25.refs_0_, bf16[128,2048]{1,0:T(8,128)(2,1)S(1)} %copy.59.refs_1_, bf16[16,128,64]{2,1,0:T(8,128)(2,1)S(1)} %fusion.8.refs_2_, bf16[512,4096]{1,0:T(8,128)(2,1)S(1)} %copy-done, ...), custom_call_target="tpu_custom_call" | custom-call | flops 2281701376 | bytes 8388608 | tf_op jit(solution)/shard_map/pallas_call | solution.py:290
  39.5 4.9 %shard_map.151 = (f32[8,256,1]{2,1,0:T(8,128)S(1)}, f32[8,256,1]{2,1,0:T(8,128)S(1)}, f32[8,256,512]{2,1,0:T(8,128)S(1)}) custom-call(s32[12]{0:T(128)S(1)} %concatenate.25.refs_0_, bf16[128,2048]{1,0:T(8,128)(2,1)S(1)} %copy.59.refs_1_, bf16[16,128,64]{2,1,0:T(8,128)(2,1)S(1)} %fusion.8.refs_2_, ...), custom_call_target="tpu_custom_call", output_to_operand_aliasing={{0}: (8, {}), {1}: (9, {}), {2}: (10, {})} | custom-call | flops 2281701376 | bytes 8388608 | tf_op jit(solution)/shard_map/pallas_call | solution.py:290
  45.2 12.3 %shard_map.152 = (f32[128,2048]{1,0:T(8,128)S(1)}, bf16[128,1024]{1,0:T(8,128)(2,1)S(1)}, bf16[128,1024]{1,0:T(8,128)(2,1)S(1)}) custom-call(s32[12]{0:T(128)S(1)} %concatenate.25.refs_0_, bf16[128,2048]{1,0:T(8,128)(2,1)S(1)} %copy.59.refs_1_, bf16[16,128,64]{2,1,0:T(8,128)(2,1)S(1)} %fusion.8.refs_2_, bf16[512,4096]{1,0:T(8,128)(2,1)S(1)} %copy-done.1, ...), custom_call_target="tpu_custom_call" | custom-call | flops 4563402752 | bytes 16777216 | tf_op jit(solution)/shard_map/pallas_call | solution.py:290
  58.5 2.8 %collective-permute-start.11 = (bf16[128,1024]{1,0:T(8,128)(2,1)S(1)}, bf16[128,1024]{1,0:T(8,128)(2,1)S(1)}, u32[]{:S(2)}, u32[]{:S(2)}) collective-permute-start(bf16[128,1024]{1,0:T(8,128)(2,1)S(1)} %get-tuple-element.73.refs_0_), channel_id=1, source_target_pairs={{2,4},{4,2},{3,5},{5,3},{10,12},{12,10},{11,13},{13,11},{18,20},{2... | collective-permute-start | bytes 786440 | tf_op jit(solution)/shard_map/ppermute | solution.py:559
  63.7 3.0 %collective-permute-start.12 = (bf16[128,1024]{1,0:T(8,128)(2,1)S(1)}, bf16[128,1024]{1,0:T(8,128)(2,1)S(1)}, u32[]{:S(2)}, u32[]{:S(2)}) collective-permute-start(bf16[128,1024]{1,0:T(8,128)(2,1)S(1)} %get-tuple-element.74.refs_1_), channel_id=1, source_target_pairs={{2,4},{4,2},{3,5},{5,3},{10,12},{12,10},{11,13},{13,11},{18,20},{2... | collective-permute-start | bytes 786440 | tf_op jit(solution)/shard_map/ppermute | solution.py:559
  66.7 2.7 %collective-permute-done.11.refs_0_ = bf16[128,1024]{1,0:T(8,128)(2,1)S(1)} collective-permute-done((bf16[128,1024]{1,0:T(8,128)(2,1)S(1)}, bf16[128,1024]{1,0:T(8,128)(2,1)S(1)}, u32[]{:S(2)}, u32[]{:S(2)}) %collective-permute-start.11) | collective-permute-done | bytes 262176 | tf_op jit(solution)/shard_map/ppermute | solution.py:559
  70.7 3.1 %collective-permute-start.14 = (bf16[128,1024]{1,0:T(8,128)(2,1)S(1)}, bf16[128,1024]{1,0:T(8,128)(2,1)S(1)}, u32[]{:S(2)}, u32[]{:S(2)}) collective-permute-start(bf16[128,1024]{1,0:T(8,128)(2,1)S(1)} %collective-permute-done.9.refs_2_), channel_id=1, source_target_pairs={{2,4},{4,2},{3,5},{5,3},{10,12},{12,10},{11,13},{13,11},{18,20},{2... | collective-permute-start | bytes 786440 | tf_op jit(solution)/shard_map/ppermute | solution.py:560
  75.2 3.7 %collective-permute-done.14.refs_4_ = bf16[128,1024]{1,0:T(8,128)(2,1)S(1)} collective-permute-done((bf16[128,1024]{1,0:T(8,128)(2,1)S(1)}, bf16[128,1024]{1,0:T(8,128)(2,1)S(1)}, u32[]{:S(2)}, u32[]{:S(2)}) %collective-permute-start.14) | collective-permute-done | bytes 262176 | tf_op jit(solution)/shard_map/ppermute | solution.py:560
  80.9 3.6 %all-to-all-start = ((bf16[8,56,2048]{2,1,0:T(8,128)(2,1)}), bf16[8,56,2048]{2,1,0:T(8,128)(2,1)S(1)}, u32[]{:S(2)}, u32[]{:S(2)}) async-start(bf16[8,56,2048]{2,1,0:T(8,128)(2,1)} %bitcast.19), calls=%async_computation | async-start | bytes 3670016 | tf_op jit(solution)/shard_map/all_to_all | solution.py:647
  84.5 3.0 %collective-permute-start.16 = (bf16[128,1024]{1,0:T(8,128)(2,1)S(1)}, bf16[128,1024]{1,0:T(8,128)(2,1)}, u32[]{:S(2)}, u32[]{:S(2)}) collective-permute-start(bf16[128,1024]{1,0:T(8,128)(2,1)S(1)} %collective-permute-done.10.refs_3_), channel_id=1, source_target_pairs={{2,4},{4,2},{3,5},{5,3},{10,12},{12,10},{11,13},{13,11},{18,20},{2... | collective-permute-start | bytes 786440 | tf_op jit(solution)/shard_map/ppermute | solution.py:560
  91.5 3.6 %collective-permute-done.16.refs_5_ = bf16[128,1024]{1,0:T(8,128)(2,1)} collective-permute-done((bf16[128,1024]{1,0:T(8,128)(2,1)S(1)}, bf16[128,1024]{1,0:T(8,128)(2,1)}, u32[]{:S(2)}, u32[]{:S(2)}) %collective-permute-start.16) | collective-permute-done | bytes 262176 | tf_op jit(solution)/shard_map/ppermute | solution.py:560
  98.7 2.3 %collective-permute-done.17.refs_6_ = bf16[128,1024]{1,0:T(8,128)(2,1)} collective-permute-done((bf16[128,1024]{1,0:T(8,128)(2,1)S(1)}, bf16[128,1024]{1,0:T(8,128)(2,1)}, u32[]{:S(2)}, u32[]{:S(2)}) %collective-permute-start.17) | collective-permute-done | bytes 262176 | tf_op jit(solution)/shard_map/ppermute | solution.py:562
  101.1 5.3 %collective-permute-done.18.refs_7_ = bf16[128,1024]{1,0:T(8,128)(2,1)S(1)} collective-permute-done((bf16[128,1024]{1,0:T(8,128)(2,1)}, bf16[128,1024]{1,0:T(8,128)(2,1)S(1)}, u32[]{:S(2)}, u32[]{:S(2)}) %collective-permute-start.18) | collective-permute-done | bytes 262176 | tf_op jit(solution)/shard_map/ppermute | solution.py:562
  107.4 3.0 %shard_map.155 = bf16[448,2048]{1,0:T(8,128)(2,1)} custom-call(bf16[448,256]{1,0:T(8,128)(2,1)S(1)} %copy.66.place_ref, bf16[128,1024]{1,0:T(8,128)(2,1)S(1)} %collective-permute-done.11.refs_0_, bf16[128,1024]{1,0:T(8,128)(2,1)S(1)} %collective-permute-done.12.refs_1_, bf16[128,1024]{1,0:T(8,128)(2,1)S(1)} %collective-permute-done.13.refs_2_, ...), custom_call_target="tpu_custom_call" | custom-call | flops 469762048 | bytes 5505024 | tf_op jit(solution)/shard_map/pallas_call | solution.py:447
  110.4 4.3 %all-to-all-start.1 = ((bf16[8,56,2048]{2,1,0:T(8,128)(2,1)}), bf16[8,56,2048]{2,1,0:T(8,128)(2,1)}, u32[]{:S(2)}, u32[]{:S(2)}) async-start(bf16[8,56,2048]{2,1,0:T(8,128)(2,1)} %bitcast.21), calls=%async_computation.1 | async-start | bytes 3670016 | tf_op jit(solution)/shard_map/all_to_all | solution.py:647
  115.0 18.2 %shard_map.154 = bf16[448,2048]{1,0:T(8,128)(2,1)S(1)} custom-call(bf16[448,2048]{1,0:T(8,128)(2,1)S(1)} %bitcast.51, bf16[2,224,448]{2,1,0:T(8,128)(2,1)S(1)} %fusion.9.refs_0_, bf16[2,448,224]{2,1,0:T(8,128)(2,1)S(1)} %fusion.10.refs_1_, bf16[4,2048,1408]{2,1,0:T(8,128)(2,1)} %refs_3_.9, bf16[4,2048,1408]{2,1,0:T(8,128)(2,1)} %refs_3_.9, ...), custom_call_target="tpu_custom_call" | custom-call | flops 7751073792 | bytes 34603008 | tf_op jit(solution)/shard_map/pallas_call | solution.py:405
  134.5 3.2 %all-to-all-done.1 = bf16[8,56,2048]{2,1,0:T(8,128)(2,1)} async-done(((bf16[8,56,2048]{2,1,0:T(8,128)(2,1)}), bf16[8,56,2048]{2,1,0:T(8,128)(2,1)}, u32[]{:S(2)}, u32[]{:S(2)}) %all-to-all-start.1) | async-done | bytes 1835040 | tf_op jit(solution)/shard_map/all_to_all | solution.py:647
  137.7 3.6 %all-to-all-start.2 = ((bf16[8,56,2048]{2,1,0:T(8,128)(2,1)}), bf16[8,56,2048]{2,1,0:T(8,128)(2,1)S(1)}, u32[]{:S(2)}, u32[]{:S(2)}) async-start(bf16[8,56,2048]{2,1,0:T(8,128)(2,1)} %bitcast.53), calls=%async_computation.2 | async-start | bytes 3670016 | tf_op jit(solution)/shard_map/all_to_all | solution.py:647
  141.3 20.9 %shard_map.156 = bf16[448,2048]{1,0:T(8,128)(2,1)S(1)} custom-call(bf16[448,2048]{1,0:T(8,128)(2,1)} %bitcast.22.x_ref, bf16[2,224,448]{2,1,0:T(8,128)(2,1)S(1)} %fusion.9.refs_0_, bf16[2,448,224]{2,1,0:T(8,128)(2,1)S(1)} %fusion.10.refs_1_, bf16[4,2048,1408]{2,1,0:T(8,128)(2,1)} %refs_3_.9, bf16[4,2048,1408]{2,1,0:T(8,128)(2,1)} %refs_3_.9, ...), custom_call_target="tpu_custom_call" | custom-call | flops 7751073792 | bytes 34603008 | tf_op jit(solution)/shard_map/pallas_call | solution.py:405
  165.4 3.8 %all-to-all-start.3 = ((bf16[8,56,2048]{2,1,0:T(8,128)(2,1)}), bf16[8,56,2048]{2,1,0:T(8,128)(2,1)S(1)}, u32[]{:S(2)}, u32[]{:S(2)}) async-start(bf16[8,56,2048]{2,1,0:T(8,128)(2,1)} %bitcast.52), calls=%async_computation.3 | async-start | bytes 3670016 | tf_op jit(solution)/shard_map/all_to_all | solution.py:647
  174.3 6.8 %collective-permute-done.19.refs_0_ = bf16[128,1024]{1,0:T(8,128)(2,1)S(1)} collective-permute-done((bf16[128,1024]{1,0:T(8,128)(2,1)S(1)}, bf16[128,1024]{1,0:T(8,128)(2,1)S(1)}, u32[]{:S(2)}, u32[]{:S(2)}) %collective-permute-start.19) | collective-permute-done | bytes 262176 | tf_op jit(solution)/shard_map/ppermute | solution.py:677
  181.1 4.9 %collective-permute-done.20.refs_1_ = bf16[128,1024]{1,0:T(8,128)(2,1)S(1)} collective-permute-done((bf16[128,1024]{1,0:T(8,128)(2,1)S(1)}, bf16[128,1024]{1,0:T(8,128)(2,1)S(1)}, u32[]{:S(2)}, u32[]{:S(2)}) %collective-permute-start.20) | collective-permute-done | bytes 262176 | tf_op jit(solution)/shard_map/ppermute | solution.py:677
  186.7 5.3 %all-to-all-done.3 = bf16[8,56,2048]{2,1,0:T(8,128)(2,1)S(1)} async-done(((bf16[8,56,2048]{2,1,0:T(8,128)(2,1)}), bf16[8,56,2048]{2,1,0:T(8,128)(2,1)S(1)}, u32[]{:S(2)}, u32[]{:S(2)}) %all-to-all-start.3) | async-done | bytes 1835040 | tf_op jit(solution)/shard_map/all_to_all | solution.py:647
  195.4 8.5 %collective-permute-done.21 = bf16[128,1024]{1,0:T(8,128)(2,1)S(1)} collective-permute-done((bf16[128,1024]{1,0:T(8,128)(2,1)S(1)}, bf16[128,1024]{1,0:T(8,128)(2,1)S(1)}, u32[]{:S(2)}, u32[]{:S(2)}) %collective-permute-start.21) | collective-permute-done | bytes 262176 | tf_op jit(solution)/shard_map/ppermute | solution.py:677
  205.2 3.0 %collective-permute-start.29 = (bf16[128,1024]{1,0:T(8,128)(2,1)S(1)}, bf16[128,1024]{1,0:T(8,128)(2,1)S(1)}, u32[]{:S(2)}, u32[]{:S(2)}) collective-permute-start(bf16[128,1024]{1,0:T(8,128)(2,1)S(1)} %add_convert_fusion), channel_id=1, source_target_pairs={{2,4},{4,2},{3,5},{5,3},{10,12},{12,10},{11,13},{13,11},{18,20},{2... | collective-permute-start | bytes 786440 | tf_op jit(solution)/shard_map/ppermute | solution.py:677
  209.5 3.0 %collective-permute-start.27 = (bf16[128,1024]{1,0:T(8,128)(2,1)S(1)}, bf16[128,1024]{1,0:T(8,128)(2,1)S(1)}, u32[]{:S(2)}, u32[]{:S(2)}) collective-permute-start(bf16[128,1024]{1,0:T(8,128)(2,1)S(1)} %add_convert_fusion.1), channel_id=1, source_target_pairs={{2,4},{4,2},{3,5},{5,3},{10,12},{12,10},{11,13},{13,11},{18,20},{2... | collective-permute-start | bytes 786440 | tf_op jit(solution)/shard_map/ppermute | solution.py:677
  214.2 3.0 %collective-permute-start.25 = (bf16[128,1024]{1,0:T(8,128)(2,1)S(1)}, bf16[128,1024]{1,0:T(8,128)(2,1)S(1)}, u32[]{:S(2)}, u32[]{:S(2)}) collective-permute-start(bf16[128,1024]{1,0:T(8,128)(2,1)S(1)} %add_convert_fusion.2), channel_id=1, source_target_pairs={{2,4},{4,2},{3,5},{5,3},{10,12},{12,10},{11,13},{13,11},{18,20},{2... | collective-permute-start | bytes 786440 | tf_op jit(solution)/shard_map/ppermute | solution.py:677
  221.8 3.0 %collective-permute-start.23 = (bf16[128,1024]{1,0:T(8,128)(2,1)S(1)}, bf16[128,1024]{1,0:T(8,128)(2,1)S(1)}, u32[]{:S(2)}, u32[]{:S(2)}) collective-permute-start(bf16[128,1024]{1,0:T(8,128)(2,1)S(1)} %add_convert_fusion.3), channel_id=1, source_target_pairs={{2,4},{4,2},{3,5},{5,3},{10,12},{12,10},{11,13},{13,11},{18,20},{2... | collective-permute-start | bytes 786440 | tf_op jit(solution)/shard_map/ppermute | solution.py:677
  225.9 3.0 %collective-permute-done.28.refs_4_ = bf16[128,1024]{1,0:T(8,128)(2,1)S(1)} collective-permute-done((bf16[128,1024]{1,0:T(8,128)(2,1)S(1)}, bf16[128,1024]{1,0:T(8,128)(2,1)S(1)}, u32[]{:S(2)}, u32[]{:S(2)}) %collective-permute-start.28) | collective-permute-done | bytes 262176 | tf_op jit(solution)/shard_map/ppermute | solution.py:677
  (134 shorter events, 67.4 us)
Async XLA Ops:
  6.1 9.7 %collective-permute-start.4 = (bf16[592,256]{1,0:T(8,128)(2,1)}, bf16[592,256]{1,0:T(8,128)(2,1)S(1)}, u32[]{:S(2)}, u32[]{:S(2)}) collective-permute-start(bf16[592,256]{1,0:T(8,128)(2,1)} %get-tuple-element.56.refs_4_), channel_id=1, source_target_pairs={{0,2},{2,0},{4,6},{6,4},{1,3},{3,1},{5,7},{7,5},{8,10},{10,8},{12,... | collective-permute-start | bytes 909320 | tf_op jit(solution)/shard_map/ppermute | solution.py:558
  6.1 22.1 %collective-permute-start.3 = (bf16[592,256]{1,0:T(8,128)(2,1)}, bf16[592,256]{1,0:T(8,128)(2,1)S(1)}, u32[]{:S(2)}, u32[]{:S(2)}) collective-permute-start(bf16[592,256]{1,0:T(8,128)(2,1)} %get-tuple-element.56.refs_4_), channel_id=1, source_target_pairs={{0,1},{1,0},{2,3},{3,2},{4,5},{5,4},{6,7},{7,6},{8,9},{9,8},{10,11... | collective-permute-start | bytes 909320 | tf_op jit(solution)/shard_map/ppermute | solution.py:35
  8.1 11.7 %collective-permute-start = (bf16[592,256]{1,0:T(8,128)(2,1)}, bf16[592,256]{1,0:T(8,128)(2,1)S(1)}, u32[]{:S(2)}, u32[]{:S(2)}) collective-permute-start(bf16[592,256]{1,0:T(8,128)(2,1)} %get-tuple-element.56.refs_4_), channel_id=1, source_target_pairs={{2,4},{4,2},{3,5},{5,3},{10,12},{12,10},{11,13},{13,11},{18,20},{2... | collective-permute-start | bytes 909320 | tf_op jit(solution)/shard_map/ppermute | solution.py:559
  15.9 10.2 %collective-permute-start.6 = (bf16[592,256]{1,0:T(8,128)(2,1)S(1)}, bf16[592,256]{1,0:T(8,128)(2,1)}, u32[]{:S(2)}, u32[]{:S(2)}) collective-permute-start(bf16[592,256]{1,0:T(8,128)(2,1)S(1)} %collective-permute-done.4.refs_6_), channel_id=1, source_target_pairs={{2,4},{4,2},{3,5},{5,3},{10,12},{12,10},{11,13},{13,11},{18,20},{2... | collective-permute-start | bytes 909320 | tf_op jit(solution)/shard_map/ppermute | solution.py:560
  21.9 8.3 %collective-permute-start.5 = (bf16[592,256]{1,0:T(8,128)(2,1)S(1)}, bf16[592,256]{1,0:T(8,128)(2,1)S(1)}, u32[]{:S(2)}, u32[]{:S(2)}) collective-permute-start(bf16[592,256]{1,0:T(8,128)(2,1)S(1)} %collective-permute-done.4.refs_6_), channel_id=1, source_target_pairs={{0,1},{1,0},{2,3},{3,2},{4,5},{5,4},{6,7},{7,6},{8,9},{9,8},{10,11... | collective-permute-start | bytes 909320 | tf_op jit(solution)/shard_map/ppermute | solution.py:35
  26.1 11.2 %collective-permute-start.7 = (bf16[592,256]{1,0:T(8,128)(2,1)}, bf16[592,256]{1,0:T(8,128)(2,1)S(1)}, u32[]{:S(2)}, u32[]{:S(2)}) collective-permute-start(bf16[592,256]{1,0:T(8,128)(2,1)} %collective-permute-done.6), channel_id=1, source_target_pairs={{2,0},{4,6},{3,1},{5,7},{10,8},{12,14},{11,9},{13,15},{18,16},{20,... | collective-permute-start | bytes 909320 | tf_op jit(solution)/shard_map/ppermute | solution.py:562
  27.5 17.0 %collective-permute-start.2 = (bf16[592,256]{1,0:T(8,128)(2,1)S(1)}, bf16[592,256]{1,0:T(8,128)(2,1)S(1)}, u32[]{:S(2)}, u32[]{:S(2)}) collective-permute-start(bf16[592,256]{1,0:T(8,128)(2,1)S(1)} %broadcast_select_fusion.1.refs_4_), channel_id=1, source_target_pairs={{0,1},{1,0},{2,3},{3,2},{4,5},{5,4},{6,7},{7,6},{8,9},{9,8},{10,11... | collective-permute-start | bytes 909320 | tf_op jit(solution)/shard_map/ppermute | solution.py:35
  58.5 10.8 %collective-permute-start.11 = (bf16[128,1024]{1,0:T(8,128)(2,1)S(1)}, bf16[128,1024]{1,0:T(8,128)(2,1)S(1)}, u32[]{:S(2)}, u32[]{:S(2)}) collective-permute-start(bf16[128,1024]{1,0:T(8,128)(2,1)S(1)} %get-tuple-element.73.refs_0_), channel_id=1, source_target_pairs={{2,4},{4,2},{3,5},{5,3},{10,12},{12,10},{11,13},{13,11},{18,20},{2... | collective-permute-start | bytes 786440 | tf_op jit(solution)/shard_map/ppermute | solution.py:559
  61.3 9.3 %collective-permute-start.9 = (bf16[128,1024]{1,0:T(8,128)(2,1)S(1)}, bf16[128,1024]{1,0:T(8,128)(2,1)S(1)}, u32[]{:S(2)}, u32[]{:S(2)}) collective-permute-start(bf16[128,1024]{1,0:T(8,128)(2,1)S(1)} %get-tuple-element.73.refs_0_), channel_id=1, source_target_pairs={{0,2},{2,0},{4,6},{6,4},{1,3},{3,1},{5,7},{7,5},{8,10},{10,8},{12,... | collective-permute-start | bytes 786440 | tf_op jit(solution)/shard_map/ppermute | solution.py:558
  61.7 12.8 %collective-permute-start.10 = (bf16[128,1024]{1,0:T(8,128)(2,1)S(1)}, bf16[128,1024]{1,0:T(8,128)(2,1)S(1)}, u32[]{:S(2)}, u32[]{:S(2)}) collective-permute-start(bf16[128,1024]{1,0:T(8,128)(2,1)S(1)} %get-tuple-element.74.refs_1_), channel_id=1, source_target_pairs={{0,2},{2,0},{4,6},{6,4},{1,3},{3,1},{5,7},{7,5},{8,10},{10,8},{12,... | collective-permute-start | bytes 786440 | tf_op jit(solution)/shard_map/ppermute | solution.py:558
  63.7 11.3 %collective-permute-start.12 = (bf16[128,1024]{1,0:T(8,128)(2,1)S(1)}, bf16[128,1024]{1,0:T(8,128)(2,1)S(1)}, u32[]{:S(2)}, u32[]{:S(2)}) collective-permute-start(bf16[128,1024]{1,0:T(8,128)(2,1)S(1)} %get-tuple-element.74.refs_1_), channel_id=1, source_target_pairs={{2,4},{4,2},{3,5},{5,3},{10,12},{12,10},{11,13},{13,11},{18,20},{2... | collective-permute-start | bytes 786440 | tf_op jit(solution)/shard_map/ppermute | solution.py:559
  70.7 8.3 %collective-permute-start.14 = (bf16[128,1024]{1,0:T(8,128)(2,1)S(1)}, bf16[128,1024]{1,0:T(8,128)(2,1)S(1)}, u32[]{:S(2)}, u32[]{:S(2)}) collective-permute-start(bf16[128,1024]{1,0:T(8,128)(2,1)S(1)} %collective-permute-done.9.refs_2_), channel_id=1, source_target_pairs={{2,4},{4,2},{3,5},{5,3},{10,12},{12,10},{11,13},{13,11},{18,20},{2... | collective-permute-start | bytes 786440 | tf_op jit(solution)/shard_map/ppermute | solution.py:560
  80.9 26.5 %all-to-all-start = ((bf16[8,56,2048]{2,1,0:T(8,128)(2,1)}), bf16[8,56,2048]{2,1,0:T(8,128)(2,1)S(1)}, u32[]{:S(2)}, u32[]{:S(2)}) async-start(bf16[8,56,2048]{2,1,0:T(8,128)(2,1)} %bitcast.19), calls=%async_computation | async-start | bytes 3670016 | tf_op jit(solution)/shard_map/all_to_all | solution.py:647
  84.5 10.6 %collective-permute-start.16 = (bf16[128,1024]{1,0:T(8,128)(2,1)S(1)}, bf16[128,1024]{1,0:T(8,128)(2,1)}, u32[]{:S(2)}, u32[]{:S(2)}) collective-permute-start(bf16[128,1024]{1,0:T(8,128)(2,1)S(1)} %collective-permute-done.10.refs_3_), channel_id=1, source_target_pairs={{2,4},{4,2},{3,5},{5,3},{10,12},{12,10},{11,13},{13,11},{18,20},{2... | collective-permute-start | bytes 786440 | tf_op jit(solution)/shard_map/ppermute | solution.py:560
  87.6 11.2 %collective-permute-start.15 = (bf16[128,1024]{1,0:T(8,128)(2,1)S(1)}, bf16[128,1024]{1,0:T(8,128)(2,1)}, u32[]{:S(2)}, u32[]{:S(2)}) collective-permute-start(bf16[128,1024]{1,0:T(8,128)(2,1)S(1)} %collective-permute-done.12.refs_1_), channel_id=1, source_target_pairs={{2,0},{4,6},{3,1},{5,7},{10,8},{12,14},{11,9},{13,15},{18,16},{20,... | collective-permute-start | bytes 786440 | tf_op jit(solution)/shard_map/ppermute | solution.py:561
  89.5 11.5 %collective-permute-start.17 = (bf16[128,1024]{1,0:T(8,128)(2,1)S(1)}, bf16[128,1024]{1,0:T(8,128)(2,1)}, u32[]{:S(2)}, u32[]{:S(2)}) collective-permute-start(bf16[128,1024]{1,0:T(8,128)(2,1)S(1)} %collective-permute-done.14.refs_4_), channel_id=1, source_target_pairs={{2,0},{4,6},{3,1},{5,7},{10,8},{12,14},{11,9},{13,15},{18,16},{20,... | collective-permute-start | bytes 786440 | tf_op jit(solution)/shard_map/ppermute | solution.py:562
  95.1 11.2 %collective-permute-start.18 = (bf16[128,1024]{1,0:T(8,128)(2,1)}, bf16[128,1024]{1,0:T(8,128)(2,1)S(1)}, u32[]{:S(2)}, u32[]{:S(2)}) collective-permute-start(bf16[128,1024]{1,0:T(8,128)(2,1)} %collective-permute-done.16.refs_5_), channel_id=1, source_target_pairs={{2,0},{4,6},{3,1},{5,7},{10,8},{12,14},{11,9},{13,15},{18,16},{20,... | collective-permute-start | bytes 786440 | tf_op jit(solution)/shard_map/ppermute | solution.py:562
  110.4 27.3 %all-to-all-start.1 = ((bf16[8,56,2048]{2,1,0:T(8,128)(2,1)}), bf16[8,56,2048]{2,1,0:T(8,128)(2,1)}, u32[]{:S(2)}, u32[]{:S(2)}) async-start(bf16[8,56,2048]{2,1,0:T(8,128)(2,1)} %bitcast.21), calls=%async_computation.1 | async-start | bytes 3670016 | tf_op jit(solution)/shard_map/all_to_all | solution.py:647
  137.7 26.5 %all-to-all-start.2 = ((bf16[8,56,2048]{2,1,0:T(8,128)(2,1)}), bf16[8,56,2048]{2,1,0:T(8,128)(2,1)S(1)}, u32[]{:S(2)}, u32[]{:S(2)}) async-start(bf16[8,56,2048]{2,1,0:T(8,128)(2,1)} %bitcast.53), calls=%async_computation.2 | async-start | bytes 3670016 | tf_op jit(solution)/shard_map/all_to_all | solution.py:647
  165.4 26.5 %all-to-all-start.3 = ((bf16[8,56,2048]{2,1,0:T(8,128)(2,1)}), bf16[8,56,2048]{2,1,0:T(8,128)(2,1)S(1)}, u32[]{:S(2)}, u32[]{:S(2)}) async-start(bf16[8,56,2048]{2,1,0:T(8,128)(2,1)} %bitcast.52), calls=%async_computation.3 | async-start | bytes 3670016 | tf_op jit(solution)/shard_map/all_to_all | solution.py:647
  171.9 9.2 %collective-permute-start.19 = (bf16[128,1024]{1,0:T(8,128)(2,1)S(1)}, bf16[128,1024]{1,0:T(8,128)(2,1)S(1)}, u32[]{:S(2)}, u32[]{:S(2)}) collective-permute-start(bf16[128,1024]{1,0:T(8,128)(2,1)S(1)} %get-tuple-element.96), channel_id=1, source_target_pairs={{0,2},{2,0},{4,6},{6,4},{1,3},{3,1},{5,7},{7,5},{8,10},{10,8},{12,... | collective-permute-start | bytes 786440 | tf_op jit(solution)/shard_map/ppermute | solution.py:677
  173.3 12.6 %collective-permute-start.20 = (bf16[128,1024]{1,0:T(8,128)(2,1)S(1)}, bf16[128,1024]{1,0:T(8,128)(2,1)S(1)}, u32[]{:S(2)}, u32[]{:S(2)}) collective-permute-start(bf16[128,1024]{1,0:T(8,128)(2,1)S(1)} %get-tuple-element.97), channel_id=1, source_target_pairs={{0,2},{2,0},{4,6},{6,4},{1,3},{3,1},{5,7},{7,5},{8,10},{10,8},{12,... | collective-permute-start | bytes 786440 | tf_op jit(solution)/shard_map/ppermute | solution.py:677
  192.7 11.2 %collective-permute-start.21 = (bf16[128,1024]{1,0:T(8,128)(2,1)S(1)}, bf16[128,1024]{1,0:T(8,128)(2,1)S(1)}, u32[]{:S(2)}, u32[]{:S(2)}) collective-permute-start(bf16[128,1024]{1,0:T(8,128)(2,1)S(1)} %get-tuple-element.104), channel_id=1, source_target_pairs={{0,2},{6,4},{1,3},{7,5},{8,10},{14,12},{9,11},{15,13},{16,18},{22,... | collective-permute-start | bytes 786440 | tf_op jit(solution)/shard_map/ppermute | solution.py:677
  194.1 15.4 %collective-permute-start.26 = (bf16[128,1024]{1,0:T(8,128)(2,1)S(1)}, bf16[128,1024]{1,0:T(8,128)(2,1)S(1)}, u32[]{:S(2)}, u32[]{:S(2)}) collective-permute-start(bf16[128,1024]{1,0:T(8,128)(2,1)S(1)} %get-tuple-element.107), channel_id=1, source_target_pairs={{0,2},{6,4},{1,3},{7,5},{8,10},{14,12},{9,11},{15,13},{16,18},{22,... | collective-permute-start | bytes 786440 | tf_op jit(solution)/shard_map/ppermute | solution.py:677
  203.9 10.3 %collective-permute-start.24 = (bf16[128,1024]{1,0:T(8,128)(2,1)S(1)}, bf16[128,1024]{1,0:T(8,128)(2,1)S(1)}, u32[]{:S(2)}, u32[]{:S(2)}) collective-permute-start(bf16[128,1024]{1,0:T(8,128)(2,1)S(1)} %get-tuple-element.106), channel_id=1, source_target_pairs={{0,2},{6,4},{1,3},{7,5},{8,10},{14,12},{9,11},{15,13},{16,18},{22,... | collective-permute-start | bytes 786440 | tf_op jit(solution)/shard_map/ppermute | solution.py:677
  205.2 12.0 %collective-permute-start.29 = (bf16[128,1024]{1,0:T(8,128)(2,1)S(1)}, bf16[128,1024]{1,0:T(8,128)(2,1)S(1)}, u32[]{:S(2)}, u32[]{:S(2)}) collective-permute-start(bf16[128,1024]{1,0:T(8,128)(2,1)S(1)} %add_convert_fusion), channel_id=1, source_target_pairs={{2,4},{4,2},{3,5},{5,3},{10,12},{12,10},{11,13},{13,11},{18,20},{2... | collective-permute-start | bytes 786440 | tf_op jit(solution)/shard_map/ppermute | solution.py:677
  209.5 10.8 %collective-permute-start.27 = (bf16[128,1024]{1,0:T(8,128)(2,1)S(1)}, bf16[128,1024]{1,0:T(8,128)(2,1)S(1)}, u32[]{:S(2)}, u32[]{:S(2)}) collective-permute-start(bf16[128,1024]{1,0:T(8,128)(2,1)S(1)} %add_convert_fusion.1), channel_id=1, source_target_pairs={{2,4},{4,2},{3,5},{5,3},{10,12},{12,10},{11,13},{13,11},{18,20},{2... | collective-permute-start | bytes 786440 | tf_op jit(solution)/shard_map/ppermute | solution.py:677
  212.5 9.2 %collective-permute-start.22 = (bf16[128,1024]{1,0:T(8,128)(2,1)S(1)}, bf16[128,1024]{1,0:T(8,128)(2,1)S(1)}, u32[]{:S(2)}, u32[]{:S(2)}) collective-permute-start(bf16[128,1024]{1,0:T(8,128)(2,1)S(1)} %get-tuple-element.105), channel_id=1, source_target_pairs={{0,2},{6,4},{1,3},{7,5},{8,10},{14,12},{9,11},{15,13},{16,18},{22,... | collective-permute-start | bytes 786440 | tf_op jit(solution)/shard_map/ppermute | solution.py:677
  214.2 14.8 %collective-permute-start.25 = (bf16[128,1024]{1,0:T(8,128)(2,1)S(1)}, bf16[128,1024]{1,0:T(8,128)(2,1)S(1)}, u32[]{:S(2)}, u32[]{:S(2)}) collective-permute-start(bf16[128,1024]{1,0:T(8,128)(2,1)S(1)} %add_convert_fusion.2), channel_id=1, source_target_pairs={{2,4},{4,2},{3,5},{5,3},{10,12},{12,10},{11,13},{13,11},{18,20},{2... | collective-permute-start | bytes 786440 | tf_op jit(solution)/shard_map/ppermute | solution.py:677
  217.2 8.7 %collective-permute-start.30 = (bf16[128,1024]{1,0:T(8,128)(2,1)S(1)}, bf16[128,1024]{1,0:T(8,128)(2,1)S(1)}, u32[]{:S(2)}, u32[]{:S(2)}) collective-permute-start(bf16[128,1024]{1,0:T(8,128)(2,1)S(1)} %collective-permute-done.29), channel_id=1, source_target_pairs={{2,0},{4,6},{3,1},{5,7},{10,8},{12,14},{11,9},{13,15},{18,16},{20,... | collective-permute-start | bytes 786440 | tf_op jit(solution)/shard_map/ppermute | solution.py:677
  220.4 8.6 %collective-permute-start.28 = (bf16[128,1024]{1,0:T(8,128)(2,1)S(1)}, bf16[128,1024]{1,0:T(8,128)(2,1)S(1)}, u32[]{:S(2)}, u32[]{:S(2)}) collective-permute-start(bf16[128,1024]{1,0:T(8,128)(2,1)S(1)} %collective-permute-done.27), channel_id=1, source_target_pairs={{2,0},{4,6},{3,1},{5,7},{10,8},{12,14},{11,9},{13,15},{18,16},{20,... | collective-permute-start | bytes 786440 | tf_op jit(solution)/shard_map/ppermute | solution.py:677
  221.8 8.6 %collective-permute-start.23 = (bf16[128,1024]{1,0:T(8,128)(2,1)S(1)}, bf16[128,1024]{1,0:T(8,128)(2,1)S(1)}, u32[]{:S(2)}, u32[]{:S(2)}) collective-permute-start(bf16[128,1024]{1,0:T(8,128)(2,1)S(1)} %add_convert_fusion.3), channel_id=1, source_target_pairs={{2,4},{4,2},{3,5},{5,3},{10,12},{12,10},{11,13},{13,11},{18,20},{2... | collective-permute-start | bytes 786440 | tf_op jit(solution)/shard_map/ppermute | solution.py:677
  (20 other events, 162.3 us)

commit v6 on v4

--- a/solution.py
+++ b/solution.py
@@ -395,7 +395,7 @@
             pltpu.VMEM((each, width), jnp.bfloat16),
             pltpu.VMEM((each, width), jnp.float32),
         ],
-        compiler_params=pltpu.CompilerParams(vmem_limit_bytes=44 * MIB),
+        compiler_params=pltpu.CompilerParams(vmem_limit_bytes=36 * MIB),
         cost_estimate=pl.CostEstimate(
             flops=6 * rows * width * half * slabs_each,
             bytes_accessed=2 * 3 * width * half * experts_here * slabs_each,
@@ -430,7 +430,7 @@
     return pl.pallas_call(
         functools.partial(pack_kernel, layers),
         out_shape=jax.ShapeDtypeStruct((rows, width), jnp.bfloat16),
-        compiler_params=pltpu.CompilerParams(vmem_limit_bytes=24 * MIB),
+        compiler_params=pltpu.CompilerParams(vmem_limit_bytes=16 * MIB),
         cost_estimate=pl.CostEstimate(
             flops=2 * rows * tokens * width, bytes_accessed=6 * rows * width, transcendentals=0
         ),
@@ -453,7 +453,7 @@
     return pl.pallas_call(
         combine_kernel,
         out_shape=out_shape,
-        compiler_params=pltpu.CompilerParams(vmem_limit_bytes=24 * MIB),
+        compiler_params=pltpu.CompilerParams(vmem_limit_bytes=16 * MIB),
         cost_estimate=pl.CostEstimate(
             flops=2 * weights.shape[0] * rows.size,
             bytes_accessed=4 * rows.size,
@@ -677,7 +677,7 @@
     layer_out = pl.pallas_call(
         finish_kernel,
         out_shape=jax.ShapeDtypeStruct((row_count, model_width), jnp.bfloat16),
-        compiler_params=pltpu.CompilerParams(vmem_limit_bytes=24 * MIB),
+        compiler_params=pltpu.CompilerParams(vmem_limit_bytes=16 * MIB),
     )(residual, own_part, *near_arrived, *middle_arrived, *far_arrived)
     return (layer_out[None], new_entries.T[None])
 

time: 235 us -> 237 us (level)
  local copies, waits for them, and re-layouts: 15.2 us -> 23.7 us
  Pallas kernels: 70.2 us -> 66.3 us
  waiting for transfers between devices: 62 us -> 58.3 us
    unnamed x37 -> x41, local copies, waits for them, and re-layouts: 11.6 us -> 20.1 us
    all_to_all x4, waiting for transfers between devices: 10.2 us -> 6.24 us  [exchanged(): lax.all_to_all(values, PLANE_AXES, split_axis=0, concat_axis=0, tiled=True)]
    pallas_call x2, Pallas kernels: 39.1 us -> 35.2 us  [experts(): pl.pallas_call(functools.partial(experts_kernel, slabs_each, sorting), gr...]
  transfers between devices with their start and end apart: 35 -> 35, of which waited for: 24 -> 22; matrix products, arithmetic and copies ran while one was open for 5% -> 5% of each run, Pallas kernels for 21% -> 20%
where the time goes in v6:
time: 237 us; the launch traced here: 233 us
  starting transfers between devices  75.1 us (32%)
  Pallas kernels  66.3 us (28%)
  waiting for transfers between devices  58.3 us (25%)
  local copies, waits for them, and re-layouts  23.7 us (10%)
  other arithmetic  5.18 us (2%)
  matrix products  2.67 us (1%)
    pallas_call x2, Pallas kernels, experts(): pl.pallas_call(functools.partial(experts_kernel, slabs_each, sorting), gr...  35.2 us
    ppermute x12, waiting for transfers between devices, moved(): return lax.ppermute(value, 'z', pairs)  28.9 us
    ppermute x12, starting transfers between devices, moved(): return lax.ppermute(value, 'z', pairs)  22.5 us
    pallas_call x3, Pallas kernels, attention_call(): pl.pallas_call(functools.partial(kernel, score_scale, first_slot, y_count...  21.8 us
    unnamed x41, local copies, waits for them, and re-layouts  20.1 us
    all_to_all x4, starting transfers between devices, exchanged(): lax.all_to_all(values, PLANE_AXES, split_axis=0, concat_axis=0, tiled=True)  16.3 us
    ppermute x3, starting transfers between devices, along_z(): middle = lax.ppermute(values, 'z', MIDDLE)  10.4 us
    ppermute x3, starting transfers between devices, along_z(): middle_far = lax.ppermute(near, 'z', MIDDLE)  9.17 us
  transfers between devices with their start and end apart: 35, of which 22 were waited for; matrix products, arithmetic and copies ran while one was open for 5% of the time, Pallas kernels for 20%

profile of v6, /device:TPU:8, one launch (start us, length us, event | category | flops | bytes accessed | tf_op | source)
XLA Modules:
  0.0 233.2 jit_solution(2313339907898799730)
XLA Ops:
  8.1 4.6 %collective-permute-start = (bf16[592,256]{1,0:T(8,128)(2,1)}, bf16[592,256]{1,0:T(8,128)(2,1)S(1)}, u32[]{:S(2)}, u32[]{:S(2)}) collective-permute-start(bf16[592,256]{1,0:T(8,128)(2,1)} %get-tuple-element.56.refs_4_), channel_id=1, source_target_pairs={{2,4},{4,2},{3,5},{5,3},{10,12},{12,10},{11,13},{13,11},{18,20},{2... | collective-permute-start | bytes 909320 | tf_op jit(solution)/shard_map/ppermute | solution.py:542
  15.7 3.0 %collective-permute-start.6 = (bf16[592,256]{1,0:T(8,128)(2,1)S(1)}, bf16[592,256]{1,0:T(8,128)(2,1)}, u32[]{:S(2)}, u32[]{:S(2)}) collective-permute-start(bf16[592,256]{1,0:T(8,128)(2,1)S(1)} %collective-permute-done.4.refs_6_), channel_id=1, source_target_pairs={{2,4},{4,2},{3,5},{5,3},{10,12},{12,10},{11,13},{13,11},{18,20},{2... | collective-permute-start | bytes 909320 | tf_op jit(solution)/shard_map/ppermute | solution.py:543
  32.3 4.8 %shard_map.150 = (f32[8,256,1]{2,1,0:T(8,128)S(1)}, f32[8,256,1]{2,1,0:T(8,128)S(1)}, f32[8,256,512]{2,1,0:T(8,128)S(1)}) custom-call(s32[12]{0:T(128)S(1)} %concatenate.26.refs_0_, bf16[128,2048]{1,0:T(8,128)(2,1)S(1)} %copy.59.refs_1_, bf16[16,128,64]{2,1,0:T(8,128)(2,1)S(1)} %pad_maximum_fusion.refs_2_, bf16[512,4096]{1,0:T(8,128)(2,1)S(1)} %copy-done.2, ...), custom_call_target="tpu_custom_call" | custom-call | flops 2281701376 | bytes 8388608 | tf_op jit(solution)/shard_map/pallas_call | solution.py:273
  39.4 4.8 %shard_map.151 = (f32[8,256,1]{2,1,0:T(8,128)S(1)}, f32[8,256,1]{2,1,0:T(8,128)S(1)}, f32[8,256,512]{2,1,0:T(8,128)S(1)}) custom-call(s32[12]{0:T(128)S(1)} %concatenate.26.refs_0_, bf16[128,2048]{1,0:T(8,128)(2,1)S(1)} %copy.59.refs_1_, ...), custom_call_target="tpu_custom_call", output_to_operand_aliasing={{0}: (8, {}), {1}: (9, {}), {2}: (10, {})} | custom-call | flops 2281701376 | bytes 8388608 | tf_op jit(solution)/shard_map/pallas_call | solution.py:273
  45.0 12.2 %shard_map.152 = (f32[128,2048]{1,0:T(8,128)S(1)}, bf16[128,1024]{1,0:T(8,128)(2,1)S(1)}, bf16[128,1024]{1,0:T(8,128)(2,1)S(1)}) custom-call(s32[12]{0:T(128)S(1)} %concatenate.26.refs_0_, bf16[128,2048]{1,0:T(8,128)(2,1)S(1)} %copy.59.refs_1_, bf16[16,128,64]{2,1,0:T(8,128)(2,1)S(1)} %pad_maximum_fusion.refs_2_, bf16[512,4096]{1,0:T(8,128)(2,1)S(1)} %copy-done.3, ...), custom_call_target="tpu_custom_call" | custom-call | flops 4563402752 | bytes 16777216 | tf_op jit(solution)/shard_map/pallas_call | solution.py:273
  58.2 3.0 %collective-permute-start.11 = (bf16[128,1024]{1,0:T(8,128)(2,1)S(1)}, bf16[128,1024]{1,0:T(8,128)(2,1)S(1)}, u32[]{:S(2)}, u32[]{:S(2)}) collective-permute-start(bf16[128,1024]{1,0:T(8,128)(2,1)S(1)} %get-tuple-element.73.refs_0_), channel_id=1, source_target_pairs={{2,4},{4,2},{3,5},{5,3},{10,12},{12,10},{11,13},{13,11},{18,20},{2... | collective-permute-start | bytes 786440 | tf_op jit(solution)/shard_map/ppermute | solution.py:542
  63.5 2.9 %collective-permute-start.12 = (bf16[128,1024]{1,0:T(8,128)(2,1)S(1)}, bf16[128,1024]{1,0:T(8,128)(2,1)S(1)}, u32[]{:S(2)}, u32[]{:S(2)}) collective-permute-start(bf16[128,1024]{1,0:T(8,128)(2,1)S(1)} %get-tuple-element.74.refs_1_), channel_id=1, source_target_pairs={{2,4},{4,2},{3,5},{5,3},{10,12},{12,10},{11,13},{13,11},{18,20},{2... | collective-permute-start | bytes 786440 | tf_op jit(solution)/shard_map/ppermute | solution.py:542
  66.4 2.7 %collective-permute-done.11.refs_0_ = bf16[128,1024]{1,0:T(8,128)(2,1)S(1)} collective-permute-done((bf16[128,1024]{1,0:T(8,128)(2,1)S(1)}, bf16[128,1024]{1,0:T(8,128)(2,1)S(1)}, u32[]{:S(2)}, u32[]{:S(2)}) %collective-permute-start.11) | collective-permute-done | bytes 262176 | tf_op jit(solution)/shard_map/ppermute | solution.py:542
  70.3 3.1 %collective-permute-start.14 = (bf16[128,1024]{1,0:T(8,128)(2,1)S(1)}, bf16[128,1024]{1,0:T(8,128)(2,1)S(1)}, u32[]{:S(2)}, u32[]{:S(2)}) collective-permute-start(bf16[128,1024]{1,0:T(8,128)(2,1)S(1)} %collective-permute-done.9.refs_2_), channel_id=1, source_target_pairs={{2,4},{4,2},{3,5},{5,3},{10,12},{12,10},{11,13},{13,11},{18,20},{2... | collective-permute-start | bytes 786440 | tf_op jit(solution)/shard_map/ppermute | solution.py:543
  74.9 3.7 %collective-permute-done.14.refs_4_ = bf16[128,1024]{1,0:T(8,128)(2,1)S(1)} collective-permute-done((bf16[128,1024]{1,0:T(8,128)(2,1)S(1)}, bf16[128,1024]{1,0:T(8,128)(2,1)S(1)}, u32[]{:S(2)}, u32[]{:S(2)}) %collective-permute-start.14) | collective-permute-done | bytes 262176 | tf_op jit(solution)/shard_map/ppermute | solution.py:543
  80.5 3.6 %all-to-all-start = ((bf16[8,56,2048]{2,1,0:T(8,128)(2,1)}), bf16[8,56,2048]{2,1,0:T(8,128)(2,1)S(1)}, u32[]{:S(2)}, u32[]{:S(2)}) async-start(bf16[8,56,2048]{2,1,0:T(8,128)(2,1)} %bitcast.19), calls=%async_computation | async-start | bytes 3670016 | tf_op jit(solution)/shard_map/all_to_all | solution.py:630
  84.2 3.1 %collective-permute-start.16 = (bf16[128,1024]{1,0:T(8,128)(2,1)S(1)}, bf16[128,1024]{1,0:T(8,128)(2,1)}, u32[]{:S(2)}, u32[]{:S(2)}) collective-permute-start(bf16[128,1024]{1,0:T(8,128)(2,1)S(1)} %collective-permute-done.10.refs_3_), channel_id=1, source_target_pairs={{2,4},{4,2},{3,5},{5,3},{10,12},{12,10},{11,13},{13,11},{18,20},{2... | collective-permute-start | bytes 786440 | tf_op jit(solution)/shard_map/ppermute | solution.py:543
  91.6 3.3 %collective-permute-done.16.refs_5_ = bf16[128,1024]{1,0:T(8,128)(2,1)} collective-permute-done((bf16[128,1024]{1,0:T(8,128)(2,1)S(1)}, bf16[128,1024]{1,0:T(8,128)(2,1)}, u32[]{:S(2)}, u32[]{:S(2)}) %collective-permute-start.16) | collective-permute-done | bytes 262176 | tf_op jit(solution)/shard_map/ppermute | solution.py:543
  98.5 2.4 %collective-permute-done.17.refs_6_ = bf16[128,1024]{1,0:T(8,128)(2,1)} collective-permute-done((bf16[128,1024]{1,0:T(8,128)(2,1)S(1)}, bf16[128,1024]{1,0:T(8,128)(2,1)}, u32[]{:S(2)}, u32[]{:S(2)}) %collective-permute-start.17) | collective-permute-done | bytes 262176 | tf_op jit(solution)/shard_map/ppermute | solution.py:545
  100.9 5.3 %collective-permute-done.18.refs_7_ = bf16[128,1024]{1,0:T(8,128)(2,1)S(1)} collective-permute-done((bf16[128,1024]{1,0:T(8,128)(2,1)}, bf16[128,1024]{1,0:T(8,128)(2,1)S(1)}, u32[]{:S(2)}, u32[]{:S(2)}) %collective-permute-start.18) | collective-permute-done | bytes 262176 | tf_op jit(solution)/shard_map/ppermute | solution.py:545
  107.2 3.0 %shard_map.155 = bf16[448,2048]{1,0:T(8,128)(2,1)} custom-call(bf16[448,256]{1,0:T(8,128)(2,1)S(1)} %copy.66.place_ref, bf16[128,1024]{1,0:T(8,128)(2,1)S(1)} %collective-permute-done.11.refs_0_, bf16[128,1024]{1,0:T(8,128)(2,1)S(1)} %collective-permute-done.12.refs_1_, bf16[128,1024]{1,0:T(8,128)(2,1)S(1)} %collective-permute-done.13.refs_2_, ...), custom_call_target="tpu_custom_call" | custom-call | flops 469762048 | bytes 5505024 | tf_op jit(solution)/shard_map/pallas_call | solution.py:430
  110.2 4.3 %all-to-all-start.1 = ((bf16[8,56,2048]{2,1,0:T(8,128)(2,1)}), bf16[8,56,2048]{2,1,0:T(8,128)(2,1)}, u32[]{:S(2)}, u32[]{:S(2)}) async-start(bf16[8,56,2048]{2,1,0:T(8,128)(2,1)} %bitcast.21), calls=%async_computation.1 | async-start | bytes 3670016 | tf_op jit(solution)/shard_map/all_to_all | solution.py:630
  114.9 4.3 %copy-done = bf16[4,704,2048]{2,1,0:T(8,128)(2,1)S(1)} copy-done((bf16[4,704,2048]{2,1,0:T(8,128)(2,1)S(1)}, bf16[4,704,2048]{2,1,0:T(8,128)(2,1)}, u32[]{:S(2)}) %copy-start) | copy-done | bytes 11534360
  119.1 17.3 %shard_map.154 = bf16[448,2048]{1,0:T(8,128)(2,1)S(1)} custom-call(bf16[448,2048]{1,0:T(8,128)(2,1)S(1)} %bitcast.51, bf16[2,224,448]{2,1,0:T(8,128)(2,1)S(1)} %fusion.8.refs_0_, bf16[2,448,224]{2,1,0:T(8,128)(2,1)S(1)} %fusion.9.refs_1_, bf16[4,2048,1408]{2,1,0:T(8,128)(2,1)} %refs_3_.9, bf16[4,2048,1408]{2,1,0:T(8,128)(2,1)} %refs_3_.9, ...), custom_call_target="tpu_custom_call" | custom-call | flops 7751073792 | bytes 34603008 | tf_op jit(solution)/shard_map/pallas_call | solution.py:388
  137.7 4.1 %all-to-all-start.2 = ((bf16[8,56,2048]{2,1,0:T(8,128)(2,1)}), bf16[8,56,2048]{2,1,0:T(8,128)(2,1)S(1)}, u32[]{:S(2)}, u32[]{:S(2)}) async-start(bf16[8,56,2048]{2,1,0:T(8,128)(2,1)} %bitcast.53), calls=%async_computation.2 | async-start | bytes 3670016 | tf_op jit(solution)/shard_map/all_to_all | solution.py:630
  141.8 4.3 %copy-done.1 = bf16[4,704,2048]{2,1,0:T(8,128)(2,1)S(1)} copy-done((bf16[4,704,2048]{2,1,0:T(8,128)(2,1)S(1)}, bf16[4,704,2048]{2,1,0:T(8,128)(2,1)}, u32[]{:S(2)}) %copy-start.1) | copy-done | bytes 11534360
  146.1 17.9 %shard_map.156 = bf16[448,2048]{1,0:T(8,128)(2,1)S(1)} custom-call(bf16[448,2048]{1,0:T(8,128)(2,1)} %bitcast.22.x_ref, bf16[2,224,448]{2,1,0:T(8,128)(2,1)S(1)} %fusion.8.refs_0_, bf16[2,448,224]{2,1,0:T(8,128)(2,1)S(1)} %fusion.9.refs_1_, bf16[4,2048,1408]{2,1,0:T(8,128)(2,1)} %refs_3_.9, bf16[4,2048,1408]{2,1,0:T(8,128)(2,1)} %refs_3_.9, ...), custom_call_target="tpu_custom_call" | custom-call | flops 7751073792 | bytes 34603008 | tf_op jit(solution)/shard_map/pallas_call | solution.py:388
  166.5 4.2 %all-to-all-start.3 = ((bf16[8,56,2048]{2,1,0:T(8,128)(2,1)}), bf16[8,56,2048]{2,1,0:T(8,128)(2,1)S(1)}, u32[]{:S(2)}, u32[]{:S(2)}) async-start(bf16[8,56,2048]{2,1,0:T(8,128)(2,1)} %bitcast.52), calls=%async_computation.3 | async-start | bytes 3670016 | tf_op jit(solution)/shard_map/all_to_all | solution.py:630
  175.7 6.7 %collective-permute-done.19.refs_0_ = bf16[128,1024]{1,0:T(8,128)(2,1)S(1)} collective-permute-done((bf16[128,1024]{1,0:T(8,128)(2,1)S(1)}, bf16[128,1024]{1,0:T(8,128)(2,1)S(1)}, u32[]{:S(2)}, u32[]{:S(2)}) %collective-permute-start.19) | collective-permute-done | bytes 262176 | tf_op jit(solution)/shard_map/ppermute | solution.py:660
  182.5 5.2 %collective-permute-done.20.refs_1_ = bf16[128,1024]{1,0:T(8,128)(2,1)S(1)} collective-permute-done((bf16[128,1024]{1,0:T(8,128)(2,1)S(1)}, bf16[128,1024]{1,0:T(8,128)(2,1)S(1)}, u32[]{:S(2)}, u32[]{:S(2)}) %collective-permute-start.20) | collective-permute-done | bytes 262176 | tf_op jit(solution)/shard_map/ppermute | solution.py:660
  188.4 5.2 %all-to-all-done.3 = bf16[8,56,2048]{2,1,0:T(8,128)(2,1)S(1)} async-done(((bf16[8,56,2048]{2,1,0:T(8,128)(2,1)}), bf16[8,56,2048]{2,1,0:T(8,128)(2,1)S(1)}, u32[]{:S(2)}, u32[]{:S(2)}) %all-to-all-start.3) | async-done | bytes 1835040 | tf_op jit(solution)/shard_map/all_to_all | solution.py:630
  197.1 8.5 %collective-permute-done.21 = bf16[128,1024]{1,0:T(8,128)(2,1)S(1)} collective-permute-done((bf16[128,1024]{1,0:T(8,128)(2,1)S(1)}, bf16[128,1024]{1,0:T(8,128)(2,1)S(1)}, u32[]{:S(2)}, u32[]{:S(2)}) %collective-permute-start.21) | collective-permute-done | bytes 262176 | tf_op jit(solution)/shard_map/ppermute | solution.py:660
  206.9 3.0 %collective-permute-start.29 = (bf16[128,1024]{1,0:T(8,128)(2,1)S(1)}, bf16[128,1024]{1,0:T(8,128)(2,1)S(1)}, u32[]{:S(2)}, u32[]{:S(2)}) collective-permute-start(bf16[128,1024]{1,0:T(8,128)(2,1)S(1)} %add_convert_fusion.1), channel_id=1, source_target_pairs={{2,4},{4,2},{3,5},{5,3},{10,12},{12,10},{11,13},{13,11},{18,20},{2... | collective-permute-start | bytes 786440 | tf_op jit(solution)/shard_map/ppermute | solution.py:660
  211.3 3.0 %collective-permute-start.27 = (bf16[128,1024]{1,0:T(8,128)(2,1)S(1)}, bf16[128,1024]{1,0:T(8,128)(2,1)S(1)}, u32[]{:S(2)}, u32[]{:S(2)}) collective-permute-start(bf16[128,1024]{1,0:T(8,128)(2,1)S(1)} %add_convert_fusion.2), channel_id=1, source_target_pairs={{2,4},{4,2},{3,5},{5,3},{10,12},{12,10},{11,13},{13,11},{18,20},{2... | collective-permute-start | bytes 786440 | tf_op jit(solution)/shard_map/ppermute | solution.py:660
  216.0 3.0 %collective-permute-start.25 = (bf16[128,1024]{1,0:T(8,128)(2,1)S(1)}, bf16[128,1024]{1,0:T(8,128)(2,1)S(1)}, u32[]{:S(2)}, u32[]{:S(2)}) collective-permute-start(bf16[128,1024]{1,0:T(8,128)(2,1)S(1)} %add_convert_fusion.3), channel_id=1, source_target_pairs={{2,4},{4,2},{3,5},{5,3},{10,12},{12,10},{11,13},{13,11},{18,20},{2... | collective-permute-start | bytes 786440 | tf_op jit(solution)/shard_map/ppermute | solution.py:660
  223.5 3.0 %collective-permute-start.23 = (bf16[128,1024]{1,0:T(8,128)(2,1)S(1)}, bf16[128,1024]{1,0:T(8,128)(2,1)S(1)}, u32[]{:S(2)}, u32[]{:S(2)}) collective-permute-start(bf16[128,1024]{1,0:T(8,128)(2,1)S(1)} %add_convert_fusion.4), channel_id=1, source_target_pairs={{2,4},{4,2},{3,5},{5,3},{10,12},{12,10},{11,13},{13,11},{18,20},{2... | collective-permute-start | bytes 786440 | tf_op jit(solution)/shard_map/ppermute | solution.py:660
  227.6 3.1 %collective-permute-done.28.refs_4_ = bf16[128,1024]{1,0:T(8,128)(2,1)S(1)} collective-permute-done((bf16[128,1024]{1,0:T(8,128)(2,1)S(1)}, bf16[128,1024]{1,0:T(8,128)(2,1)S(1)}, u32[]{:S(2)}, u32[]{:S(2)}) %collective-permute-start.28) | collective-permute-done | bytes 262176 | tf_op jit(solution)/shard_map/ppermute | solution.py:660
  (138 shorter events, 68.8 us)
Async XLA Ops:
  6.1 9.6 %collective-permute-start.4 = (bf16[592,256]{1,0:T(8,128)(2,1)}, bf16[592,256]{1,0:T(8,128)(2,1)S(1)}, u32[]{:S(2)}, u32[]{:S(2)}) collective-permute-start(bf16[592,256]{1,0:T(8,128)(2,1)} %get-tuple-element.56.refs_4_), channel_id=1, source_target_pairs={{0,2},{2,0},{4,6},{6,4},{1,3},{3,1},{5,7},{7,5},{8,10},{10,8},{12,... | collective-permute-start | bytes 909320 | tf_op jit(solution)/shard_map/ppermute | solution.py:541
  6.1 22.1 %collective-permute-start.3 = (bf16[592,256]{1,0:T(8,128)(2,1)}, bf16[592,256]{1,0:T(8,128)(2,1)S(1)}, u32[]{:S(2)}, u32[]{:S(2)}) collective-permute-start(bf16[592,256]{1,0:T(8,128)(2,1)} %get-tuple-element.56.refs_4_), channel_id=1, source_target_pairs={{0,1},{1,0},{2,3},{3,2},{4,5},{5,4},{6,7},{7,6},{8,9},{9,8},{10,11... | collective-permute-start | bytes 909320 | tf_op jit(solution)/shard_map/ppermute | solution.py:35
  8.1 11.7 %collective-permute-start = (bf16[592,256]{1,0:T(8,128)(2,1)}, bf16[592,256]{1,0:T(8,128)(2,1)S(1)}, u32[]{:S(2)}, u32[]{:S(2)}) collective-permute-start(bf16[592,256]{1,0:T(8,128)(2,1)} %get-tuple-element.56.refs_4_), channel_id=1, source_target_pairs={{2,4},{4,2},{3,5},{5,3},{10,12},{12,10},{11,13},{13,11},{18,20},{2... | collective-permute-start | bytes 909320 | tf_op jit(solution)/shard_map/ppermute | solution.py:542
  15.7 10.4 %collective-permute-start.6 = (bf16[592,256]{1,0:T(8,128)(2,1)S(1)}, bf16[592,256]{1,0:T(8,128)(2,1)}, u32[]{:S(2)}, u32[]{:S(2)}) collective-permute-start(bf16[592,256]{1,0:T(8,128)(2,1)S(1)} %collective-permute-done.4.refs_6_), channel_id=1, source_target_pairs={{2,4},{4,2},{3,5},{5,3},{10,12},{12,10},{11,13},{13,11},{18,20},{2... | collective-permute-start | bytes 909320 | tf_op jit(solution)/shard_map/ppermute | solution.py:543
  21.9 8.2 %collective-permute-start.5 = (bf16[592,256]{1,0:T(8,128)(2,1)S(1)}, bf16[592,256]{1,0:T(8,128)(2,1)S(1)}, u32[]{:S(2)}, u32[]{:S(2)}) collective-permute-start(bf16[592,256]{1,0:T(8,128)(2,1)S(1)} %collective-permute-done.4.refs_6_), channel_id=1, source_target_pairs={{0,1},{1,0},{2,3},{3,2},{4,5},{5,4},{6,7},{7,6},{8,9},{9,8},{10,11... | collective-permute-start | bytes 909320 | tf_op jit(solution)/shard_map/ppermute | solution.py:35
  26.1 10.9 %collective-permute-start.7 = (bf16[592,256]{1,0:T(8,128)(2,1)}, bf16[592,256]{1,0:T(8,128)(2,1)S(1)}, u32[]{:S(2)}, u32[]{:S(2)}) collective-permute-start(bf16[592,256]{1,0:T(8,128)(2,1)} %collective-permute-done.6), channel_id=1, source_target_pairs={{2,0},{4,6},{3,1},{5,7},{10,8},{12,14},{11,9},{13,15},{18,16},{20,... | collective-permute-start | bytes 909320 | tf_op jit(solution)/shard_map/ppermute | solution.py:545
  27.5 16.7 %collective-permute-start.2 = (bf16[592,256]{1,0:T(8,128)(2,1)S(1)}, bf16[592,256]{1,0:T(8,128)(2,1)S(1)}, u32[]{:S(2)}, u32[]{:S(2)}) collective-permute-start(bf16[592,256]{1,0:T(8,128)(2,1)S(1)} %broadcast_select_fusion.1.refs_4_), channel_id=1, source_target_pairs={{0,1},{1,0},{2,3},{3,2},{4,5},{5,4},{6,7},{7,6},{8,9},{9,8},{10,11... | collective-permute-start | bytes 909320 | tf_op jit(solution)/shard_map/ppermute | solution.py:35
  58.2 10.8 %collective-permute-start.11 = (bf16[128,1024]{1,0:T(8,128)(2,1)S(1)}, bf16[128,1024]{1,0:T(8,128)(2,1)S(1)}, u32[]{:S(2)}, u32[]{:S(2)}) collective-permute-start(bf16[128,1024]{1,0:T(8,128)(2,1)S(1)} %get-tuple-element.73.refs_0_), channel_id=1, source_target_pairs={{2,4},{4,2},{3,5},{5,3},{10,12},{12,10},{11,13},{13,11},{18,20},{2... | collective-permute-start | bytes 786440 | tf_op jit(solution)/shard_map/ppermute | solution.py:542
  61.1 9.2 %collective-permute-start.9 = (bf16[128,1024]{1,0:T(8,128)(2,1)S(1)}, bf16[128,1024]{1,0:T(8,128)(2,1)S(1)}, u32[]{:S(2)}, u32[]{:S(2)}) collective-permute-start(bf16[128,1024]{1,0:T(8,128)(2,1)S(1)} %get-tuple-element.73.refs_0_), channel_id=1, source_target_pairs={{0,2},{2,0},{4,6},{6,4},{1,3},{3,1},{5,7},{7,5},{8,10},{10,8},{12,... | collective-permute-start | bytes 786440 | tf_op jit(solution)/shard_map/ppermute | solution.py:541
  61.5 12.7 %collective-permute-start.10 = (bf16[128,1024]{1,0:T(8,128)(2,1)S(1)}, bf16[128,1024]{1,0:T(8,128)(2,1)S(1)}, u32[]{:S(2)}, u32[]{:S(2)}) collective-permute-start(bf16[128,1024]{1,0:T(8,128)(2,1)S(1)} %get-tuple-element.74.refs_1_), channel_id=1, source_target_pairs={{0,2},{2,0},{4,6},{6,4},{1,3},{3,1},{5,7},{7,5},{8,10},{10,8},{12,... | collective-permute-start | bytes 786440 | tf_op jit(solution)/shard_map/ppermute | solution.py:541
  63.5 11.2 %collective-permute-start.12 = (bf16[128,1024]{1,0:T(8,128)(2,1)S(1)}, bf16[128,1024]{1,0:T(8,128)(2,1)S(1)}, u32[]{:S(2)}, u32[]{:S(2)}) collective-permute-start(bf16[128,1024]{1,0:T(8,128)(2,1)S(1)} %get-tuple-element.74.refs_1_), channel_id=1, source_target_pairs={{2,4},{4,2},{3,5},{5,3},{10,12},{12,10},{11,13},{13,11},{18,20},{2... | collective-permute-start | bytes 786440 | tf_op jit(solution)/shard_map/ppermute | solution.py:542
  70.3 8.3 %collective-permute-start.14 = (bf16[128,1024]{1,0:T(8,128)(2,1)S(1)}, bf16[128,1024]{1,0:T(8,128)(2,1)S(1)}, u32[]{:S(2)}, u32[]{:S(2)}) collective-permute-start(bf16[128,1024]{1,0:T(8,128)(2,1)S(1)} %collective-permute-done.9.refs_2_), channel_id=1, source_target_pairs={{2,4},{4,2},{3,5},{5,3},{10,12},{12,10},{11,13},{13,11},{18,20},{2... | collective-permute-start | bytes 786440 | tf_op jit(solution)/shard_map/ppermute | solution.py:543
  80.5 26.6 %all-to-all-start = ((bf16[8,56,2048]{2,1,0:T(8,128)(2,1)}), bf16[8,56,2048]{2,1,0:T(8,128)(2,1)S(1)}, u32[]{:S(2)}, u32[]{:S(2)}) async-start(bf16[8,56,2048]{2,1,0:T(8,128)(2,1)} %bitcast.19), calls=%async_computation | async-start | bytes 3670016 | tf_op jit(solution)/shard_map/all_to_all | solution.py:630
  84.2 10.7 %collective-permute-start.16 = (bf16[128,1024]{1,0:T(8,128)(2,1)S(1)}, bf16[128,1024]{1,0:T(8,128)(2,1)}, u32[]{:S(2)}, u32[]{:S(2)}) collective-permute-start(bf16[128,1024]{1,0:T(8,128)(2,1)S(1)} %collective-permute-done.10.refs_3_), channel_id=1, source_target_pairs={{2,4},{4,2},{3,5},{5,3},{10,12},{12,10},{11,13},{13,11},{18,20},{2... | collective-permute-start | bytes 786440 | tf_op jit(solution)/shard_map/ppermute | solution.py:543
  87.4 11.1 %collective-permute-start.15 = (bf16[128,1024]{1,0:T(8,128)(2,1)S(1)}, bf16[128,1024]{1,0:T(8,128)(2,1)}, u32[]{:S(2)}, u32[]{:S(2)}) collective-permute-start(bf16[128,1024]{1,0:T(8,128)(2,1)S(1)} %collective-permute-done.12.refs_1_), channel_id=1, source_target_pairs={{2,0},{4,6},{3,1},{5,7},{10,8},{12,14},{11,9},{13,15},{18,16},{20,... | collective-permute-start | bytes 786440 | tf_op jit(solution)/shard_map/ppermute | solution.py:544
  89.4 11.5 %collective-permute-start.17 = (bf16[128,1024]{1,0:T(8,128)(2,1)S(1)}, bf16[128,1024]{1,0:T(8,128)(2,1)}, u32[]{:S(2)}, u32[]{:S(2)}) collective-permute-start(bf16[128,1024]{1,0:T(8,128)(2,1)S(1)} %collective-permute-done.14.refs_4_), channel_id=1, source_target_pairs={{2,0},{4,6},{3,1},{5,7},{10,8},{12,14},{11,9},{13,15},{18,16},{20,... | collective-permute-start | bytes 786440 | tf_op jit(solution)/shard_map/ppermute | solution.py:545
  94.9 11.3 %collective-permute-start.18 = (bf16[128,1024]{1,0:T(8,128)(2,1)}, bf16[128,1024]{1,0:T(8,128)(2,1)S(1)}, u32[]{:S(2)}, u32[]{:S(2)}) collective-permute-start(bf16[128,1024]{1,0:T(8,128)(2,1)} %collective-permute-done.16.refs_5_), channel_id=1, source_target_pairs={{2,0},{4,6},{3,1},{5,7},{10,8},{12,14},{11,9},{13,15},{18,16},{20,... | collective-permute-start | bytes 786440 | tf_op jit(solution)/shard_map/ppermute | solution.py:545
  110.2 27.5 %all-to-all-start.1 = ((bf16[8,56,2048]{2,1,0:T(8,128)(2,1)}), bf16[8,56,2048]{2,1,0:T(8,128)(2,1)}, u32[]{:S(2)}, u32[]{:S(2)}) async-start(bf16[8,56,2048]{2,1,0:T(8,128)(2,1)} %bitcast.21), calls=%async_computation.1 | async-start | bytes 3670016 | tf_op jit(solution)/shard_map/all_to_all | solution.py:630
  137.7 27.5 %all-to-all-start.2 = ((bf16[8,56,2048]{2,1,0:T(8,128)(2,1)}), bf16[8,56,2048]{2,1,0:T(8,128)(2,1)S(1)}, u32[]{:S(2)}, u32[]{:S(2)}) async-start(bf16[8,56,2048]{2,1,0:T(8,128)(2,1)} %bitcast.53), calls=%async_computation.2 | async-start | bytes 3670016 | tf_op jit(solution)/shard_map/all_to_all | solution.py:630
  166.5 27.2 %all-to-all-start.3 = ((bf16[8,56,2048]{2,1,0:T(8,128)(2,1)}), bf16[8,56,2048]{2,1,0:T(8,128)(2,1)S(1)}, u32[]{:S(2)}, u32[]{:S(2)}) async-start(bf16[8,56,2048]{2,1,0:T(8,128)(2,1)} %bitcast.52), calls=%async_computation.3 | async-start | bytes 3670016 | tf_op jit(solution)/shard_map/all_to_all | solution.py:630
  173.3 9.2 %collective-permute-start.19 = (bf16[128,1024]{1,0:T(8,128)(2,1)S(1)}, bf16[128,1024]{1,0:T(8,128)(2,1)S(1)}, u32[]{:S(2)}, u32[]{:S(2)}) collective-permute-start(bf16[128,1024]{1,0:T(8,128)(2,1)S(1)} %get-tuple-element.96), channel_id=1, source_target_pairs={{0,2},{2,0},{4,6},{6,4},{1,3},{3,1},{5,7},{7,5},{8,10},{10,8},{12,... | collective-permute-start | bytes 786440 | tf_op jit(solution)/shard_map/ppermute | solution.py:660
  174.8 13.0 %collective-permute-start.20 = (bf16[128,1024]{1,0:T(8,128)(2,1)S(1)}, bf16[128,1024]{1,0:T(8,128)(2,1)S(1)}, u32[]{:S(2)}, u32[]{:S(2)}) collective-permute-start(bf16[128,1024]{1,0:T(8,128)(2,1)S(1)} %get-tuple-element.97), channel_id=1, source_target_pairs={{0,2},{2,0},{4,6},{6,4},{1,3},{3,1},{5,7},{7,5},{8,10},{10,8},{12,... | collective-permute-start | bytes 786440 | tf_op jit(solution)/shard_map/ppermute | solution.py:660
  194.4 11.2 %collective-permute-start.21 = (bf16[128,1024]{1,0:T(8,128)(2,1)S(1)}, bf16[128,1024]{1,0:T(8,128)(2,1)S(1)}, u32[]{:S(2)}, u32[]{:S(2)}) collective-permute-start(bf16[128,1024]{1,0:T(8,128)(2,1)S(1)} %get-tuple-element.104), channel_id=1, source_target_pairs={{0,2},{6,4},{1,3},{7,5},{8,10},{14,12},{9,11},{15,13},{16,18},{22,... | collective-permute-start | bytes 786440 | tf_op jit(solution)/shard_map/ppermute | solution.py:660
  195.8 15.4 %collective-permute-start.26 = (bf16[128,1024]{1,0:T(8,128)(2,1)S(1)}, bf16[128,1024]{1,0:T(8,128)(2,1)S(1)}, u32[]{:S(2)}, u32[]{:S(2)}) collective-permute-start(bf16[128,1024]{1,0:T(8,128)(2,1)S(1)} %get-tuple-element.107), channel_id=1, source_target_pairs={{0,2},{6,4},{1,3},{7,5},{8,10},{14,12},{9,11},{15,13},{16,18},{22,... | collective-permute-start | bytes 786440 | tf_op jit(solution)/shard_map/ppermute | solution.py:660
  205.6 10.3 %collective-permute-start.24 = (bf16[128,1024]{1,0:T(8,128)(2,1)S(1)}, bf16[128,1024]{1,0:T(8,128)(2,1)S(1)}, u32[]{:S(2)}, u32[]{:S(2)}) collective-permute-start(bf16[128,1024]{1,0:T(8,128)(2,1)S(1)} %get-tuple-element.106), channel_id=1, source_target_pairs={{0,2},{6,4},{1,3},{7,5},{8,10},{14,12},{9,11},{15,13},{16,18},{22,... | collective-permute-start | bytes 786440 | tf_op jit(solution)/shard_map/ppermute | solution.py:660
  206.9 12.0 %collective-permute-start.29 = (bf16[128,1024]{1,0:T(8,128)(2,1)S(1)}, bf16[128,1024]{1,0:T(8,128)(2,1)S(1)}, u32[]{:S(2)}, u32[]{:S(2)}) collective-permute-start(bf16[128,1024]{1,0:T(8,128)(2,1)S(1)} %add_convert_fusion.1), channel_id=1, source_target_pairs={{2,4},{4,2},{3,5},{5,3},{10,12},{12,10},{11,13},{13,11},{18,20},{2... | collective-permute-start | bytes 786440 | tf_op jit(solution)/shard_map/ppermute | solution.py:660
  211.3 10.9 %collective-permute-start.27 = (bf16[128,1024]{1,0:T(8,128)(2,1)S(1)}, bf16[128,1024]{1,0:T(8,128)(2,1)S(1)}, u32[]{:S(2)}, u32[]{:S(2)}) collective-permute-start(bf16[128,1024]{1,0:T(8,128)(2,1)S(1)} %add_convert_fusion.2), channel_id=1, source_target_pairs={{2,4},{4,2},{3,5},{5,3},{10,12},{12,10},{11,13},{13,11},{18,20},{2... | collective-permute-start | bytes 786440 | tf_op jit(solution)/shard_map/ppermute | solution.py:660
  214.3 9.2 %collective-permute-start.22 = (bf16[128,1024]{1,0:T(8,128)(2,1)S(1)}, bf16[128,1024]{1,0:T(8,128)(2,1)S(1)}, u32[]{:S(2)}, u32[]{:S(2)}) collective-permute-start(bf16[128,1024]{1,0:T(8,128)(2,1)S(1)} %get-tuple-element.105), channel_id=1, source_target_pairs={{0,2},{6,4},{1,3},{7,5},{8,10},{14,12},{9,11},{15,13},{16,18},{22,... | collective-permute-start | bytes 786440 | tf_op jit(solution)/shard_map/ppermute | solution.py:660
  216.0 14.8 %collective-permute-start.25 = (bf16[128,1024]{1,0:T(8,128)(2,1)S(1)}, bf16[128,1024]{1,0:T(8,128)(2,1)S(1)}, u32[]{:S(2)}, u32[]{:S(2)}) collective-permute-start(bf16[128,1024]{1,0:T(8,128)(2,1)S(1)} %add_convert_fusion.3), channel_id=1, source_target_pairs={{2,4},{4,2},{3,5},{5,3},{10,12},{12,10},{11,13},{13,11},{18,20},{2... | collective-permute-start | bytes 786440 | tf_op jit(solution)/shard_map/ppermute | solution.py:660
  219.0 8.7 %collective-permute-start.30 = (bf16[128,1024]{1,0:T(8,128)(2,1)S(1)}, bf16[128,1024]{1,0:T(8,128)(2,1)S(1)}, u32[]{:S(2)}, u32[]{:S(2)}) collective-permute-start(bf16[128,1024]{1,0:T(8,128)(2,1)S(1)} %collective-permute-done.29), channel_id=1, source_target_pairs={{2,0},{4,6},{3,1},{5,7},{10,8},{12,14},{11,9},{13,15},{18,16},{20,... | collective-permute-start | bytes 786440 | tf_op jit(solution)/shard_map/ppermute | solution.py:660
  222.2 8.6 %collective-permute-start.28 = (bf16[128,1024]{1,0:T(8,128)(2,1)S(1)}, bf16[128,1024]{1,0:T(8,128)(2,1)S(1)}, u32[]{:S(2)}, u32[]{:S(2)}) collective-permute-start(bf16[128,1024]{1,0:T(8,128)(2,1)S(1)} %collective-permute-done.27), channel_id=1, source_target_pairs={{2,0},{4,6},{3,1},{5,7},{10,8},{12,14},{11,9},{13,15},{18,16},{20,... | collective-permute-start | bytes 786440 | tf_op jit(solution)/shard_map/ppermute | solution.py:660
  223.5 8.6 %collective-permute-start.23 = (bf16[128,1024]{1,0:T(8,128)(2,1)S(1)}, bf16[128,1024]{1,0:T(8,128)(2,1)S(1)}, u32[]{:S(2)}, u32[]{:S(2)}) collective-permute-start(bf16[128,1024]{1,0:T(8,128)(2,1)S(1)} %add_convert_fusion.4), channel_id=1, source_target_pairs={{2,4},{4,2},{3,5},{5,3},{10,12},{12,10},{11,13},{13,11},{18,20},{2... | collective-permute-start | bytes 786440 | tf_op jit(solution)/shard_map/ppermute | solution.py:660
  (22 other events, 170.4 us)
